TPU v7x, 256 devices: a whole 4x4x8 slice. The times are simulated.
256 devices in a mesh: row: 16 (over y, x), col: 8 (over z), layer: 2 (over core).
Axes of the slice: x: 4, y: 4, z: 8, core: 2. Of those that a mesh axis runs over, the one named last changes fastest.
Arguments:
- density: bfloat16 [4096, 4096], P('row', 'col'), may hold values from -0.125 to 0.125
- panel: bfloat16 [4096, 16384], P('row', 'col'), may hold values from -6 to 6
- pattern: int32 [32, 32], P('row', 'col'), may hold values 0 or 1
Outputs:
- purified: bfloat16 [4096, 16384], P('row', ('col', 'layer'))
All inputs are finite; a program needn't handle non-finite values. No bound on the sum of `pattern` on one device may be relied on, other than what follows from the above.
Results may differ from a plain program's by a relative error of at most 0.0034.
Values may be sent and summed in bfloat16 or wider, within the bound.
No kernel may reach another device: no remote copies, remote signals or barrier semaphores. Data moves between devices by JAX's collectives and lax.ppermute only.
A program may use at most 64 MiB of HBM per device.

v0:
```python
import jax
import jax.numpy as jnp
from jax import lax
from jax.sharding import PartitionSpec as P

BS = 128


def passed_along(block, axis, distance):
    devices = range(lax.axis_size(axis))
    route = [((i - distance) % len(devices), i) for i in devices]
    return lax.ppermute(block, axis, route)


def multiply(left_tile, right_tile, step_count, offset, left_shift, right_shift):
    row_count = lax.axis_size("row")
    col_count = lax.axis_size("col")
    group_size = row_count // col_count
    row_index = lax.axis_index("row")
    col_index = lax.axis_index("col")
    slice_width = left_tile.shape[1] // group_size
    left_amount = (row_index + offset) // group_size % col_count
    right_amount = (group_size * col_index + offset) % row_count
    for bit_number in range((col_count - 1).bit_length()):
        shifted = left_shift(left_tile, col_count - (1 << bit_number))
        left_tile = jnp.where(left_amount // (1 << bit_number) % 2 == 1, shifted, left_tile)
    for bit_number in range((row_count - 1).bit_length()):
        shifted = right_shift(right_tile, row_count - (1 << bit_number))
        right_tile = jnp.where(right_amount // (1 << bit_number) % 2 == 1, shifted, right_tile)
    running = jnp.zeros((left_tile.shape[0], right_tile.shape[1]), jnp.float32)
    for segment in range(step_count):
        position = (row_index + offset + segment) % group_size
        section = lax.dynamic_slice_in_dim(left_tile, position * slice_width, slice_width, 1)
        running = running + jnp.dot(section, right_tile, preferred_element_type=jnp.float32)
        if segment + 1 < step_count:
            right_tile = right_shift(right_tile, row_count - 1)
            shifted = left_shift(left_tile, col_count - 1)
            left_tile = jnp.where(
                (row_index + offset + segment + 1) % group_size == 0, shifted, left_tile
            )
    return running


def shards(density, panel, pattern):
    row_count = lax.axis_size("row")
    layer_count = lax.axis_size("layer")
    layer_index = lax.axis_index("layer")
    mask_rows, mask_cols = pattern.shape
    tile_rows, tile_inner = density.shape
    block_mask = pattern.astype(jnp.bfloat16)
    filtered = (
        density.reshape(mask_rows, BS, mask_cols, BS) * block_mask[:, None, :, None]
    ).reshape(tile_rows, tile_inner)
    quarter = panel.shape[1] // layer_count

    def move_left(tile_data, amount):
        return passed_along(tile_data, "col", amount)

    def move_right(tile_data, amount):
        return passed_along(tile_data, "row", amount)

    layer_depth = row_count // layer_count
    offset = layer_index * layer_depth
    partial_value = multiply(filtered, panel, layer_depth, offset, move_left, move_right)
    square = lax.psum(partial_value, "layer")
    partial_cubic = multiply(
        filtered, square.astype(jnp.bfloat16), layer_depth, offset, move_left, move_right
    )
    cubic = lax.psum_scatter(partial_cubic, "layer", scatter_dimension=1, tiled=True)
    squares_kept = lax.dynamic_slice_in_dim(square, layer_index * quarter, quarter, 1)
    return (3.0 * squares_kept - 2.0 * cubic).astype(jnp.bfloat16)


def solution(mesh):
    in_specs = (P("row", "col"), P("row", "col"), P("row", "col"))
    out_specs = P("row", ("col", "layer"))
    return jax.shard_map(shards, mesh=mesh, in_specs=in_specs, out_specs=out_specs, check_vma=False)
```

profile of v0, /device:TPU:1, one launch (start us, length us, event | category | flops | bytes accessed | tf_op | source)
XLA Modules:
  0.0 609.9 jit_solution(18231696401720986830)
XLA Ops:
  6.5 5.8 collective-permute-start.3
  12.3 22.1 %collective-permute-done.3 = bf16[256,2048]{1,0:T(8,128)(2,1)S(1)} collective-permute-done((bf16[256,2048]{1,0:T(8,128)(2,1)}, bf16[256,2048]{1,0:T(8,128)(2,1)S(1)}, u32[]{:S(2)}, u32[]{:S(2)}) %collective-permute-start.3) | collective-permute-done | bytes 1048608 | tf_op jit(solution)/shard_map/ppermute | solution.py:12
  38.2 22.2 %collective-permute-done.4 = bf16[256,2048]{1,0:T(8,128)(2,1)S(1)} collective-permute-done((bf16[256,2048]{1,0:T(8,128)(2,1)S(1)}, bf16[256,2048]{1,0:T(8,128)(2,1)S(1)}, u32[]{:S(2)}, u32[]{:S(2)}) %collective-permute-start.4) | collective-permute-done | bytes 1048608 | tf_op jit(solution)/shard_map/ppermute | solution.py:12
  61.1 21.7 %collective-permute-done.5 = bf16[256,2048]{1,0:T(8,128)(2,1)S(1)} collective-permute-done((bf16[256,2048]{1,0:T(8,128)(2,1)S(1)}, bf16[256,2048]{1,0:T(8,128)(2,1)S(1)}, u32[]{:S(2)}, u32[]{:S(2)}) %collective-permute-start.5) | collective-permute-done | bytes 1048608 | tf_op jit(solution)/shard_map/ppermute | solution.py:12
  83.4 22.4 %collective-permute-done.6 = bf16[256,2048]{1,0:T(8,128)(2,1)S(1)} collective-permute-done((bf16[256,2048]{1,0:T(8,128)(2,1)S(1)}, bf16[256,2048]{1,0:T(8,128)(2,1)S(1)}, u32[]{:S(2)}, u32[]{:S(2)}) %collective-permute-start.6) | collective-permute-done | bytes 1048608 | tf_op jit(solution)/shard_map/ppermute | solution.py:12
  105.9 8.8 %collective-permute-start.8 = (bf16[256,2048]{1,0:T(8,128)(2,1)S(1)}, bf16[256,2048]{1,0:T(8,128)(2,1)S(1)}, u32[]{:S(2)}, u32[]{:S(2)}) collective-permute-start(bf16[256,2048]{1,0:T(8,128)(2,1)S(1)} %broadcast_select_fusion.7), channel_id=1, source_target_pairs={{16,0},{32,16},{48,32},{64,48},{80,64},{96,80},{112,96},{128,112},... | collective-permute-start | bytes 3145736 | tf_op jit(solution)/shard_map/ppermute | solution.py:12
  115.0 5.6 collective-permute-start
  120.6 3.3 collective-permute-done
  126.7 6.2 %collective-permute-done.8 = bf16[256,2048]{1,0:T(8,128)(2,1)S(1)} collective-permute-done((bf16[256,2048]{1,0:T(8,128)(2,1)S(1)}, bf16[256,2048]{1,0:T(8,128)(2,1)S(1)}, u32[]{:S(2)}, u32[]{:S(2)}) %collective-permute-start.8) | collective-permute-done | bytes 1048608 | tf_op jit(solution)/shard_map/ppermute | solution.py:12
  132.9 5.5 collective-permute-start.10
  138.5 7.0 %collective-permute-start.2 = (bf16[256,512]{1,0:T(8,128)(2,1)S(1)}, bf16[256,512]{1,0:T(8,128)(2,1)S(1)}, u32[]{:S(2)}, u32[]{:S(2)}) collective-permute-start(bf16[256,512]{1,0:T(8,128)(2,1)S(1)} %broadcast_select_fusion.15), channel_id=1, source_target_pairs={{8,0},{10,2},{12,4},{14,6},{0,8},{2,10},{4,12},{6,14},{9,1},{11,3}... | collective-permute-start | bytes 786440 | tf_op jit(solution)/shard_map/ppermute | solution.py:12
  145.5 3.9 collective-permute-done.2
  149.4 5.1 collective-permute-start.7
  155.6 5.6 collective-permute-start.12
  161.6 5.4 collective-permute-start.9
  167.0 3.3 collective-permute-done.9
  173.5 4.4 collective-permute-done.12
  177.9 5.5 collective-permute-start.14
  183.4 5.8 collective-permute-start.13
  195.8 3.7 collective-permute-done.14
  199.5 5.5 collective-permute-start.16
  205.1 5.6 collective-permute-start.17
  210.7 3.3 collective-permute-done.17
  221.1 5.5 collective-permute-start.18
  230.5 12.3 %collective-permute-done.18 = bf16[256,2048]{1,0:T(8,128)(2,1)S(1)} collective-permute-done((bf16[256,2048]{1,0:T(8,128)(2,1)}, bf16[256,2048]{1,0:T(8,128)(2,1)S(1)}, u32[]{:S(2)}, u32[]{:S(2)}) %collective-permute-start.18) | collective-permute-done | bytes 1048608 | tf_op jit(solution)/shard_map/ppermute | solution.py:12
  242.7 5.4 collective-permute-start.20
  252.0 12.2 %collective-permute-done.20 = bf16[256,2048]{1,0:T(8,128)(2,1)S(1)} collective-permute-done((bf16[256,2048]{1,0:T(8,128)(2,1)S(1)}, bf16[256,2048]{1,0:T(8,128)(2,1)S(1)}, u32[]{:S(2)}, u32[]{:S(2)}) %collective-permute-start.20) | collective-permute-done | bytes 1048608 | tf_op jit(solution)/shard_map/ppermute | solution.py:12
  266.1 45.8 %all-reduce.2.cloned.1.call-done = f32[256,2048]{1,0:T(8,128)} async-done(((f32[256,2048]{1,0:T(8,128)}), f32[256,2048]{1,0:T(8,128)}) %all-reduce.2.cloned.1.call-update) | async-done | bytes 2097168 | tf_op jit(solution)/shard_map/psum | solution.py:65
  313.8 4.4 collective-permute-start.21
  318.2 22.3 %collective-permute-done.21 = bf16[256,2048]{1,0:T(8,128)(2,1)S(1)} collective-permute-done((bf16[256,2048]{1,0:T(8,128)(2,1)S(1)}, bf16[256,2048]{1,0:T(8,128)(2,1)S(1)}, u32[]{:S(2)}, u32[]{:S(2)}) %collective-permute-start.21) | collective-permute-done | bytes 1048608 | tf_op jit(solution)/shard_map/ppermute | solution.py:12
  343.3 22.6 %collective-permute-done.22 = bf16[256,2048]{1,0:T(8,128)(2,1)S(1)} collective-permute-done((bf16[256,2048]{1,0:T(8,128)(2,1)S(1)}, bf16[256,2048]{1,0:T(8,128)(2,1)S(1)}, u32[]{:S(2)}, u32[]{:S(2)}) %collective-permute-start.22) | collective-permute-done | bytes 1048608 | tf_op jit(solution)/shard_map/ppermute | solution.py:12
  366.7 22.2 %collective-permute-done.23 = bf16[256,2048]{1,0:T(8,128)(2,1)S(1)} collective-permute-done((bf16[256,2048]{1,0:T(8,128)(2,1)S(1)}, bf16[256,2048]{1,0:T(8,128)(2,1)S(1)}, u32[]{:S(2)}, u32[]{:S(2)}) %collective-permute-start.23) | collective-permute-done | bytes 1048608 | tf_op jit(solution)/shard_map/ppermute | solution.py:12
  389.6 22.8 %collective-permute-done.24 = bf16[256,2048]{1,0:T(8,128)(2,1)S(1)} collective-permute-done((bf16[256,2048]{1,0:T(8,128)(2,1)S(1)}, bf16[256,2048]{1,0:T(8,128)(2,1)S(1)}, u32[]{:S(2)}, u32[]{:S(2)}) %collective-permute-start.24) | collective-permute-done | bytes 1048608 | tf_op jit(solution)/shard_map/ppermute | solution.py:12
  412.5 9.1 %collective-permute-start.25 = (bf16[256,2048]{1,0:T(8,128)(2,1)S(1)}, bf16[256,2048]{1,0:T(8,128)(2,1)S(1)}, u32[]{:S(2)}, u32[]{:S(2)}) collective-permute-start(bf16[256,2048]{1,0:T(8,128)(2,1)S(1)} %broadcast_select_fusion.6), channel_id=1, source_target_pairs={{16,0},{32,16},{48,32},{64,48},{80,64},{96,80},{112,96},{128,112},... | collective-permute-start | bytes 3145736 | tf_op jit(solution)/shard_map/ppermute | solution.py:12
  421.6 18.7 %collective-permute-done.25 = bf16[256,2048]{1,0:T(8,128)(2,1)S(1)} collective-permute-done((bf16[256,2048]{1,0:T(8,128)(2,1)S(1)}, bf16[256,2048]{1,0:T(8,128)(2,1)S(1)}, u32[]{:S(2)}, u32[]{:S(2)}) %collective-permute-start.25) | collective-permute-done | bytes 1048608 | tf_op jit(solution)/shard_map/ppermute | solution.py:12
  440.3 5.5 collective-permute-start.26
  445.8 17.7 %collective-permute-done.26 = bf16[256,2048]{1,0:T(8,128)(2,1)S(1)} collective-permute-done((bf16[256,2048]{1,0:T(8,128)(2,1)S(1)}, bf16[256,2048]{1,0:T(8,128)(2,1)S(1)}, u32[]{:S(2)}, u32[]{:S(2)}) %collective-permute-start.26) | collective-permute-done | bytes 1048608 | tf_op jit(solution)/shard_map/ppermute | solution.py:12
  463.5 5.5 collective-permute-start.27
  469.0 16.8 %collective-permute-done.27 = bf16[256,2048]{1,0:T(8,128)(2,1)S(1)} collective-permute-done((bf16[256,2048]{1,0:T(8,128)(2,1)S(1)}, bf16[256,2048]{1,0:T(8,128)(2,1)S(1)}, u32[]{:S(2)}, u32[]{:S(2)}) %collective-permute-start.27) | collective-permute-done | bytes 1048608 | tf_op jit(solution)/shard_map/ppermute | solution.py:12
  485.9 5.5 collective-permute-start.28
  491.4 16.1 %collective-permute-done.28 = bf16[256,2048]{1,0:T(8,128)(2,1)S(1)} collective-permute-done((bf16[256,2048]{1,0:T(8,128)(2,1)S(1)}, bf16[256,2048]{1,0:T(8,128)(2,1)S(1)}, u32[]{:S(2)}, u32[]{:S(2)}) %collective-permute-start.28) | collective-permute-done | bytes 1048608 | tf_op jit(solution)/shard_map/ppermute | solution.py:12
  507.5 5.5 collective-permute-start.29
  513.4 15.7 %collective-permute-done.29 = bf16[256,2048]{1,0:T(8,128)(2,1)S(1)} collective-permute-done((bf16[256,2048]{1,0:T(8,128)(2,1)S(1)}, bf16[256,2048]{1,0:T(8,128)(2,1)S(1)}, u32[]{:S(2)}, u32[]{:S(2)}) %collective-permute-start.29) | collective-permute-done | bytes 1048608 | tf_op jit(solution)/shard_map/ppermute | solution.py:12
  529.1 5.5 collective-permute-start.30
  536.1 14.7 %collective-permute-done.30 = bf16[256,2048]{1,0:T(8,128)(2,1)S(1)} collective-permute-done((bf16[256,2048]{1,0:T(8,128)(2,1)S(1)}, bf16[256,2048]{1,0:T(8,128)(2,1)S(1)}, u32[]{:S(2)}, u32[]{:S(2)}) %collective-permute-start.30) | collective-permute-done | bytes 1048608 | tf_op jit(solution)/shard_map/ppermute | solution.py:12
  550.7 5.5 collective-permute-start.31
  557.6 14.7 %collective-permute-done.31 = bf16[256,2048]{1,0:T(8,128)(2,1)S(1)} collective-permute-done((bf16[256,2048]{1,0:T(8,128)(2,1)S(1)}, bf16[256,2048]{1,0:T(8,128)(2,1)S(1)}, u32[]{:S(2)}, u32[]{:S(2)}) %collective-permute-start.31) | collective-permute-done | bytes 1048608 | tf_op jit(solution)/shard_map/ppermute | solution.py:12
  574.2 26.6 %reduce-scatter.2.cloned.1.call-done = f32[256,1024]{1,0:T(8,128)} async-done(((f32[256,2048]{1,0:T(8,128)}), f32[256,1024]{1,0:T(8,128)}) %reduce-scatter.2.cloned.1.call-update) | async-done | bytes 1048592 | tf_op jit(solution)/shard_map/reduce_scatter | solution.py:69
  (80 shorter events, 49.6 us)
Async XLA Ops:
  6.5 305.3 %all-reduce.2.cloned.1.call-start = ((), (), s32[]{:S(2)}) async-start(), calls=%async_computation.1 | async-start | bytes 4194304 | tf_op jit(solution)/shard_map/psum | solution.py:65
  6.5 27.9 %collective-permute-start.3 = (bf16[256,2048]{1,0:T(8,128)(2,1)}, bf16[256,2048]{1,0:T(8,128)(2,1)S(1)}, u32[]{:S(2)}, u32[]{:S(2)}) collective-permute-start(bf16[256,2048]{1,0:T(8,128)(2,1)} %param.4), channel_id=1, source_target_pairs={{16,0},{32,16},{48,32},{64,48},{80,64},{96,80},{112,96},{128,112},... | collective-permute-start | bytes 3145736 | tf_op jit(solution)/shard_map/ppermute | solution.py:12
  35.8 24.7 %collective-permute-start.4 = (bf16[256,2048]{1,0:T(8,128)(2,1)S(1)}, bf16[256,2048]{1,0:T(8,128)(2,1)S(1)}, u32[]{:S(2)}, u32[]{:S(2)}) collective-permute-start(bf16[256,2048]{1,0:T(8,128)(2,1)S(1)} %broadcast_select_fusion.1), channel_id=1, source_target_pairs={{32,0},{48,16},{64,32},{80,48},{96,64},{112,80},{128,96},{144,112}... | collective-permute-start | bytes 3145736 | tf_op jit(solution)/shard_map/ppermute | solution.py:12
  60.6 22.3 %collective-permute-start.5 = (bf16[256,2048]{1,0:T(8,128)(2,1)S(1)}, bf16[256,2048]{1,0:T(8,128)(2,1)S(1)}, u32[]{:S(2)}, u32[]{:S(2)}) collective-permute-start(bf16[256,2048]{1,0:T(8,128)(2,1)S(1)} %broadcast_select_fusion.3), channel_id=1, source_target_pairs={{64,0},{80,16},{96,32},{112,48},{128,64},{144,80},{160,96},{176,11... | collective-permute-start | bytes 3145736 | tf_op jit(solution)/shard_map/ppermute | solution.py:12
  83.0 31.8 %copy-start.9 = (s32[2,4]{1,0:T(2,128)S(1)}, s32[2,4]{1,0:T(2,128)}, u32[]{:S(2)}) copy-start(s32[2,4]{1,0:T(2,128)} %param.5) | copy-start | bytes 100
  83.0 31.9 %copy-start.6 = (bf16[256,512]{1,0:T(8,128)(2,1)S(1)}, bf16[256,512]{1,0:T(8,128)(2,1)}, u32[]{:S(2)}) copy-start(bf16[256,512]{1,0:T(8,128)(2,1)} %param.3) | copy-start | bytes 786436
  83.0 22.9 %collective-permute-start.6 = (bf16[256,2048]{1,0:T(8,128)(2,1)S(1)}, bf16[256,2048]{1,0:T(8,128)(2,1)S(1)}, u32[]{:S(2)}, u32[]{:S(2)}) collective-permute-start(bf16[256,2048]{1,0:T(8,128)(2,1)S(1)} %broadcast_select_fusion.5), channel_id=1, source_target_pairs={{128,0},{144,16},{160,32},{176,48},{192,64},{208,80},{224,96},{240... | collective-permute-start | bytes 3145736 | tf_op jit(solution)/shard_map/ppermute | solution.py:12
  105.9 27.0 %collective-permute-start.8 = (bf16[256,2048]{1,0:T(8,128)(2,1)S(1)}, bf16[256,2048]{1,0:T(8,128)(2,1)S(1)}, u32[]{:S(2)}, u32[]{:S(2)}) collective-permute-start(bf16[256,2048]{1,0:T(8,128)(2,1)S(1)} %broadcast_select_fusion.7), channel_id=1, source_target_pairs={{16,0},{32,16},{48,32},{64,48},{80,64},{96,80},{112,96},{128,112},... | collective-permute-start | bytes 3145736 | tf_op jit(solution)/shard_map/ppermute | solution.py:12
  115.0 9.0 %collective-permute-start = (bf16[256,512]{1,0:T(8,128)(2,1)S(1)}, bf16[256,512]{1,0:T(8,128)(2,1)S(1)}, u32[]{:S(2)}, u32[]{:S(2)}) collective-permute-start(bf16[256,512]{1,0:T(8,128)(2,1)S(1)} %bitcast_multiply_fusion), channel_id=1, source_target_pairs={{2,0},{4,2},{6,4},{8,6},{10,8},{12,10},{14,12},{0,14},{3,1},{5,3},... | collective-permute-start | bytes 786440 | tf_op jit(solution)/shard_map/ppermute | solution.py:12
  124.0 14.5 %collective-permute-start.1 = (bf16[256,512]{1,0:T(8,128)(2,1)S(1)}, bf16[256,512]{1,0:T(8,128)(2,1)S(1)}, u32[]{:S(2)}, u32[]{:S(2)}) collective-permute-start(bf16[256,512]{1,0:T(8,128)(2,1)S(1)} %broadcast_select_fusion.14), channel_id=1, source_target_pairs={{4,0},{6,2},{8,4},{10,6},{12,8},{14,10},{0,12},{2,14},{5,1},{7,3},... | collective-permute-start | bytes 786440 | tf_op jit(solution)/shard_map/ppermute | solution.py:12
  132.9 56.4 %copy-start.5 = (bf16[256,2048]{1,0:T(8,128)(2,1)}, bf16[256,2048]{1,0:T(8,128)(2,1)S(1)}, u32[]{:S(2)}) copy-start(bf16[256,2048]{1,0:T(8,128)(2,1)S(1)} %collective-permute-done.8) | copy-start | bytes 3145732
  132.9 22.7 %collective-permute-start.10 = (bf16[256,2048]{1,0:T(8,128)(2,1)S(1)}, bf16[256,2048]{1,0:T(8,128)(2,1)}, u32[]{:S(2)}, u32[]{:S(2)}) collective-permute-start(bf16[256,2048]{1,0:T(8,128)(2,1)S(1)} %collective-permute-done.8), channel_id=1, source_target_pairs={{16,0},{32,16},{48,32},{64,48},{80,64},{96,80},{112,96},{128,112},... | collective-permute-start | bytes 3145736 | tf_op jit(solution)/shard_map/ppermute | solution.py:12
  138.5 10.9 %collective-permute-start.2 = (bf16[256,512]{1,0:T(8,128)(2,1)S(1)}, bf16[256,512]{1,0:T(8,128)(2,1)S(1)}, u32[]{:S(2)}, u32[]{:S(2)}) collective-permute-start(bf16[256,512]{1,0:T(8,128)(2,1)S(1)} %broadcast_select_fusion.15), channel_id=1, source_target_pairs={{8,0},{10,2},{12,4},{14,6},{0,8},{2,10},{4,12},{6,14},{9,1},{11,3}... | collective-permute-start | bytes 786440 | tf_op jit(solution)/shard_map/ppermute | solution.py:12
  149.4 12.2 %collective-permute-start.7 = (bf16[256,512]{1,0:T(8,128)(2,1)S(1)}, bf16[256,512]{1,0:T(8,128)(2,1)S(1)}, u32[]{:S(2)}, u32[]{:S(2)}) collective-permute-start(bf16[256,512]{1,0:T(8,128)(2,1)S(1)} %broadcast_select_fusion.16), channel_id=1, source_target_pairs={{2,0},{4,2},{6,4},{8,6},{10,8},{12,10},{14,12},{0,14},{3,1},{5,3},... | collective-permute-start | bytes 786440 | tf_op jit(solution)/shard_map/ppermute | solution.py:12
  155.6 22.2 %collective-permute-start.12 = (bf16[256,2048]{1,0:T(8,128)(2,1)}, bf16[256,2048]{1,0:T(8,128)(2,1)}, u32[]{:S(2)}, u32[]{:S(2)}) collective-permute-start(bf16[256,2048]{1,0:T(8,128)(2,1)} %collective-permute-done.10), channel_id=1, source_target_pairs={{16,0},{32,16},{48,32},{64,48},{80,64},{96,80},{112,96},{128,112},... | collective-permute-start | bytes 3145736 | tf_op jit(solution)/shard_map/ppermute | solution.py:12
  161.6 8.7 %collective-permute-start.9 = (bf16[256,512]{1,0:T(8,128)(2,1)S(1)}, bf16[256,512]{1,0:T(8,128)(2,1)S(1)}, u32[]{:S(2)}, u32[]{:S(2)}) collective-permute-start(bf16[256,512]{1,0:T(8,128)(2,1)S(1)} %broadcast_select_fusion.13), channel_id=1, source_target_pairs={{2,0},{4,2},{6,4},{8,6},{10,8},{12,10},{14,12},{0,14},{3,1},{5,3},... | collective-permute-start | bytes 786440 | tf_op jit(solution)/shard_map/ppermute | solution.py:12
  170.3 13.1 %collective-permute-start.11 = (bf16[256,512]{1,0:T(8,128)(2,1)S(1)}, bf16[256,512]{1,0:T(8,128)(2,1)S(1)}, u32[]{:S(2)}, u32[]{:S(2)}) collective-permute-start(bf16[256,512]{1,0:T(8,128)(2,1)S(1)} %broadcast_select_fusion.12), channel_id=1, source_target_pairs={{2,0},{4,2},{6,4},{8,6},{10,8},{12,10},{14,12},{0,14},{3,1},{5,3},... | collective-permute-start | bytes 786440 | tf_op jit(solution)/shard_map/ppermute | solution.py:12
  177.9 21.6 %collective-permute-start.14 = (bf16[256,2048]{1,0:T(8,128)(2,1)}, bf16[256,2048]{1,0:T(8,128)(2,1)}, u32[]{:S(2)}, u32[]{:S(2)}) collective-permute-start(bf16[256,2048]{1,0:T(8,128)(2,1)} %collective-permute-done.12), channel_id=1, source_target_pairs={{16,0},{32,16},{48,32},{64,48},{80,64},{96,80},{112,96},{128,112},... | collective-permute-start | bytes 3145736 | tf_op jit(solution)/shard_map/ppermute | solution.py:12
  183.4 9.1 %collective-permute-start.13 = (bf16[256,512]{1,0:T(8,128)(2,1)S(1)}, bf16[256,512]{1,0:T(8,128)(2,1)S(1)}, u32[]{:S(2)}, u32[]{:S(2)}) collective-permute-start(bf16[256,512]{1,0:T(8,128)(2,1)S(1)} %broadcast_select_fusion.11), channel_id=1, source_target_pairs={{2,0},{4,2},{6,4},{8,6},{10,8},{12,10},{14,12},{0,14},{3,1},{5,3},... | collective-permute-start | bytes 786440 | tf_op jit(solution)/shard_map/ppermute | solution.py:12
  192.6 55.5 %copy-start.1 = (bf16[256,512]{1,0:T(8,128)(2,1)}, bf16[256,512]{1,0:T(8,128)(2,1)S(1)}, u32[]{:S(2)}) copy-start(bf16[256,512]{1,0:T(8,128)(2,1)S(1)} %broadcast_select_fusion.10) | copy-start | bytes 786436
  192.6 12.4 %collective-permute-start.15 = (bf16[256,512]{1,0:T(8,128)(2,1)S(1)}, bf16[256,512]{1,0:T(8,128)(2,1)S(1)}, u32[]{:S(2)}, u32[]{:S(2)}) collective-permute-start(bf16[256,512]{1,0:T(8,128)(2,1)S(1)} %broadcast_select_fusion.10), channel_id=1, source_target_pairs={{2,0},{4,2},{6,4},{8,6},{10,8},{12,10},{14,12},{0,14},{3,1},{5,3},... | collective-permute-start | bytes 786440 | tf_op jit(solution)/shard_map/ppermute | solution.py:12
  199.5 21.6 %collective-permute-start.16 = (bf16[256,2048]{1,0:T(8,128)(2,1)}, bf16[256,2048]{1,0:T(8,128)(2,1)}, u32[]{:S(2)}, u32[]{:S(2)}) collective-permute-start(bf16[256,2048]{1,0:T(8,128)(2,1)} %collective-permute-done.14), channel_id=1, source_target_pairs={{16,0},{32,16},{48,32},{64,48},{80,64},{96,80},{112,96},{128,112},... | collective-permute-start | bytes 3145736 | tf_op jit(solution)/shard_map/ppermute | solution.py:12
  205.1 44.8 %copy-start.3 = (bf16[256,512]{1,0:T(8,128)(2,1)}, bf16[256,512]{1,0:T(8,128)(2,1)S(1)}, u32[]{:S(2)}) copy-start(bf16[256,512]{1,0:T(8,128)(2,1)S(1)} %broadcast_select_fusion.9) | copy-start | bytes 786436
  205.1 9.0 %collective-permute-start.17 = (bf16[256,512]{1,0:T(8,128)(2,1)S(1)}, bf16[256,512]{1,0:T(8,128)(2,1)S(1)}, u32[]{:S(2)}, u32[]{:S(2)}) collective-permute-start(bf16[256,512]{1,0:T(8,128)(2,1)S(1)} %broadcast_select_fusion.9), channel_id=1, source_target_pairs={{2,0},{4,2},{6,4},{8,6},{10,8},{12,10},{14,12},{0,14},{3,1},{5,3},... | collective-permute-start | bytes 786440 | tf_op jit(solution)/shard_map/ppermute | solution.py:12
  214.1 37.9 %collective-permute-start.19 = (bf16[256,512]{1,0:T(8,128)(2,1)S(1)}, bf16[256,512]{1,0:T(8,128)(2,1)S(1)}, u32[]{:S(2)}, u32[]{:S(2)}) collective-permute-start(bf16[256,512]{1,0:T(8,128)(2,1)S(1)} %broadcast_select_fusion.8), channel_id=1, source_target_pairs={{2,0},{4,2},{6,4},{8,6},{10,8},{12,10},{14,12},{0,14},{3,1},{5,3},... | collective-permute-start | bytes 786440 | tf_op jit(solution)/shard_map/ppermute | solution.py:12
  221.1 21.6 %collective-permute-start.18 = (bf16[256,2048]{1,0:T(8,128)(2,1)}, bf16[256,2048]{1,0:T(8,128)(2,1)S(1)}, u32[]{:S(2)}, u32[]{:S(2)}) collective-permute-start(bf16[256,2048]{1,0:T(8,128)(2,1)} %collective-permute-done.16), channel_id=1, source_target_pairs={{16,0},{32,16},{48,32},{64,48},{80,64},{96,80},{112,96},{128,112},... | collective-permute-start | bytes 3145736 | tf_op jit(solution)/shard_map/ppermute | solution.py:12
  242.7 21.5 %collective-permute-start.20 = (bf16[256,2048]{1,0:T(8,128)(2,1)S(1)}, bf16[256,2048]{1,0:T(8,128)(2,1)S(1)}, u32[]{:S(2)}, u32[]{:S(2)}) collective-permute-start(bf16[256,2048]{1,0:T(8,128)(2,1)S(1)} %collective-permute-done.18), channel_id=1, source_target_pairs={{16,0},{32,16},{48,32},{64,48},{80,64},{96,80},{112,96},{128,112},... | collective-permute-start | bytes 3145736 | tf_op jit(solution)/shard_map/ppermute | solution.py:12
  252.0 12.2 %copy-start.7 = (bf16[256,512]{1,0:T(8,128)(2,1)}, bf16[256,512]{1,0:T(8,128)(2,1)S(1)}, u32[]{:S(2)}) copy-start(bf16[256,512]{1,0:T(8,128)(2,1)S(1)} %collective-permute-done.19) | copy-start | bytes 786436
  266.1 334.8 %reduce-scatter.2.cloned.1.call-start = ((), (), s32[]{:S(2)}) async-start(), calls=%async_computation.2 | async-start | bytes 3145728 | tf_op jit(solution)/shard_map/reduce_scatter | solution.py:69
  311.9 28.6 %copy-start = (f32[256,2048]{1,0:T(8,128)S(1)}, f32[256,2048]{1,0:T(8,128)}, u32[]{:S(2)}) copy-start(f32[256,2048]{1,0:T(8,128)} %all-reduce.2.cloned.1.call-done) | copy-start | bytes 6291460
  313.8 26.7 %collective-permute-start.21 = (bf16[256,2048]{1,0:T(8,128)(2,1)S(1)}, bf16[256,2048]{1,0:T(8,128)(2,1)S(1)}, u32[]{:S(2)}, u32[]{:S(2)}) collective-permute-start(bf16[256,2048]{1,0:T(8,128)(2,1)S(1)} %convert_element_type.10), channel_id=1, source_target_pairs={{16,0},{32,16},{48,32},{64,48},{80,64},{96,80},{112,96},{128,112},... | collective-permute-start | bytes 3145736 | tf_op jit(solution)/shard_map/ppermute | solution.py:12
  340.8 25.2 %collective-permute-start.22 = (bf16[256,2048]{1,0:T(8,128)(2,1)S(1)}, bf16[256,2048]{1,0:T(8,128)(2,1)S(1)}, u32[]{:S(2)}, u32[]{:S(2)}) collective-permute-start(bf16[256,2048]{1,0:T(8,128)(2,1)S(1)} %broadcast_select_fusion), channel_id=1, source_target_pairs={{32,0},{48,16},{64,32},{80,48},{96,64},{112,80},{128,96},{144,112}... | collective-permute-start | bytes 3145736 | tf_op jit(solution)/shard_map/ppermute | solution.py:12
  366.1 22.8 %collective-permute-start.23 = (bf16[256,2048]{1,0:T(8,128)(2,1)S(1)}, bf16[256,2048]{1,0:T(8,128)(2,1)S(1)}, u32[]{:S(2)}, u32[]{:S(2)}) collective-permute-start(bf16[256,2048]{1,0:T(8,128)(2,1)S(1)} %broadcast_select_fusion.2), channel_id=1, source_target_pairs={{64,0},{80,16},{96,32},{112,48},{128,64},{144,80},{160,96},{176,11... | collective-permute-start | bytes 3145736 | tf_op jit(solution)/shard_map/ppermute | solution.py:12
  389.0 23.4 %collective-permute-start.24 = (bf16[256,2048]{1,0:T(8,128)(2,1)S(1)}, bf16[256,2048]{1,0:T(8,128)(2,1)S(1)}, u32[]{:S(2)}, u32[]{:S(2)}) collective-permute-start(bf16[256,2048]{1,0:T(8,128)(2,1)S(1)} %broadcast_select_fusion.4), channel_id=1, source_target_pairs={{128,0},{144,16},{160,32},{176,48},{192,64},{208,80},{224,96},{240... | collective-permute-start | bytes 3145736 | tf_op jit(solution)/shard_map/ppermute | solution.py:12
  412.5 27.8 %collective-permute-start.25 = (bf16[256,2048]{1,0:T(8,128)(2,1)S(1)}, bf16[256,2048]{1,0:T(8,128)(2,1)S(1)}, u32[]{:S(2)}, u32[]{:S(2)}) collective-permute-start(bf16[256,2048]{1,0:T(8,128)(2,1)S(1)} %broadcast_select_fusion.6), channel_id=1, source_target_pairs={{16,0},{32,16},{48,32},{64,48},{80,64},{96,80},{112,96},{128,112},... | collective-permute-start | bytes 3145736 | tf_op jit(solution)/shard_map/ppermute | solution.py:12
  440.3 23.3 %collective-permute-start.26 = (bf16[256,2048]{1,0:T(8,128)(2,1)S(1)}, bf16[256,2048]{1,0:T(8,128)(2,1)S(1)}, u32[]{:S(2)}, u32[]{:S(2)}) collective-permute-start(bf16[256,2048]{1,0:T(8,128)(2,1)S(1)} %collective-permute-done.25), channel_id=1, source_target_pairs={{16,0},{32,16},{48,32},{64,48},{80,64},{96,80},{112,96},{128,112},... | collective-permute-start | bytes 3145736 | tf_op jit(solution)/shard_map/ppermute | solution.py:12
  463.5 22.3 %collective-permute-start.27 = (bf16[256,2048]{1,0:T(8,128)(2,1)S(1)}, bf16[256,2048]{1,0:T(8,128)(2,1)S(1)}, u32[]{:S(2)}, u32[]{:S(2)}) collective-permute-start(bf16[256,2048]{1,0:T(8,128)(2,1)S(1)} %collective-permute-done.26), channel_id=1, source_target_pairs={{16,0},{32,16},{48,32},{64,48},{80,64},{96,80},{112,96},{128,112},... | collective-permute-start | bytes 3145736 | tf_op jit(solution)/shard_map/ppermute | solution.py:12
  485.9 21.6 %collective-permute-start.28 = (bf16[256,2048]{1,0:T(8,128)(2,1)S(1)}, bf16[256,2048]{1,0:T(8,128)(2,1)S(1)}, u32[]{:S(2)}, u32[]{:S(2)}) collective-permute-start(bf16[256,2048]{1,0:T(8,128)(2,1)S(1)} %collective-permute-done.27), channel_id=1, source_target_pairs={{16,0},{32,16},{48,32},{64,48},{80,64},{96,80},{112,96},{128,112},... | collective-permute-start | bytes 3145736 | tf_op jit(solution)/shard_map/ppermute | solution.py:12
  507.5 21.6 %collective-permute-start.29 = (bf16[256,2048]{1,0:T(8,128)(2,1)S(1)}, bf16[256,2048]{1,0:T(8,128)(2,1)S(1)}, u32[]{:S(2)}, u32[]{:S(2)}) collective-permute-start(bf16[256,2048]{1,0:T(8,128)(2,1)S(1)} %collective-permute-done.28), channel_id=1, source_target_pairs={{16,0},{32,16},{48,32},{64,48},{80,64},{96,80},{112,96},{128,112},... | collective-permute-start | bytes 3145736 | tf_op jit(solution)/shard_map/ppermute | solution.py:12
  529.1 21.6 %collective-permute-start.30 = (bf16[256,2048]{1,0:T(8,128)(2,1)S(1)}, bf16[256,2048]{1,0:T(8,128)(2,1)S(1)}, u32[]{:S(2)}, u32[]{:S(2)}) collective-permute-start(bf16[256,2048]{1,0:T(8,128)(2,1)S(1)} %collective-permute-done.29), channel_id=1, source_target_pairs={{16,0},{32,16},{48,32},{64,48},{80,64},{96,80},{112,96},{128,112},... | collective-permute-start | bytes 3145736 | tf_op jit(solution)/shard_map/ppermute | solution.py:12
  535.6 20.7 %copy-start.2 = (bf16[256,512]{1,0:T(8,128)(2,1)S(1)}, bf16[256,512]{1,0:T(8,128)(2,1)}, u32[]{:S(2)}) copy-start(bf16[256,512]{1,0:T(8,128)(2,1)} %copy-done.1) | copy-start | bytes 786436
  536.1 20.6 %copy-start.4 = (bf16[256,512]{1,0:T(8,128)(2,1)S(1)}, bf16[256,512]{1,0:T(8,128)(2,1)}, u32[]{:S(2)}) copy-start(bf16[256,512]{1,0:T(8,128)(2,1)} %copy-done.3) | copy-start | bytes 786436
  550.7 21.6 %collective-permute-start.31 = (bf16[256,2048]{1,0:T(8,128)(2,1)S(1)}, bf16[256,2048]{1,0:T(8,128)(2,1)S(1)}, u32[]{:S(2)}, u32[]{:S(2)}) collective-permute-start(bf16[256,2048]{1,0:T(8,128)(2,1)S(1)} %collective-permute-done.30), channel_id=1, source_target_pairs={{16,0},{32,16},{48,32},{64,48},{80,64},{96,80},{112,96},{128,112},... | collective-permute-start | bytes 3145736 | tf_op jit(solution)/shard_map/ppermute | solution.py:12
  557.2 15.1 %copy-start.8 = (bf16[256,512]{1,0:T(8,128)(2,1)S(1)}, bf16[256,512]{1,0:T(8,128)(2,1)}, u32[]{:S(2)}) copy-start(bf16[256,512]{1,0:T(8,128)(2,1)} %copy-done.7) | copy-start | bytes 786436
Sparse Core Ops, SparseCore 0:
  266.2 45.6 all-reduce.1
  574.3 26.4 reduce-scatter.1
where the time goes:
time: 610 us
  waiting for transfers between devices  425 us (70%)
  starting transfers between devices  149 us (24%)
  matrix products  16.1 us (3%)
  between operations  13.7 us (2%)
  other arithmetic  6.65 us (1%)
    ppermute x32, waiting for transfers between devices, passed_along(): return lax.ppermute(block, axis, route)  352 us
    ppermute x32, starting transfers between devices, passed_along(): return lax.ppermute(block, axis, route)  148 us
    psum x1, waiting for transfers between devices, shards(): square = lax.psum(partial_value, 'layer')  45.8 us
    reduce_scatter x1, waiting for transfers between devices, shards(): lax.psum_scatter(partial_cubic, 'layer', scatter_dimension=1, tiled=True)  26.6 us
    dot_general x16, matrix products, multiply(): jnp.dot(section, right_tile, preferred_element_type=jnp.float32)  16.1 us
  transfers between devices with their start and end apart: 34, of which 30 were waited for; matrix products, arithmetic and copies ran while one was open for 2% of the time, Pallas kernels for 0%

commit v1 on v0

v1 whole, which is shorter than its diff:
```python
import jax
import jax.numpy as jnp
from jax import lax
from jax.experimental import pallas as pl
from jax.experimental.pallas import tpu as pltpu
from jax.sharding import Mesh, PartitionSpec as P

BS = 128
NY, NX, NZ, NC = 4, 4, 8, 2
ROWS, INNER = 256, 512
HALF = NZ // 2
BF16, F32 = jnp.bfloat16, jnp.float32


def row_routes():
    routes = []
    for k in range(HALF):
        route = []
        for z in range(NZ):
            for c in range(NC):
                source = (HALF * c + (z + k) % HALF) * NC + z // HALF
                route.append((source, z * NC + c))
        routes.append(route)
    return routes


def column_routes():
    routes = []
    for i in range(2):
        for j in range(NX):
            route = []
            for y in range(NY):
                for x in range(NX):
                    for c in range(NC):
                        source_y, source_x = 2 * c + (y + i) % 2, (x + j) % NX
                        source = (source_y * NX + source_x) * NC + y // 2
                        route.append((source, (y * NX + x) * NC + c))
            routes.append(route)
    return routes


SWAP = [(0, 1), (1, 0)]


def square_kernel(place, *refs):
    row_refs, col_refs = refs[:HALF], refs[HALF : HALF + 2 * NX]
    out_ref, left, right = refs[HALF + 2 * NX :]
    y, x, z = place[0], place[1], place[2]
    for k in range(HALF):
        at = pl.multiple_of((z + k) % HALF * INNER, INNER)
        left[:, pl.ds(at, INNER)] = row_refs[k][...]
    for i in range(2):
        for j in range(NX):
            at = pl.multiple_of(((y + i) % 2 * NX + (x + j) % NX) * ROWS, ROWS)
            right[pl.ds(at, ROWS), :] = col_refs[i * NX + j][...]
    out_ref[...] = jnp.dot(left[...], right[...], preferred_element_type=F32)


def partial_square(place, rows, cols):
    vmem = pl.BlockSpec(memory_space=pltpu.VMEM)
    return pl.pallas_call(
        square_kernel,
        out_shape=jax.ShapeDtypeStruct((ROWS, INNER), F32),
        in_specs=[pl.BlockSpec(memory_space=pltpu.SMEM)] + [vmem] * (len(rows) + len(cols)),
        out_specs=vmem,
        scratch_shapes=[
            pltpu.VMEM((ROWS, HALF * INNER), BF16),
            pltpu.VMEM((HALF * INNER, INNER), BF16),
        ],
        compiler_params=pltpu.CompilerParams(vmem_limit_bytes=32 * 1024 * 1024),
        cost_estimate=pl.CostEstimate(
            flops=2 * ROWS * INNER * HALF * INNER, bytes_accessed=4 << 20, transcendentals=0
        ),
    )(place, *rows, *cols)


def gather_rows(block):
    return [lax.ppermute(block, ("z", "c"), route) for route in row_routes()]


def assemble(own, core, z):
    other = lax.ppermute(jnp.concatenate(own, 1), "c", SWAP)
    mine = jnp.concatenate(own, 1)
    start = (HALF - z % HALF) % HALF * INNER

    def in_place(part):
        return lax.dynamic_slice_in_dim(
            jnp.concatenate([part, part], 1), start, HALF * INNER, 1
        )

    mine, other = in_place(mine), in_place(other)
    return jnp.where(
        core == 0,
        jnp.concatenate([mine, other], 1),
        jnp.concatenate([other, mine], 1),
    )


def shards(density, panel, pattern):
    y, x, z, core = (lax.axis_index(name) for name in ("y", "x", "z", "c"))
    mask = pattern.astype(BF16)
    filtered = (
        density.reshape(ROWS // BS, BS, INNER // BS, BS) * mask[:, None, :, None]
    ).reshape(ROWS, INNER)
    width = panel.shape[1] // NC
    mine = lax.dynamic_slice_in_dim(panel, core * width, width, 1)
    panel_cols = lax.all_gather(mine, ("y", "x"), axis=0, tiled=True)

    rows = gather_rows(filtered)
    cols = [lax.ppermute(filtered, ("y", "x", "c"), route) for route in column_routes()]
    place = jnp.stack([y, x, z]).astype(jnp.int32)
    part = partial_square(place, rows, cols)
    squared = (part + lax.ppermute(part, "c", SWAP)).astype(BF16)
    squared_rows = assemble(gather_rows(squared), core, z)
    filtered_rows = assemble(rows, core, z)
    first = jnp.dot(filtered_rows, panel_cols, preferred_element_type=F32)
    second = jnp.dot(squared_rows, panel_cols, preferred_element_type=F32)
    return (3.0 * first - 2.0 * second).astype(BF16)


def solution(mesh):
    fine = Mesh(mesh.devices.reshape(NY, NX, NZ, NC), ("y", "x", "z", "c"))
    rows = ("y", "x")
    return jax.shard_map(
        shards,
        mesh=fine,
        in_specs=(P(rows, "z"), P(rows, "z"), P(rows, "z")),
        out_specs=P(rows, ("z", "c")),
        check_vma=False,
    )
```

time: 610 us -> 130 us (0.21)
  waiting for transfers between devices: 425 us -> 52.1 us
  starting transfers between devices: 149 us -> 42.1 us
  matrix products: 16.1 us -> 9.75 us
    ppermute x32 -> x19, waiting for transfers between devices: 352 us -> 52.1 us  [the longest x8 35.8 us: gather_rows(): return [lax.ppermute(block, ('z', 'c'), route) for route in row_routes()]]
    ppermute x32 -> x19, starting transfers between devices: 148 us -> 42.1 us  [the longest x8 28.2 us: gather_rows(): return [lax.ppermute(block, ('z', 'c'), route) for route in row_routes()]]
    psum x1 -> x0, waiting for transfers between devices: 45.8 us -> none  [shards(): square = lax.psum(partial_value, 'layer')]
    reduce_scatter x1 -> x0, waiting for transfers between devices: 26.6 us -> none  [shards(): lax.psum_scatter(partial_cubic, 'layer', scatter_dimension=1, tiled=True)]
    dot_general x16 -> x2, matrix products: 16.1 us -> 9.75 us  [the longest x1 6.49 us: shards(): second = jnp.dot(squared_rows, panel_cols, preferred_element_type=F32)]
  transfers between devices with their start and end apart: 34 -> 20, of which waited for: 30 -> 13; matrix products, arithmetic and copies ran while one was open for 2% -> 5% of each run, Pallas kernels for 0% -> 2%
where the time goes in v1:
time: 130 us; the launch traced here: 129 us
  waiting for transfers between devices  52.1 us (40%)
  starting transfers between devices  42.1 us (32%)
  between operations  13.7 us (11%)
  matrix products  9.75 us (8%)
  other arithmetic  5.99 us (5%)
  local copies, waits for them, and re-layouts  3.02 us (2%)
  Pallas kernels  2.01 us (2%)
    ppermute x8, waiting for transfers between devices, gather_rows(): return [lax.ppermute(block, ('z', 'c'), route) for route in row_routes()]  35.8 us
    ppermute x8, starting transfers between devices, gather_rows(): return [lax.ppermute(block, ('z', 'c'), route) for route in row_routes()]  28.2 us
    ppermute x8, waiting for transfers between devices, shards(): lax.ppermute(filtered, ('y', 'x', 'c'), route)  14.8 us
    ppermute x8, starting transfers between devices, shards(): lax.ppermute(filtered, ('y', 'x', 'c'), route)  13 us
    dot_general x1, matrix products, shards(): second = jnp.dot(squared_rows, panel_cols, preferred_element_type=F32)  6.49 us
    dot_general x1, matrix products, shards(): first = jnp.dot(filtered_rows, panel_cols, preferred_element_type=F32)  3.26 us
    concatenate x2, other arithmetic, in_place(): jnp.concatenate([part, part], 1)  3.18 us
  transfers between devices with their start and end apart: 20, of which 13 were waited for; matrix products, arithmetic and copies ran while one was open for 5% of the time, Pallas kernels for 2%

profile of v1, /device:TPU:1, one launch (start us, length us, event | category | flops | bytes accessed | tf_op | source)
XLA Modules:
  0.0 128.7 jit_solution(15517354936880953091)
XLA Ops:
  6.5 1.2 copy-done
  7.8 0.8 constant_dynamic-slice_fusion.1
  8.6 0.0 all-gather.2.cloned.1.call-update
  8.6 0.7 convert_element_type.9
  9.3 0.1 mul.30
  9.5 1.7 %bitcast_multiply_fusion = bf16[256,512]{1,0:T(8,128)(2,1)} fusion(bf16[256,512]{1,0:T(8,128)(2,1)} %param.3, bf16[32,8,4,128]{3,2,1,0:T(4,128)(2,1)S(1)} %bitcast.9), kind=kLoop, calls=%fused_computation.29 | loop fusion | flops 131072 | bytes 786432 | tf_op jit(solution)/shard_map/mul | solution.py:103
  11.2 10.2 %collective-permute-start = (bf16[256,512]{1,0:T(8,128)(2,1)}, bf16[256,512]{1,0:T(8,128)(2,1)S(1)}, u32[]{:S(2)}, u32[]{:S(2)}) collective-permute-start(bf16[256,512]{1,0:T(8,128)(2,1)} %bitcast_multiply_fusion), channel_id=1, source_target_pairs={{0,0},{8,1},{2,2},{10,3},{4,4},{12,5},{6,6},{14,7},{1,8},{9,9},{3,... | collective-permute-start | bytes 786440 | tf_op jit(solution)/shard_map/ppermute | solution.py:78
  21.4 0.1 collective-permute-start.1
  21.4 4.3 %collective-permute-start.2 = (bf16[256,512]{1,0:T(8,128)(2,1)}, bf16[256,512]{1,0:T(8,128)(2,1)S(1)}, u32[]{:S(2)}, u32[]{:S(2)}) collective-permute-start(bf16[256,512]{1,0:T(8,128)(2,1)} %bitcast_multiply_fusion), channel_id=1, source_target_pairs={{4,0},{12,1},{6,2},{14,3},{0,4},{8,5},{2,6},{10,7},{5,8},{13,9},{7... | collective-permute-start | bytes 786440 | tf_op jit(solution)/shard_map/ppermute | solution.py:78
  25.7 0.4 collective-permute-start.3
  26.2 0.0 collective-permute-start.10
  26.2 9.4 %collective-permute-done.refs_0_ = bf16[256,512]{1,0:T(8,128)(2,1)S(1)} collective-permute-done((bf16[256,512]{1,0:T(8,128)(2,1)}, bf16[256,512]{1,0:T(8,128)(2,1)S(1)}, u32[]{:S(2)}, u32[]{:S(2)}) %collective-permute-start) | collective-permute-done | bytes 262176 | tf_op jit(solution)/shard_map/ppermute | solution.py:78
  35.6 7.0 %collective-permute-done.1.refs_1_ = bf16[256,512]{1,0:T(8,128)(2,1)S(1)} collective-permute-done((bf16[256,512]{1,0:T(8,128)(2,1)}, bf16[256,512]{1,0:T(8,128)(2,1)S(1)}, u32[]{:S(2)}, u32[]{:S(2)}) %collective-permute-start.1) | collective-permute-done | bytes 262176 | tf_op jit(solution)/shard_map/ppermute | solution.py:78
  42.6 1.8 %collective-permute-done.2.refs_2_ = bf16[256,512]{1,0:T(8,128)(2,1)S(1)} collective-permute-done((bf16[256,512]{1,0:T(8,128)(2,1)}, bf16[256,512]{1,0:T(8,128)(2,1)S(1)}, u32[]{:S(2)}, u32[]{:S(2)}) %collective-permute-start.2) | collective-permute-done | bytes 262176 | tf_op jit(solution)/shard_map/ppermute | solution.py:78
  44.4 4.4 %collective-permute-start.5 = (bf16[256,512]{1,0:T(8,128)(2,1)}, bf16[256,512]{1,0:T(8,128)(2,1)S(1)}, u32[]{:S(2)}, u32[]{:S(2)}) collective-permute-start(bf16[256,512]{1,0:T(8,128)(2,1)} %bitcast_multiply_fusion), channel_id=1, source_target_pairs={{0,0},{128,1},{16,16},{144,17},{32,32},{160,33},{48,48},{176,49},{... | collective-permute-start | bytes 786440 | tf_op jit(solution)/shard_map/ppermute | solution.py:110
  48.8 3.1 %collective-permute-start.6 = (bf16[256,512]{1,0:T(8,128)(2,1)}, bf16[256,512]{1,0:T(8,128)(2,1)S(1)}, u32[]{:S(2)}, u32[]{:S(2)}) collective-permute-start(bf16[256,512]{1,0:T(8,128)(2,1)} %bitcast_multiply_fusion), channel_id=1, source_target_pairs={{16,0},{144,1},{32,16},{160,17},{48,32},{176,33},{0,48},{128,49},{... | collective-permute-start | bytes 786440 | tf_op jit(solution)/shard_map/ppermute | solution.py:110
  51.9 2.7 %collective-permute-start.7 = (bf16[256,512]{1,0:T(8,128)(2,1)}, bf16[256,512]{1,0:T(8,128)(2,1)}, u32[]{:S(2)}, u32[]{:S(2)}) collective-permute-start(bf16[256,512]{1,0:T(8,128)(2,1)} %bitcast_multiply_fusion), channel_id=1, source_target_pairs={{32,0},{160,1},{48,16},{176,17},{0,32},{128,33},{16,48},{144,49},{... | collective-permute-start | bytes 786440 | tf_op jit(solution)/shard_map/ppermute | solution.py:110
  54.6 1.1 collective-permute-start.8
  55.7 1.8 %collective-permute-start.9 = (bf16[256,512]{1,0:T(8,128)(2,1)}, bf16[256,512]{1,0:T(8,128)(2,1)}, u32[]{:S(2)}, u32[]{:S(2)}) collective-permute-start(bf16[256,512]{1,0:T(8,128)(2,1)} %bitcast_multiply_fusion), channel_id=1, source_target_pairs={{64,0},{192,1},{80,16},{208,17},{96,32},{224,33},{112,48},{240,49}... | collective-permute-start | bytes 786440 | tf_op jit(solution)/shard_map/ppermute | solution.py:110
  57.5 0.1 pad_add_fusion.place
  57.5 6.9 %collective-permute-done.5.refs_4_ = bf16[256,512]{1,0:T(8,128)(2,1)S(1)} collective-permute-done((bf16[256,512]{1,0:T(8,128)(2,1)}, bf16[256,512]{1,0:T(8,128)(2,1)S(1)}, u32[]{:S(2)}, u32[]{:S(2)}) %collective-permute-start.5) | collective-permute-done | bytes 262176 | tf_op jit(solution)/shard_map/ppermute | solution.py:110
  64.4 0.3 collective-permute-done.7.refs_6_
  64.7 6.3 %collective-permute-done.8.refs_7_ = bf16[256,512]{1,0:T(8,128)(2,1)} collective-permute-done((bf16[256,512]{1,0:T(8,128)(2,1)}, bf16[256,512]{1,0:T(8,128)(2,1)}, u32[]{:S(2)}, u32[]{:S(2)}) %collective-permute-start.8) | collective-permute-done | bytes 262176 | tf_op jit(solution)/shard_map/ppermute | solution.py:110
  71.0 1.3 %collective-permute-done.9.refs_8_ = bf16[256,512]{1,0:T(8,128)(2,1)} collective-permute-done((bf16[256,512]{1,0:T(8,128)(2,1)}, bf16[256,512]{1,0:T(8,128)(2,1)}, u32[]{:S(2)}, u32[]{:S(2)}) %collective-permute-start.9) | collective-permute-done | bytes 262176 | tf_op jit(solution)/shard_map/ppermute | solution.py:110
  72.3 2.0 %shard_map.37 = f32[256,512]{1,0:T(8,128)S(1)} custom-call(s32[3]{0:T(128)S(1)} %pad_add_fusion.place, bf16[256,512]{1,0:T(8,128)(2,1)S(1)} %collective-permute-done.refs_0_, bf16[256,512]{1,0:T(8,128)(2,1)S(1)} %collective-permute-done.1.refs_1_, bf16[256,512]{1,0:T(8,128)(2,1)S(1)} %collective-permute-done.2.refs_2_, ...), custom_call_target="tpu_custom_call" | custom-call | flops 536870912 | bytes 4194304 | tf_op jit(solution)/shard_map/pallas_call | solution.py:61
  74.3 0.1 collective-permute-start.13
  74.4 0.1 pad_maximum_fusion
  74.6 0.6 collective-permute-start.4
  75.4 0.9 collective-permute-done.13
  76.3 0.1 add_convert_fusion
  76.4 8.3 %collective-permute-start.14 = (bf16[256,512]{1,0:T(8,128)(2,1)S(1)}, bf16[256,512]{1,0:T(8,128)(2,1)S(1)}, u32[]{:S(2)}, u32[]{:S(2)}) collective-permute-start(bf16[256,512]{1,0:T(8,128)(2,1)S(1)} %add_convert_fusion), channel_id=1, source_target_pairs={{0,0},{8,1},{2,2},{10,3},{4,4},{12,5},{6,6},{14,7},{1,8},{9,9},{3,... | collective-permute-start | bytes 786440 | tf_op jit(solution)/shard_map/ppermute | solution.py:78
  84.8 0.1 collective-permute-start.15
  84.9 3.1 %collective-permute-start.16 = (bf16[256,512]{1,0:T(8,128)(2,1)S(1)}, bf16[256,512]{1,0:T(8,128)(2,1)S(1)}, u32[]{:S(2)}, u32[]{:S(2)}) collective-permute-start(bf16[256,512]{1,0:T(8,128)(2,1)S(1)} %add_convert_fusion), channel_id=1, source_target_pairs={{4,0},{12,1},{6,2},{14,3},{0,4},{8,5},{2,6},{10,7},{5,8},{13,9},{7... | collective-permute-start | bytes 786440 | tf_op jit(solution)/shard_map/ppermute | solution.py:78
  88.0 1.6 %collective-permute-start.17 = (bf16[256,512]{1,0:T(8,128)(2,1)S(1)}, bf16[256,512]{1,0:T(8,128)(2,1)S(1)}, u32[]{:S(2)}, u32[]{:S(2)}) collective-permute-start(bf16[256,512]{1,0:T(8,128)(2,1)S(1)} %add_convert_fusion), channel_id=1, source_target_pairs={{6,0},{14,1},{0,2},{8,3},{2,4},{10,5},{4,6},{12,7},{7,8},{15,9},{1... | collective-permute-start | bytes 786440 | tf_op jit(solution)/shard_map/ppermute | solution.py:78
  89.6 0.1 constant_dynamic-slice_fusion.2
  89.7 13.1 %collective-permute-done.14 = bf16[256,512]{1,0:T(8,128)(2,1)S(1)} collective-permute-done((bf16[256,512]{1,0:T(8,128)(2,1)S(1)}, bf16[256,512]{1,0:T(8,128)(2,1)S(1)}, u32[]{:S(2)}, u32[]{:S(2)}) %collective-permute-start.14) | collective-permute-done | bytes 262176 | tf_op jit(solution)/shard_map/ppermute | solution.py:78
  102.8 1.6 %collective-permute-done.15 = bf16[256,512]{1,0:T(8,128)(2,1)S(1)} collective-permute-done((bf16[256,512]{1,0:T(8,128)(2,1)S(1)}, bf16[256,512]{1,0:T(8,128)(2,1)S(1)}, u32[]{:S(2)}, u32[]{:S(2)}) %collective-permute-start.15) | collective-permute-done | bytes 262176 | tf_op jit(solution)/shard_map/ppermute | solution.py:78
  104.4 0.8 collective-permute-done.16
  105.1 2.1 %collective-permute-done.17 = bf16[256,512]{1,0:T(8,128)(2,1)S(1)} collective-permute-done((bf16[256,512]{1,0:T(8,128)(2,1)S(1)}, bf16[256,512]{1,0:T(8,128)(2,1)S(1)}, u32[]{:S(2)}, u32[]{:S(2)}) %collective-permute-start.17) | collective-permute-done | bytes 262176 | tf_op jit(solution)/shard_map/ppermute | solution.py:78
  107.2 0.1 pad_maximum_fusion.1
  107.4 0.3 collective-permute-start.18
  107.9 0.1 constant_dynamic-slice_fusion
  108.0 1.6 %fusion.19 = bf16[256,2048]{1,0:T(8,128)(2,1)} fusion(s32[]{:T(128)S(6)} %select_n.39, bf16[256,2048]{1,0:T(8,128)(2,1)S(1)} %collective-permute-done.4), kind=kLoop, calls=%fused_computation.25 | loop fusion | flops 2097152 | bytes 2097156 | tf_op jit(solution)/shard_map/concatenate | solution.py:88
  109.7 0.6 collective-permute-done.18
  110.3 1.6 %fusion.18 = bf16[256,2048]{1,0:T(8,128)(2,1)} fusion(s32[]{:T(128)S(6)} %select_n.39, bf16[256,2048]{1,0:T(8,128)(2,1)S(1)} %collective-permute-done.18), kind=kLoop, calls=%fused_computation.24 | loop fusion | flops 2097152 | bytes 2097156 | tf_op jit(solution)/shard_map/concatenate | solution.py:88
  111.9 6.5 %fusion.14 = f32[256,1024]{1,0:T(8,128)S(1)} fusion(bf16[4096,1024]{1,0:T(8,128)(2,1)} %all-gather.2.cloned.1.call-done, bf16[256,2048]{1,0:T(8,128)(2,1)} %fusion.18, bf16[256,2048]{1,0:T(8,128)(2,1)S(1)} %constant_dynamic-slice_fusion, pred[]{:T(512)S(6)} %eq.9), kind=kOutput, calls=%fused_computation.20 | convolution fusion | flops 2157182976 | bytes 11534337 | tf_op jit(solution)/shard_map/dot_general | solution.py:117
  118.4 0.2 copy-done.2
  118.6 3.3 %fusion.17 = bf16[256,1024]{1,0:T(8,128)(2,1)} fusion(f32[256,1024]{1,0:T(8,128)S(1)} %fusion.14, bf16[4096,1024]{1,0:T(8,128)(2,1)S(1)} %copy-done.2, bf16[256,2048]{1,0:T(8,128)(2,1)S(1)} %copy-done.1, bf16[256,2048]{1,0:T(8,128)(2,1)S(1)} %constant_dynamic-slice_fusion.2, pred[]{:T(512)S(6)} %eq.9), kind=kOutput, calls=%fused_computation.23 | convolution fusion | flops 2157707264 | bytes 12058625 | tf_op jit(solution)/shard_map/dot_general | solution.py:116
  (30 shorter events, 0.4 us)
Async XLA Ops:
  6.5 1.2 copy-start
  6.5 105.3 %all-gather.2.cloned.1.call-start = ((), (), s32[]{:S(2)}) async-start(), calls=%async_computation | async-start | bytes 8912896 | tf_op jit(solution)/shard_map/all_gather | solution.py:107
  11.2 24.4 %collective-permute-start = (bf16[256,512]{1,0:T(8,128)(2,1)}, bf16[256,512]{1,0:T(8,128)(2,1)S(1)}, u32[]{:S(2)}, u32[]{:S(2)}) collective-permute-start(bf16[256,512]{1,0:T(8,128)(2,1)} %bitcast_multiply_fusion), channel_id=1, source_target_pairs={{0,0},{8,1},{2,2},{10,3},{4,4},{12,5},{6,6},{14,7},{1,8},{9,9},{3,... | collective-permute-start | bytes 786440 | tf_op jit(solution)/shard_map/ppermute | solution.py:78
  21.4 21.3 %collective-permute-start.1 = (bf16[256,512]{1,0:T(8,128)(2,1)}, bf16[256,512]{1,0:T(8,128)(2,1)S(1)}, u32[]{:S(2)}, u32[]{:S(2)}) collective-permute-start(bf16[256,512]{1,0:T(8,128)(2,1)} %bitcast_multiply_fusion), channel_id=1, source_target_pairs={{2,0},{10,1},{4,2},{12,3},{6,4},{14,5},{0,6},{8,7},{3,8},{11,9},{5... | collective-permute-start | bytes 786440 | tf_op jit(solution)/shard_map/ppermute | solution.py:78
  21.4 23.0 %collective-permute-start.2 = (bf16[256,512]{1,0:T(8,128)(2,1)}, bf16[256,512]{1,0:T(8,128)(2,1)S(1)}, u32[]{:S(2)}, u32[]{:S(2)}) collective-permute-start(bf16[256,512]{1,0:T(8,128)(2,1)} %bitcast_multiply_fusion), channel_id=1, source_target_pairs={{4,0},{12,1},{6,2},{14,3},{0,4},{8,5},{2,6},{10,7},{5,8},{13,9},{7... | collective-permute-start | bytes 786440 | tf_op jit(solution)/shard_map/ppermute | solution.py:78
  25.7 23.1 %collective-permute-start.3 = (bf16[256,512]{1,0:T(8,128)(2,1)}, bf16[256,512]{1,0:T(8,128)(2,1)S(1)}, u32[]{:S(2)}, u32[]{:S(2)}) collective-permute-start(bf16[256,512]{1,0:T(8,128)(2,1)} %bitcast_multiply_fusion), channel_id=1, source_target_pairs={{6,0},{14,1},{0,2},{8,3},{2,4},{10,5},{4,6},{12,7},{7,8},{15,9},{1... | collective-permute-start | bytes 786440 | tf_op jit(solution)/shard_map/ppermute | solution.py:78
  26.2 25.7 %collective-permute-start.10 = (bf16[256,512]{1,0:T(8,128)(2,1)}, bf16[256,512]{1,0:T(8,128)(2,1)S(1)}, u32[]{:S(2)}, u32[]{:S(2)}) collective-permute-start(bf16[256,512]{1,0:T(8,128)(2,1)} %bitcast_multiply_fusion), channel_id=1, source_target_pairs={{80,0},{208,1},{96,16},{224,17},{112,32},{240,33},{64,48},{192,49}... | collective-permute-start | bytes 786440 | tf_op jit(solution)/shard_map/ppermute | solution.py:110
  35.6 19.0 %collective-permute-start.11 = (bf16[256,512]{1,0:T(8,128)(2,1)}, bf16[256,512]{1,0:T(8,128)(2,1)S(1)}, u32[]{:S(2)}, u32[]{:S(2)}) collective-permute-start(bf16[256,512]{1,0:T(8,128)(2,1)} %bitcast_multiply_fusion), channel_id=1, source_target_pairs={{96,0},{224,1},{112,16},{240,17},{64,32},{192,33},{80,48},{208,49}... | collective-permute-start | bytes 786440 | tf_op jit(solution)/shard_map/ppermute | solution.py:110
  42.6 13.1 %collective-permute-start.12 = (bf16[256,512]{1,0:T(8,128)(2,1)}, bf16[256,512]{1,0:T(8,128)(2,1)S(1)}, u32[]{:S(2)}, u32[]{:S(2)}) collective-permute-start(bf16[256,512]{1,0:T(8,128)(2,1)} %bitcast_multiply_fusion), channel_id=1, source_target_pairs={{112,0},{240,1},{64,16},{192,17},{80,32},{208,33},{96,48},{224,49}... | collective-permute-start | bytes 786440 | tf_op jit(solution)/shard_map/ppermute | solution.py:110
  44.4 20.0 %collective-permute-start.5 = (bf16[256,512]{1,0:T(8,128)(2,1)}, bf16[256,512]{1,0:T(8,128)(2,1)S(1)}, u32[]{:S(2)}, u32[]{:S(2)}) collective-permute-start(bf16[256,512]{1,0:T(8,128)(2,1)} %bitcast_multiply_fusion), channel_id=1, source_target_pairs={{0,0},{128,1},{16,16},{144,17},{32,32},{160,33},{48,48},{176,49},{... | collective-permute-start | bytes 786440 | tf_op jit(solution)/shard_map/ppermute | solution.py:110
  48.8 15.6 %collective-permute-start.6 = (bf16[256,512]{1,0:T(8,128)(2,1)}, bf16[256,512]{1,0:T(8,128)(2,1)S(1)}, u32[]{:S(2)}, u32[]{:S(2)}) collective-permute-start(bf16[256,512]{1,0:T(8,128)(2,1)} %bitcast_multiply_fusion), channel_id=1, source_target_pairs={{16,0},{144,1},{32,16},{160,17},{48,32},{176,33},{0,48},{128,49},{... | collective-permute-start | bytes 786440 | tf_op jit(solution)/shard_map/ppermute | solution.py:110
  51.9 12.8 %collective-permute-start.7 = (bf16[256,512]{1,0:T(8,128)(2,1)}, bf16[256,512]{1,0:T(8,128)(2,1)}, u32[]{:S(2)}, u32[]{:S(2)}) collective-permute-start(bf16[256,512]{1,0:T(8,128)(2,1)} %bitcast_multiply_fusion), channel_id=1, source_target_pairs={{32,0},{160,1},{48,16},{176,17},{0,32},{128,33},{16,48},{144,49},{... | collective-permute-start | bytes 786440 | tf_op jit(solution)/shard_map/ppermute | solution.py:110
  54.6 16.4 %collective-permute-start.8 = (bf16[256,512]{1,0:T(8,128)(2,1)}, bf16[256,512]{1,0:T(8,128)(2,1)}, u32[]{:S(2)}, u32[]{:S(2)}) collective-permute-start(bf16[256,512]{1,0:T(8,128)(2,1)} %bitcast_multiply_fusion), channel_id=1, source_target_pairs={{48,0},{176,1},{0,16},{128,17},{16,32},{144,33},{32,48},{160,49},{... | collective-permute-start | bytes 786440 | tf_op jit(solution)/shard_map/ppermute | solution.py:110
  55.7 16.6 %collective-permute-start.9 = (bf16[256,512]{1,0:T(8,128)(2,1)}, bf16[256,512]{1,0:T(8,128)(2,1)}, u32[]{:S(2)}, u32[]{:S(2)}) collective-permute-start(bf16[256,512]{1,0:T(8,128)(2,1)} %bitcast_multiply_fusion), channel_id=1, source_target_pairs={{64,0},{192,1},{80,16},{208,17},{96,32},{224,33},{112,48},{240,49}... | collective-permute-start | bytes 786440 | tf_op jit(solution)/shard_map/ppermute | solution.py:110
  74.3 2.0 %collective-permute-start.13 = (f32[256,512]{1,0:T(8,128)S(1)}, f32[256,512]{1,0:T(8,128)S(1)}, u32[]{:S(2)}, u32[]{:S(2)}) collective-permute-start(f32[256,512]{1,0:T(8,128)S(1)} %shard_map.37), channel_id=1, source_target_pairs={{0,1},{1,0},{2,3},{3,2},{4,5},{5,4},{6,7},{7,6},{8,9},{9,8},{10,11... | collective-permute-start | bytes 1572872 | tf_op jit(solution)/shard_map/ppermute | solution.py:113
  74.6 33.5 %collective-permute-start.4 = (bf16[256,2048]{1,0:T(8,128)(2,1)S(1)}, bf16[256,2048]{1,0:T(8,128)(2,1)S(1)}, u32[]{:S(2)}, u32[]{:S(2)}) collective-permute-start(bf16[256,2048]{1,0:T(8,128)(2,1)S(1)} %pad_maximum_fusion), channel_id=1, source_target_pairs={{0,1},{1,0},{2,3},{3,2},{4,5},{5,4},{6,7},{7,6},{8,9},{9,8},{10,11... | collective-permute-start | bytes 3145736 | tf_op jit(solution)/shard_map/ppermute | solution.py:82
  76.4 26.4 %collective-permute-start.14 = (bf16[256,512]{1,0:T(8,128)(2,1)S(1)}, bf16[256,512]{1,0:T(8,128)(2,1)S(1)}, u32[]{:S(2)}, u32[]{:S(2)}) collective-permute-start(bf16[256,512]{1,0:T(8,128)(2,1)S(1)} %add_convert_fusion), channel_id=1, source_target_pairs={{0,0},{8,1},{2,2},{10,3},{4,4},{12,5},{6,6},{14,7},{1,8},{9,9},{3,... | collective-permute-start | bytes 786440 | tf_op jit(solution)/shard_map/ppermute | solution.py:78
  84.8 19.6 %collective-permute-start.15 = (bf16[256,512]{1,0:T(8,128)(2,1)S(1)}, bf16[256,512]{1,0:T(8,128)(2,1)S(1)}, u32[]{:S(2)}, u32[]{:S(2)}) collective-permute-start(bf16[256,512]{1,0:T(8,128)(2,1)S(1)} %add_convert_fusion), channel_id=1, source_target_pairs={{2,0},{10,1},{4,2},{12,3},{6,4},{14,5},{0,6},{8,7},{3,8},{11,9},{5... | collective-permute-start | bytes 786440 | tf_op jit(solution)/shard_map/ppermute | solution.py:78
  84.9 20.3 %collective-permute-start.16 = (bf16[256,512]{1,0:T(8,128)(2,1)S(1)}, bf16[256,512]{1,0:T(8,128)(2,1)S(1)}, u32[]{:S(2)}, u32[]{:S(2)}) collective-permute-start(bf16[256,512]{1,0:T(8,128)(2,1)S(1)} %add_convert_fusion), channel_id=1, source_target_pairs={{4,0},{12,1},{6,2},{14,3},{0,4},{8,5},{2,6},{10,7},{5,8},{13,9},{7... | collective-permute-start | bytes 786440 | tf_op jit(solution)/shard_map/ppermute | solution.py:78
  88.0 19.3 %collective-permute-start.17 = (bf16[256,512]{1,0:T(8,128)(2,1)S(1)}, bf16[256,512]{1,0:T(8,128)(2,1)S(1)}, u32[]{:S(2)}, u32[]{:S(2)}) collective-permute-start(bf16[256,512]{1,0:T(8,128)(2,1)S(1)} %add_convert_fusion), channel_id=1, source_target_pairs={{6,0},{14,1},{0,2},{8,3},{2,4},{10,5},{4,6},{12,7},{7,8},{15,9},{1... | collective-permute-start | bytes 786440 | tf_op jit(solution)/shard_map/ppermute | solution.py:78
  107.4 2.9 %collective-permute-start.18 = (bf16[256,2048]{1,0:T(8,128)(2,1)S(1)}, bf16[256,2048]{1,0:T(8,128)(2,1)S(1)}, u32[]{:S(2)}, u32[]{:S(2)}) collective-permute-start(bf16[256,2048]{1,0:T(8,128)(2,1)S(1)} %pad_maximum_fusion.1), channel_id=1, source_target_pairs={{0,1},{1,0},{2,3},{3,2},{4,5},{5,4},{6,7},{7,6},{8,9},{9,8},{10,11... | collective-permute-start | bytes 3145736 | tf_op jit(solution)/shard_map/ppermute | solution.py:82
  111.9 6.5 %copy-start.1 = (bf16[256,2048]{1,0:T(8,128)(2,1)S(1)}, bf16[256,2048]{1,0:T(8,128)(2,1)}, u32[]{:S(2)}) copy-start(bf16[256,2048]{1,0:T(8,128)(2,1)} %fusion.19) | copy-start | bytes 3145732
  111.9 6.7 %copy-start.2 = (bf16[4096,1024]{1,0:T(8,128)(2,1)S(1)}, bf16[4096,1024]{1,0:T(8,128)(2,1)}, u32[]{:S(2)}) copy-start(bf16[4096,1024]{1,0:T(8,128)(2,1)} %all-gather.2.cloned.1.call-done) | copy-start | bytes 25165828
Sparse Core Ops, SparseCore 0:
  9.8 92.7 all-gather.1

commit v2 on v0

v2 whole, which is shorter than its diff:
```python
import functools

import jax
import jax.numpy as jnp
from jax import lax
from jax.experimental import pallas as pl
from jax.experimental.pallas import tpu as pltpu
from jax.sharding import Mesh, PartitionSpec as P

BS = 128
NY, NX, NZ, NC = 4, 4, 8, 2
ROWS, INNER, WIDTH = 256, 512, 1024
PART = INNER // NC
DEPTH = NY * NX * ROWS
AXES = ("y", "x", "z", "c")
BF16, F32 = jnp.bfloat16, jnp.float32


def moved(block, source_of):
    def index(y, x, z, c):
        return ((y * NX + x) * NZ + z) * NC + c

    route = []
    for y in range(NY):
        for x in range(NX):
            for z in range(NZ):
                for c in range(NC):
                    source = source_of(y, x, z, c)
                    if source is not None:
                        route.append((index(*source), index(y, x, z, c)))
    return lax.ppermute(block, AXES, route)


def first(block, step):
    return moved(
        block,
        lambda y, x, z, c: ((y + step) % NY, x, z, c) if c == 0 else (y, (x + step) % NX, z, c),
    )


def second(block, step):
    return moved(
        block,
        lambda y, x, z, c: (y, (x + step) % NX, z, c) if c == 0 else ((y + step) % NY, x, z, c),
    )


def swapped(block):
    return moved(block, lambda y, x, z, c: (y, x, z, 1 - c))


def along(block, step):
    return moved(block, lambda y, x, z, c: (y, x, (z + (step if c == 0 else -step)) % NZ, c))


def joined(blocks):
    return jnp.stack(blocks)


def after(value, *others):
    return lax.optimization_barrier((value, others))[0]


def farther(two_on):
    four = moved(two_on, lambda y, x, z, c: (y, x, (z + 2) % NZ, c) if c == 0 else None)
    return along(two_on, 1), four


def positions():
    y, x, z, c = (lax.axis_index(name) for name in AXES)

    def place(offset, half):
        block = 2 * ((z + offset + NZ) % NZ) + half
        down, right = (block // NX - y + NY) % NY, (block % NX - x + NX) % NX
        d = jnp.where(c == 0, down, right)
        e = jnp.where(c == 0, right, down)
        return pl.multiple_of((e * NY + d) * ROWS, ROWS)

    return c, place


def reorder(own_ref, mine_ref, other_ref, out_ref, halves):
    c, place = positions()
    way = 1 - 2 * c
    for h in range(2):
        out_ref[:, pl.ds(place(0, halves(c, h)), ROWS)] = own_ref(h)
        for k in range(3):
            out_ref[:, pl.ds(place(way * (k + 1), halves(c, h)), ROWS)] = mine_ref(k, h)
            out_ref[:, pl.ds(place(-way * (k + 1), halves(1 - c, h)), ROWS)] = other_ref(k, h)
        far = place(4, halves(0, h))

        @pl.when(c == 0)
        def _():
            out_ref[:, pl.ds(far, ROWS)] = mine_ref(3, h)

        @pl.when(c == 1)
        def _():
            out_ref[:, pl.ds(far, ROWS)] = other_ref(3, h)


def contract(row_ref, places, stacks):
    total = None
    for (e, d), ref in zip(places, stacks):
        count = ref.shape[0] * ROWS
        at = (e * NY + d) * ROWS
        panel = ref[...].reshape(count, ref.shape[2])
        term = jnp.dot(row_ref[:, at : at + count], panel, preferred_element_type=F32)
        total = term if total is None else total + term
    return total


def square_kernel(places, own, mine, other, *refs):
    stacks, (row_ref, out_ref) = refs[: len(places)], refs[len(places) :]

    def half(h):
        return slice(h * ROWS, (h + 1) * ROWS)

    reorder(
        lambda h: own[:, half(h)],
        lambda k, h: mine[k, :, half(h)],
        lambda k, h: other[k, :, half(h)],
        row_ref,
        lambda core, h: h,
    )
    out_ref[...] = contract(row_ref, places, stacks).astype(BF16)


def single_kernel(places, row_ref, *refs):
    stacks, (out_ref,) = refs[: len(places)], refs[len(places) :]
    out_ref[...] = contract(row_ref, places, stacks)


def final_kernel(places, own, mine, other, one, *refs):
    stacks, (out_ref, row_ref) = refs[: len(places)], refs[len(places) :]
    reorder(
        lambda h: own[h],
        lambda k, h: mine[k, h],
        lambda k, h: other[k, h],
        row_ref,
        lambda core, h: core if h == 0 else 1 - core,
    )
    two = contract(row_ref, places, stacks)
    out_ref[...] = (3.0 * one[...] - 2.0 * two).astype(BF16)


def call(kernel, out_shape, scratch, flops, *operands):
    vmem = pl.BlockSpec(memory_space=pltpu.VMEM)
    return pl.pallas_call(
        kernel,
        out_shape=out_shape,
        in_specs=[vmem] * len(operands),
        out_specs=jax.tree.map(lambda _: vmem, out_shape),
        scratch_shapes=scratch,
        compiler_params=pltpu.CompilerParams(vmem_limit_bytes=16 * 1024 * 1024),
        cost_estimate=pl.CostEstimate(flops=flops, bytes_accessed=1 << 20, transcendentals=0),
    )(*operands)


def shards(density, panel, pattern):
    core = lax.axis_index("c")
    mask = pattern.astype(BF16)
    filtered = (
        density.reshape(ROWS // BS, BS, INNER // BS, BS) * mask[:, None, :, None]
    ).reshape(ROWS, INNER)
    own_columns = lax.dynamic_slice_in_dim(filtered, core * PART, PART, 1)
    own_panel = lax.dynamic_slice_in_dim(panel, core * WIDTH, WIDTH, 1)

    both = jnp.concatenate([own_columns, own_panel], 1)
    near = [both] + [first(both, d) for d in (1, 2, 3)]
    one_on, two_on = along(filtered, 1), along(filtered, 2)
    near_columns = joined([block[:, :PART] for block in near])
    near_panel = joined([block[:, PART:] for block in near])

    near_columns = after(near_columns, one_on, two_on)
    two_tied = after(two_on, *near[1:])
    columns = [near_columns] + [second(near_columns, e) for e in (1, 2, 3)]
    filtered_mine = joined([one_on, two_on, *farther(two_tied)])
    filtered_mine = after(filtered_mine, *columns[1:])
    filtered_line = (filtered, filtered_mine, swapped(filtered_mine))

    near_panel = after(near_panel, *columns[1:])
    plus, minus = second(near_panel, 1), second(near_panel, 3)
    row, squared = call(
        functools.partial(square_kernel, [(e, 0) for e in range(NX)]),
        (jax.ShapeDtypeStruct((ROWS, DEPTH), BF16), jax.ShapeDtypeStruct((ROWS, PART), BF16)),
        [],
        2 * ROWS * DEPTH * PART,
        *filtered_line,
        *columns,
    )
    squared = joined([squared, swapped(squared)])
    one_on, two_on = along(squared, 1), along(squared, 2)
    squared_mine = joined([one_on, two_on, *farther(two_on)])
    squared_mine = after(squared_mine, plus, minus)
    squared_line = (squared, squared_mine, swapped(squared_mine))
    parts = [
        (0, 0, near_panel),
        (1, 0, plus),
        (3, 0, minus),
        (2, 0, second(plus[:2], 1)),
        (2, 2, second(minus[2:], 3)),
    ]
    places, stacks = [(e, d) for e, d, _ in parts], [blocks for _, _, blocks in parts]
    one = call(
        functools.partial(single_kernel, places),
        jax.ShapeDtypeStruct((ROWS, WIDTH), F32),
        [],
        2 * ROWS * DEPTH * WIDTH,
        row,
        *stacks,
    )
    return call(
        functools.partial(final_kernel, places),
        jax.ShapeDtypeStruct((ROWS, WIDTH), BF16),
        [pltpu.VMEM((ROWS, DEPTH), BF16)],
        2 * ROWS * DEPTH * WIDTH,
        *squared_line,
        one,
        *stacks,
    )


def solution(mesh):
    fine = Mesh(mesh.devices.reshape(NY, NX, NZ, NC), AXES)
    rows = ("y", "x")
    return jax.shard_map(
        shards,
        mesh=fine,
        in_specs=(P(rows, "z"), P(rows, "z"), P(rows, "z")),
        out_specs=P(rows, ("z", "c")),
        check_vma=False,
    )
```

time: 610 us -> 98.8 us (0.16)
  the two profiles are of different devices: /device:TPU:1 before, /device:TPU:14 now
where the time goes in v2:
time: 98.8 us; the launch traced here: 98.6 us
  waiting for transfers between devices  53.2 us (54%)
  starting transfers between devices  35.4 us (36%)
  Pallas kernels  6.82 us (7%)
  other arithmetic  2.44 us (2%)
    ppermute x21, waiting for transfers between devices, moved(): return lax.ppermute(block, AXES, route)  53.2 us
    ppermute x21, starting transfers between devices, moved(): return lax.ppermute(block, AXES, route)  35.4 us
    pallas_call x3, Pallas kernels, call(): pl.pallas_call(kernel, out_shape=out_shape, in_specs=[vmem] * len(operand...  6.82 us
  transfers between devices with their start and end apart: 21, of which 13 were waited for; matrix products, arithmetic and copies ran while one was open for 1% of the time, Pallas kernels for 3%

profile of v2, /device:TPU:14, one launch (start us, length us, event | category | flops | bytes accessed | tf_op | source)
XLA Modules:
  0.0 98.6 jit_solution(14620698928583749384)
XLA Ops:
  0.0 0.8 convert_element_type.3
  0.8 0.1 mul.17
  0.9 1.0 %bitcast_multiply_fusion.own = bf16[256,512]{1,0:T(8,128)(2,1)S(1)} fusion(bf16[256,512]{1,0:T(8,128)(2,1)} %param.3, bf16[32,8,4,128]{3,2,1,0:T(4,128)(2,1)S(1)} %bitcast.31), kind=kLoop, calls=%fused_computation.8 | loop fusion | flops 131072 | bytes 786432 | tf_op jit(solution)/shard_map/mul | solution.py:163
  2.1 1.7 %collective-permute-start.4 = (bf16[256,1280]{1,0:T(8,128)(2,1)S(1)}, bf16[256,1280]{1,0:T(8,128)(2,1)S(1)}, u32[]{:S(2)}, u32[]{:S(2)}) collective-permute-start(bf16[256,1280]{1,0:T(8,128)(2,1)S(1)} %pad_maximum_fusion.3), channel_id=1, source_target_pairs={{192,0},{49,1},{194,2},{51,3},{196,4},{53,5},{198,6},{55,7},{200,8... | collective-permute-start | bytes 1966088 | tf_op jit(solution)/shard_map/ppermute | solution.py:31
  3.7 0.9 collective-permute-start.3
  4.7 2.4 %collective-permute-start.2 = (bf16[256,1280]{1,0:T(8,128)(2,1)S(1)}, bf16[256,1280]{1,0:T(8,128)(2,1)S(1)}, u32[]{:S(2)}, u32[]{:S(2)}) collective-permute-start(bf16[256,1280]{1,0:T(8,128)(2,1)S(1)} %pad_maximum_fusion.3), channel_id=1, source_target_pairs={{64,0},{17,1},{66,2},{19,3},{68,4},{21,5},{70,6},{23,7},{72,8},{25... | collective-permute-start | bytes 1966088 | tf_op jit(solution)/shard_map/ppermute | solution.py:31
  7.1 6.3 %collective-permute-start.1 = (bf16[256,512]{1,0:T(8,128)(2,1)S(1)}, bf16[256,512]{1,0:T(8,128)(2,1)S(1)}, u32[]{:S(2)}, u32[]{:S(2)}) collective-permute-start(bf16[256,512]{1,0:T(8,128)(2,1)S(1)} %bitcast_multiply_fusion.own), channel_id=1, source_target_pairs={{4,0},{13,1},{6,2},{15,3},{8,4},{1,5},{10,6},{3,7},{12,8},{5,9},{1... | collective-permute-start | bytes 786440 | tf_op jit(solution)/shard_map/ppermute | solution.py:31
  13.4 1.0 %collective-permute-start = (bf16[256,512]{1,0:T(8,128)(2,1)S(1)}, bf16[256,512]{1,0:T(8,128)(2,1)S(1)}, u32[]{:S(2)}, u32[]{:S(2)}) collective-permute-start(bf16[256,512]{1,0:T(8,128)(2,1)S(1)} %bitcast_multiply_fusion.own), channel_id=1, source_target_pairs={{2,0},{15,1},{4,2},{1,3},{6,4},{3,5},{8,6},{5,7},{10,8},{7,9},{12,... | collective-permute-start | bytes 786440 | tf_op jit(solution)/shard_map/ppermute | solution.py:31
  14.4 5.7 %collective-permute-done.1 = bf16[256,512]{1,0:T(8,128)(2,1)S(1)} collective-permute-done((bf16[256,512]{1,0:T(8,128)(2,1)S(1)}, bf16[256,512]{1,0:T(8,128)(2,1)S(1)}, u32[]{:S(2)}, u32[]{:S(2)}) %collective-permute-start.1) | collective-permute-done | bytes 262176 | tf_op jit(solution)/shard_map/ppermute | solution.py:31
  20.1 2.2 %collective-permute-done.2 = bf16[256,1280]{1,0:T(8,128)(2,1)S(1)} collective-permute-done((bf16[256,1280]{1,0:T(8,128)(2,1)S(1)}, bf16[256,1280]{1,0:T(8,128)(2,1)S(1)}, u32[]{:S(2)}, u32[]{:S(2)}) %collective-permute-start.2) | collective-permute-done | bytes 655392 | tf_op jit(solution)/shard_map/ppermute | solution.py:31
  22.3 8.2 %collective-permute-start.6 = (bf16[256,512]{1,0:T(8,128)(2,1)S(1)}, bf16[256,512]{1,0:T(8,128)(2,1)S(1)}, u32[]{:S(2)}, u32[]{:S(2)}) collective-permute-start(bf16[256,512]{1,0:T(8,128)(2,1)S(1)} %collective-permute-done.1), channel_id=1, source_target_pairs={{4,0},{6,2},{8,4},{10,6},{12,8},{14,10},{0,12},{2,14},{20,16},{22,... | collective-permute-start | bytes 786440 | tf_op jit(solution)/shard_map/ppermute | solution.py:31
  30.5 1.1 %collective-permute-start.5 = (bf16[256,512]{1,0:T(8,128)(2,1)S(1)}, bf16[256,512]{1,0:T(8,128)(2,1)S(1)}, u32[]{:S(2)}, u32[]{:S(2)}) collective-permute-start(bf16[256,512]{1,0:T(8,128)(2,1)S(1)} %collective-permute-done.1), channel_id=1, source_target_pairs={{2,0},{15,1},{4,2},{1,3},{6,4},{3,5},{8,6},{5,7},{10,8},{7,9},{12,... | collective-permute-start | bytes 786440 | tf_op jit(solution)/shard_map/ppermute | solution.py:31
  31.6 0.1 pad_maximum_fusion.4.refs_0_
  31.7 0.6 collective-permute-start.9
  32.3 2.4 %collective-permute-start.8 = (bf16[4,256,256]{2,1,0:T(8,128)(2,1)S(1)}, bf16[4,256,256]{2,1,0:T(8,128)(2,1)S(1)}, u32[]{:S(2)}, u32[]{:S(2)}) collective-permute-start(bf16[4,256,256]{2,1,0:T(8,128)(2,1)S(1)} %pad_maximum_fusion.4.refs_0_), channel_id=1, source_target_pairs={{32,0},{129,1},{34,2},{131,3},{36,4},{133,5},{38,6},{135,7},{40,8}... | collective-permute-start | bytes 1572872 | tf_op jit(solution)/shard_map/ppermute | solution.py:31
  34.7 0.1 slice_bitcast_fusion
  34.7 0.1 slice_bitcast_fusion.1
  34.8 0.1 slice_bitcast_fusion.2
  34.9 0.3 pad_maximum_fusion.refs_0_
  35.1 5.8 %collective-permute-done.9.refs_3_ = bf16[4,256,256]{2,1,0:T(8,128)(2,1)S(1)} collective-permute-done((bf16[4,256,256]{2,1,0:T(8,128)(2,1)S(1)}, bf16[4,256,256]{2,1,0:T(8,128)(2,1)S(1)}, u32[]{:S(2)}, u32[]{:S(2)}) %collective-permute-start.9) | collective-permute-done | bytes 524320 | tf_op jit(solution)/shard_map/ppermute | solution.py:31
  41.0 2.1 %collective-permute-done.8.refs_2_ = bf16[4,256,256]{2,1,0:T(8,128)(2,1)S(1)} collective-permute-done((bf16[4,256,256]{2,1,0:T(8,128)(2,1)S(1)}, bf16[4,256,256]{2,1,0:T(8,128)(2,1)S(1)}, u32[]{:S(2)}, u32[]{:S(2)}) %collective-permute-start.8) | collective-permute-done | bytes 524320 | tf_op jit(solution)/shard_map/ppermute | solution.py:31
  43.0 5.5 %collective-permute-done.7.refs_1_ = bf16[4,256,256]{2,1,0:T(8,128)(2,1)S(1)} collective-permute-done((bf16[4,256,256]{2,1,0:T(8,128)(2,1)S(1)}, bf16[4,256,256]{2,1,0:T(8,128)(2,1)S(1)}, u32[]{:S(2)}, u32[]{:S(2)}) %collective-permute-start.7) | collective-permute-done | bytes 524320 | tf_op jit(solution)/shard_map/ppermute | solution.py:31
  48.6 0.7 collective-permute-start.17
  49.3 1.3 %collective-permute-start.16 = (bf16[4,256,1024]{2,1,0:T(8,128)(2,1)S(1)}, bf16[4,256,1024]{2,1,0:T(8,128)(2,1)S(1)}, u32[]{:S(2)}, u32[]{:S(2)}) collective-permute-start(bf16[4,256,1024]{2,1,0:T(8,128)(2,1)S(1)} %pad_maximum_fusion.refs_0_), channel_id=1, source_target_pairs={{16,0},{65,1},{18,2},{67,3},{20,4},{69,5},{22,6},{71,7},{24,8},{73... | collective-permute-start | bytes 6291464 | tf_op jit(solution)/shard_map/ppermute | solution.py:31
  50.6 0.1 pad_maximum_fusion.1.mine
  50.7 0.1 collective-permute-start.10
  50.8 2.6 %collective-permute-done.10.other = bf16[4,256,512]{2,1,0:T(8,128)(2,1)S(1)} collective-permute-done((bf16[4,256,512]{2,1,0:T(8,128)(2,1)S(1)}, bf16[4,256,512]{2,1,0:T(8,128)(2,1)S(1)}, u32[]{:S(2)}, u32[]{:S(2)}) %collective-permute-start.10) | collective-permute-done | bytes 1048608 | tf_op jit(solution)/shard_map/ppermute | solution.py:31
  53.5 1.0 %shard_map.37 = (bf16[256,4096]{1,0:T(8,128)(2,1)S(1)}, bf16[256,256]{1,0:T(8,128)(2,1)S(1)}) custom-call(bf16[256,512]{1,0:T(8,128)(2,1)S(1)} %bitcast_multiply_fusion.own, bf16[4,256,512]{2,1,0:T(8,128)(2,1)S(1)} %pad_maximum_fusion.1.mine, bf16[4,256,512]{2,1,0:T(8,128)(2,1)S(1)} %collective-permute-done.10.other, ...), custom_call_target="tpu_custom_call" | custom-call | flops 536870912 | bytes 1048576 | tf_op jit(solution)/shard_map/pallas_call | solution.py:148
  54.5 0.2 collective-permute-start.11
  54.7 1.2 %collective-permute-done.11 = bf16[256,256]{1,0:T(8,128)(2,1)S(1)} collective-permute-done((bf16[256,256]{1,0:T(8,128)(2,1)S(1)}, bf16[256,256]{1,0:T(8,128)(2,1)S(1)}, u32[]{:S(2)}, u32[]{:S(2)}) %collective-permute-start.11) | collective-permute-done | bytes 131104 | tf_op jit(solution)/shard_map/ppermute | solution.py:31
  56.0 0.6 collective-permute-start.13
  56.6 0.7 collective-permute-start.12
  57.3 8.3 %collective-permute-done.13 = bf16[2,256,256]{2,1,0:T(8,128)(2,1)S(1)} collective-permute-done((bf16[2,256,256]{2,1,0:T(8,128)(2,1)S(1)}, bf16[2,256,256]{2,1,0:T(8,128)(2,1)S(1)}, u32[]{:S(2)}, u32[]{:S(2)}) %collective-permute-start.13) | collective-permute-done | bytes 262176 | tf_op jit(solution)/shard_map/ppermute | solution.py:31
  65.6 4.2 %collective-permute-start.15 = (bf16[2,256,256]{2,1,0:T(8,128)(2,1)S(1)}, bf16[2,256,256]{2,1,0:T(8,128)(2,1)S(1)}, u32[]{:S(2)}, u32[]{:S(2)}) collective-permute-start(bf16[2,256,256]{2,1,0:T(8,128)(2,1)S(1)} %collective-permute-done.13), channel_id=1, source_target_pairs={{4,0},{6,2},{8,4},{10,6},{12,8},{14,10},{0,12},{2,14},{20,16},{22,... | collective-permute-start | bytes 786440 | tf_op jit(solution)/shard_map/ppermute | solution.py:31
  69.8 0.7 collective-permute-start.14
  70.4 4.1 %collective-permute-done.17.refs_2_ = bf16[4,256,1024]{2,1,0:T(8,128)(2,1)S(1)} collective-permute-done((bf16[4,256,1024]{2,1,0:T(8,128)(2,1)S(1)}, bf16[4,256,1024]{2,1,0:T(8,128)(2,1)S(1)}, u32[]{:S(2)}, u32[]{:S(2)}) %collective-permute-start.17) | collective-permute-done | bytes 2097184 | tf_op jit(solution)/shard_map/ppermute | solution.py:31
  74.6 0.1 slice.39
  74.7 2.0 %collective-permute-start.20 = (bf16[2,256,1024]{2,1,0:T(8,128)(2,1)S(1)}, bf16[2,256,1024]{2,1,0:T(8,128)(2,1)S(1)}, u32[]{:S(2)}, u32[]{:S(2)}) collective-permute-start(bf16[2,256,1024]{2,1,0:T(8,128)(2,1)S(1)} %slice.39), channel_id=1, source_target_pairs={{48,0},{193,1},{50,2},{195,3},{52,4},{197,5},{54,6},{199,7},{56,8}... | collective-permute-start | bytes 3145736 | tf_op jit(solution)/shard_map/ppermute | solution.py:31
  76.6 0.1 slice.38
  76.7 0.2 collective-permute-start.19
  76.9 0.7 collective-permute-done.15
  77.6 2.9 %collective-permute-done.14 = bf16[2,256,256]{2,1,0:T(8,128)(2,1)S(1)} collective-permute-done((bf16[2,256,256]{2,1,0:T(8,128)(2,1)S(1)}, bf16[2,256,256]{2,1,0:T(8,128)(2,1)S(1)}, u32[]{:S(2)}, u32[]{:S(2)}) %collective-permute-start.14) | collective-permute-done | bytes 262176 | tf_op jit(solution)/shard_map/ppermute | solution.py:31
  80.5 0.1 pad_maximum_fusion.2.mine
  80.6 0.1 collective-permute-start.18
  80.7 8.8 %collective-permute-done.20.refs_4_ = bf16[2,256,1024]{2,1,0:T(8,128)(2,1)S(1)} collective-permute-done((bf16[2,256,1024]{2,1,0:T(8,128)(2,1)S(1)}, bf16[2,256,1024]{2,1,0:T(8,128)(2,1)S(1)}, u32[]{:S(2)}, u32[]{:S(2)}) %collective-permute-start.20) | collective-permute-done | bytes 1048608 | tf_op jit(solution)/shard_map/ppermute | solution.py:31
  89.5 3.3 %collective-permute-done.19.refs_3_ = bf16[2,256,1024]{2,1,0:T(8,128)(2,1)S(1)} collective-permute-done((bf16[2,256,1024]{2,1,0:T(8,128)(2,1)S(1)}, bf16[2,256,1024]{2,1,0:T(8,128)(2,1)S(1)}, u32[]{:S(2)}, u32[]{:S(2)}) %collective-permute-start.19) | collective-permute-done | bytes 1048608 | tf_op jit(solution)/shard_map/ppermute | solution.py:31
  92.8 2.3 %shard_map.38.one = f32[256,1024]{1,0:T(8,128)S(1)} custom-call(bf16[256,4096]{1,0:T(8,128)(2,1)S(1)} %get-tuple-element.18.row_ref, bf16[4,256,1024]{2,1,0:T(8,128)(2,1)S(1)} %pad_maximum_fusion.refs_0_, bf16[4,256,1024]{2,1,0:T(8,128)(2,1)S(1)} %collective-permute-done.16.refs_1_, bf16[4,256,1024]{2,1,0:T(8,128)(2,1)S(1)} %collective-permute-done.17.refs_2_, ...), custom_call_target="tpu_custom_call" | custom-call | flops 2147483648 | bytes 1048576 | tf_op jit(solution)/shard_map/pallas_call | solution.py:148
  95.1 3.5 %shard_map.39 = bf16[256,1024]{1,0:T(8,128)(2,1)} custom-call(bf16[2,256,256]{2,1,0:T(8,128)(2,1)S(1)} %pad_maximum_fusion.5.own, bf16[4,2,256,256]{3,2,1,0:T(8,128)(2,1)S(1)} %pad_maximum_fusion.2.mine, bf16[4,2,256,256]{3,2,1,0:T(8,128)(2,1)S(1)} %collective-permute-done.18.other, f32[256,1024]{1,0:T(8,128)S(1)} %shard_map.38.one, ...), custom_call_target="tpu_custom_call" | custom-call | flops 2147483648 | bytes 1048576 | tf_op jit(solution)/shard_map/pallas_call | solution.py:148
  (20 shorter events, 0.3 us)
Async XLA Ops:
  0.0 1.9 %copy-start = (bf16[256,2048]{1,0:T(8,128)(2,1)S(1)}, bf16[256,2048]{1,0:T(8,128)(2,1)}, u32[]{:S(2)}) copy-start(bf16[256,2048]{1,0:T(8,128)(2,1)} %param.4) | copy-start | bytes 3145732
  2.1 18.0 %collective-permute-start.4 = (bf16[256,1280]{1,0:T(8,128)(2,1)S(1)}, bf16[256,1280]{1,0:T(8,128)(2,1)S(1)}, u32[]{:S(2)}, u32[]{:S(2)}) collective-permute-start(bf16[256,1280]{1,0:T(8,128)(2,1)S(1)} %pad_maximum_fusion.3), channel_id=1, source_target_pairs={{192,0},{49,1},{194,2},{51,3},{196,4},{53,5},{198,6},{55,7},{200,8... | collective-permute-start | bytes 1966088 | tf_op jit(solution)/shard_map/ppermute | solution.py:31
  3.7 16.4 %collective-permute-start.3 = (bf16[256,1280]{1,0:T(8,128)(2,1)S(1)}, bf16[256,1280]{1,0:T(8,128)(2,1)S(1)}, u32[]{:S(2)}, u32[]{:S(2)}) collective-permute-start(bf16[256,1280]{1,0:T(8,128)(2,1)S(1)} %pad_maximum_fusion.3), channel_id=1, source_target_pairs={{128,0},{33,1},{130,2},{35,3},{132,4},{37,5},{134,6},{39,7},{136,8... | collective-permute-start | bytes 1966088 | tf_op jit(solution)/shard_map/ppermute | solution.py:31
  4.7 17.6 %collective-permute-start.2 = (bf16[256,1280]{1,0:T(8,128)(2,1)S(1)}, bf16[256,1280]{1,0:T(8,128)(2,1)S(1)}, u32[]{:S(2)}, u32[]{:S(2)}) collective-permute-start(bf16[256,1280]{1,0:T(8,128)(2,1)S(1)} %pad_maximum_fusion.3), channel_id=1, source_target_pairs={{64,0},{17,1},{66,2},{19,3},{68,4},{21,5},{70,6},{23,7},{72,8},{25... | collective-permute-start | bytes 1966088 | tf_op jit(solution)/shard_map/ppermute | solution.py:31
  7.1 13.0 %collective-permute-start.1 = (bf16[256,512]{1,0:T(8,128)(2,1)S(1)}, bf16[256,512]{1,0:T(8,128)(2,1)S(1)}, u32[]{:S(2)}, u32[]{:S(2)}) collective-permute-start(bf16[256,512]{1,0:T(8,128)(2,1)S(1)} %bitcast_multiply_fusion.own), channel_id=1, source_target_pairs={{4,0},{13,1},{6,2},{15,3},{8,4},{1,5},{10,6},{3,7},{12,8},{5,9},{1... | collective-permute-start | bytes 786440 | tf_op jit(solution)/shard_map/ppermute | solution.py:31
  13.4 18.3 %collective-permute-start = (bf16[256,512]{1,0:T(8,128)(2,1)S(1)}, bf16[256,512]{1,0:T(8,128)(2,1)S(1)}, u32[]{:S(2)}, u32[]{:S(2)}) collective-permute-start(bf16[256,512]{1,0:T(8,128)(2,1)S(1)} %bitcast_multiply_fusion.own), channel_id=1, source_target_pairs={{2,0},{15,1},{4,2},{1,3},{6,4},{3,5},{8,6},{5,7},{10,8},{7,9},{12,... | collective-permute-start | bytes 786440 | tf_op jit(solution)/shard_map/ppermute | solution.py:31
  22.3 28.3 %collective-permute-start.6 = (bf16[256,512]{1,0:T(8,128)(2,1)S(1)}, bf16[256,512]{1,0:T(8,128)(2,1)S(1)}, u32[]{:S(2)}, u32[]{:S(2)}) collective-permute-start(bf16[256,512]{1,0:T(8,128)(2,1)S(1)} %collective-permute-done.1), channel_id=1, source_target_pairs={{4,0},{6,2},{8,4},{10,6},{12,8},{14,10},{0,12},{2,14},{20,16},{22,... | collective-permute-start | bytes 786440 | tf_op jit(solution)/shard_map/ppermute | solution.py:31
  30.5 20.1 %collective-permute-start.5 = (bf16[256,512]{1,0:T(8,128)(2,1)S(1)}, bf16[256,512]{1,0:T(8,128)(2,1)S(1)}, u32[]{:S(2)}, u32[]{:S(2)}) collective-permute-start(bf16[256,512]{1,0:T(8,128)(2,1)S(1)} %collective-permute-done.1), channel_id=1, source_target_pairs={{2,0},{15,1},{4,2},{1,3},{6,4},{3,5},{8,6},{5,7},{10,8},{7,9},{12,... | collective-permute-start | bytes 786440 | tf_op jit(solution)/shard_map/ppermute | solution.py:31
  31.7 9.3 %collective-permute-start.9 = (bf16[4,256,256]{2,1,0:T(8,128)(2,1)S(1)}, bf16[4,256,256]{2,1,0:T(8,128)(2,1)S(1)}, u32[]{:S(2)}, u32[]{:S(2)}) collective-permute-start(bf16[4,256,256]{2,1,0:T(8,128)(2,1)S(1)} %pad_maximum_fusion.4.refs_0_), channel_id=1, source_target_pairs={{48,0},{193,1},{50,2},{195,3},{52,4},{197,5},{54,6},{199,7},{56,8}... | collective-permute-start | bytes 1572872 | tf_op jit(solution)/shard_map/ppermute | solution.py:31
  32.3 10.8 %collective-permute-start.8 = (bf16[4,256,256]{2,1,0:T(8,128)(2,1)S(1)}, bf16[4,256,256]{2,1,0:T(8,128)(2,1)S(1)}, u32[]{:S(2)}, u32[]{:S(2)}) collective-permute-start(bf16[4,256,256]{2,1,0:T(8,128)(2,1)S(1)} %pad_maximum_fusion.4.refs_0_), channel_id=1, source_target_pairs={{32,0},{129,1},{34,2},{131,3},{36,4},{133,5},{38,6},{135,7},{40,8}... | collective-permute-start | bytes 1572872 | tf_op jit(solution)/shard_map/ppermute | solution.py:31
  34.7 13.9 %collective-permute-start.7 = (bf16[4,256,256]{2,1,0:T(8,128)(2,1)S(1)}, bf16[4,256,256]{2,1,0:T(8,128)(2,1)S(1)}, u32[]{:S(2)}, u32[]{:S(2)}) collective-permute-start(bf16[4,256,256]{2,1,0:T(8,128)(2,1)S(1)} %pad_maximum_fusion.4.refs_0_), channel_id=1, source_target_pairs={{16,0},{65,1},{18,2},{67,3},{20,4},{69,5},{22,6},{71,7},{24,8},{73... | collective-permute-start | bytes 1572872 | tf_op jit(solution)/shard_map/ppermute | solution.py:31
  48.6 26.0 %collective-permute-start.17 = (bf16[4,256,1024]{2,1,0:T(8,128)(2,1)S(1)}, bf16[4,256,1024]{2,1,0:T(8,128)(2,1)S(1)}, u32[]{:S(2)}, u32[]{:S(2)}) collective-permute-start(bf16[4,256,1024]{2,1,0:T(8,128)(2,1)S(1)} %pad_maximum_fusion.refs_0_), channel_id=1, source_target_pairs={{48,0},{193,1},{50,2},{195,3},{52,4},{197,5},{54,6},{199,7},{56,8}... | collective-permute-start | bytes 6291464 | tf_op jit(solution)/shard_map/ppermute | solution.py:31
  49.3 27.4 %collective-permute-start.16 = (bf16[4,256,1024]{2,1,0:T(8,128)(2,1)S(1)}, bf16[4,256,1024]{2,1,0:T(8,128)(2,1)S(1)}, u32[]{:S(2)}, u32[]{:S(2)}) collective-permute-start(bf16[4,256,1024]{2,1,0:T(8,128)(2,1)S(1)} %pad_maximum_fusion.refs_0_), channel_id=1, source_target_pairs={{16,0},{65,1},{18,2},{67,3},{20,4},{69,5},{22,6},{71,7},{24,8},{73... | collective-permute-start | bytes 6291464 | tf_op jit(solution)/shard_map/ppermute | solution.py:31
  50.7 2.7 %collective-permute-start.10 = (bf16[4,256,512]{2,1,0:T(8,128)(2,1)S(1)}, bf16[4,256,512]{2,1,0:T(8,128)(2,1)S(1)}, u32[]{:S(2)}, u32[]{:S(2)}) collective-permute-start(bf16[4,256,512]{2,1,0:T(8,128)(2,1)S(1)} %pad_maximum_fusion.1.mine), channel_id=1, source_target_pairs={{1,0},{0,1},{3,2},{2,3},{5,4},{4,5},{7,6},{6,7},{9,8},{8,9},{11,10... | collective-permute-start | bytes 3145736 | tf_op jit(solution)/shard_map/ppermute | solution.py:31
  54.5 1.4 %collective-permute-start.11 = (bf16[256,256]{1,0:T(8,128)(2,1)S(1)}, bf16[256,256]{1,0:T(8,128)(2,1)S(1)}, u32[]{:S(2)}, u32[]{:S(2)}) collective-permute-start(bf16[256,256]{1,0:T(8,128)(2,1)S(1)} %get-tuple-element.15), channel_id=1, source_target_pairs={{1,0},{0,1},{3,2},{2,3},{5,4},{4,5},{7,6},{6,7},{9,8},{8,9},{11,10... | collective-permute-start | bytes 393224 | tf_op jit(solution)/shard_map/ppermute | solution.py:31
  56.0 9.6 %collective-permute-start.13 = (bf16[2,256,256]{2,1,0:T(8,128)(2,1)S(1)}, bf16[2,256,256]{2,1,0:T(8,128)(2,1)S(1)}, u32[]{:S(2)}, u32[]{:S(2)}) collective-permute-start(bf16[2,256,256]{2,1,0:T(8,128)(2,1)S(1)} %pad_maximum_fusion.5.own), channel_id=1, source_target_pairs={{4,0},{13,1},{6,2},{15,3},{8,4},{1,5},{10,6},{3,7},{12,8},{5,9},{1... | collective-permute-start | bytes 786440 | tf_op jit(solution)/shard_map/ppermute | solution.py:31
  56.6 20.3 %collective-permute-start.12 = (bf16[2,256,256]{2,1,0:T(8,128)(2,1)S(1)}, bf16[2,256,256]{2,1,0:T(8,128)(2,1)S(1)}, u32[]{:S(2)}, u32[]{:S(2)}) collective-permute-start(bf16[2,256,256]{2,1,0:T(8,128)(2,1)S(1)} %pad_maximum_fusion.5.own), channel_id=1, source_target_pairs={{2,0},{15,1},{4,2},{1,3},{6,4},{3,5},{8,6},{5,7},{10,8},{7,9},{12,... | collective-permute-start | bytes 786440 | tf_op jit(solution)/shard_map/ppermute | solution.py:31
  65.6 12.0 %collective-permute-start.15 = (bf16[2,256,256]{2,1,0:T(8,128)(2,1)S(1)}, bf16[2,256,256]{2,1,0:T(8,128)(2,1)S(1)}, u32[]{:S(2)}, u32[]{:S(2)}) collective-permute-start(bf16[2,256,256]{2,1,0:T(8,128)(2,1)S(1)} %collective-permute-done.13), channel_id=1, source_target_pairs={{4,0},{6,2},{8,4},{10,6},{12,8},{14,10},{0,12},{2,14},{20,16},{22,... | collective-permute-start | bytes 786440 | tf_op jit(solution)/shard_map/ppermute | solution.py:31
  69.8 10.7 %collective-permute-start.14 = (bf16[2,256,256]{2,1,0:T(8,128)(2,1)S(1)}, bf16[2,256,256]{2,1,0:T(8,128)(2,1)S(1)}, u32[]{:S(2)}, u32[]{:S(2)}) collective-permute-start(bf16[2,256,256]{2,1,0:T(8,128)(2,1)S(1)} %collective-permute-done.13), channel_id=1, source_target_pairs={{2,0},{15,1},{4,2},{1,3},{6,4},{3,5},{8,6},{5,7},{10,8},{7,9},{12,... | collective-permute-start | bytes 786440 | tf_op jit(solution)/shard_map/ppermute | solution.py:31
  74.7 14.9 %collective-permute-start.20 = (bf16[2,256,1024]{2,1,0:T(8,128)(2,1)S(1)}, bf16[2,256,1024]{2,1,0:T(8,128)(2,1)S(1)}, u32[]{:S(2)}, u32[]{:S(2)}) collective-permute-start(bf16[2,256,1024]{2,1,0:T(8,128)(2,1)S(1)} %slice.39), channel_id=1, source_target_pairs={{48,0},{193,1},{50,2},{195,3},{52,4},{197,5},{54,6},{199,7},{56,8}... | collective-permute-start | bytes 3145736 | tf_op jit(solution)/shard_map/ppermute | solution.py:31
  76.7 16.1 %collective-permute-start.19 = (bf16[2,256,1024]{2,1,0:T(8,128)(2,1)S(1)}, bf16[2,256,1024]{2,1,0:T(8,128)(2,1)S(1)}, u32[]{:S(2)}, u32[]{:S(2)}) collective-permute-start(bf16[2,256,1024]{2,1,0:T(8,128)(2,1)S(1)} %slice.38), channel_id=1, source_target_pairs={{16,0},{65,1},{18,2},{67,3},{20,4},{69,5},{22,6},{71,7},{24,8},{73... | collective-permute-start | bytes 3145736 | tf_op jit(solution)/shard_map/ppermute | solution.py:31
  80.6 14.5 %collective-permute-start.18 = (bf16[4,2,256,256]{3,2,1,0:T(8,128)(2,1)S(1)}, bf16[4,2,256,256]{3,2,1,0:T(8,128)(2,1)S(1)}, u32[]{:S(2)}, u32[]{:S(2)}) collective-permute-start(bf16[4,2,256,256]{3,2,1,0:T(8,128)(2,1)S(1)} %pad_maximum_fusion.2.mine), channel_id=1, source_target_pairs={{1,0},{0,1},{3,2},{2,3},{5,4},{4,5},{7,6},{6,7},{9,8},{8,9},{11,10... | collective-permute-start | bytes 3145736 | tf_op jit(solution)/shard_map/ppermute | solution.py:31

commit v3 on v2

--- a/solution.py
+++ b/solution.py
@@ -166,15 +166,17 @@
     own_panel = lax.dynamic_slice_in_dim(panel, core * WIDTH, WIDTH, 1)
 
     both = jnp.concatenate([own_columns, own_panel], 1)
-    near = [both] + [first(both, d) for d in (1, 2, 3)]
+    both_one, both_three = first(both, 1), first(both, 3)
+    columns_two = first(own_columns, 2)
     one_on, two_on = along(filtered, 1), along(filtered, 2)
-    near_columns = joined([block[:, :PART] for block in near])
-    near_panel = joined([block[:, PART:] for block in near])
+    near_columns = joined([own_columns, both_one[:, :PART], columns_two, both_three[:, :PART]])
 
     near_columns = after(near_columns, one_on, two_on)
-    two_tied = after(two_on, *near[1:])
+    pair = after(joined([one_on, two_on]), both_one, both_three, columns_two)
+    panel_two = first(after(own_panel, both_one, both_three, columns_two), 2)
+    near_panel = joined([own_panel, both_one[:, PART:], panel_two, both_three[:, PART:]])
     columns = [near_columns] + [second(near_columns, e) for e in (1, 2, 3)]
-    filtered_mine = joined([one_on, two_on, *farther(two_tied)])
+    filtered_mine = jnp.concatenate([pair, along(pair, 2)], 0)
     filtered_mine = after(filtered_mine, *columns[1:])
     filtered_line = (filtered, filtered_mine, swapped(filtered_mine))
 

time: 98.8 us -> 91.4 us (0.925)
  the two profiles are of different devices: /device:TPU:14 before, /device:TPU:1 now
where the time goes in v3:
time: 91.4 us; the launch traced here: 91.3 us
  waiting for transfers between devices  49.2 us (54%)
  starting transfers between devices  32 us (35%)
  Pallas kernels  6.84 us (7%)
  other arithmetic  2.45 us (3%)
    ppermute x21, waiting for transfers between devices, moved(): return lax.ppermute(block, AXES, route)  49.2 us
    ppermute x21, starting transfers between devices, moved(): return lax.ppermute(block, AXES, route)  32 us
    pallas_call x3, Pallas kernels, call(): pl.pallas_call(kernel, out_shape=out_shape, in_specs=[vmem] * len(operand...  6.84 us
  transfers between devices with their start and end apart: 21, of which 10 were waited for; matrix products, arithmetic and copies ran while one was open for 1% of the time, Pallas kernels for 4%

profile of v3, /device:TPU:1, one launch (start us, length us, event | category | flops | bytes accessed | tf_op | source)
XLA Modules:
  0.0 91.3 jit_solution(2978769010371361023)
XLA Ops:
  0.0 0.8 convert_element_type.3
  0.8 0.1 mul.17
  0.9 1.0 %bitcast_multiply_fusion.own = bf16[256,512]{1,0:T(8,128)(2,1)S(1)} fusion(bf16[256,512]{1,0:T(8,128)(2,1)} %param.3, bf16[32,8,4,128]{3,2,1,0:T(4,128)(2,1)S(1)} %bitcast.27), kind=kLoop, calls=%fused_computation.8 | loop fusion | flops 131072 | bytes 786432 | tf_op jit(solution)/shard_map/mul | solution.py:163
  2.1 2.1 %collective-permute-start.3 = (bf16[256,1280]{1,0:T(8,128)(2,1)S(1)}, bf16[256,1280]{1,0:T(8,128)(2,1)S(1)}, u32[]{:S(2)}, u32[]{:S(2)}) collective-permute-start(bf16[256,1280]{1,0:T(8,128)(2,1)S(1)} %pad_maximum_fusion.3), channel_id=1, source_target_pairs={{192,0},{49,1},{194,2},{51,3},{196,4},{53,5},{198,6},{55,7},{200,8... | collective-permute-start | bytes 1966088 | tf_op jit(solution)/shard_map/ppermute | solution.py:31
  4.2 1.4 %collective-permute-start.2 = (bf16[256,1280]{1,0:T(8,128)(2,1)S(1)}, bf16[256,1280]{1,0:T(8,128)(2,1)S(1)}, u32[]{:S(2)}, u32[]{:S(2)}) collective-permute-start(bf16[256,1280]{1,0:T(8,128)(2,1)S(1)} %pad_maximum_fusion.3), channel_id=1, source_target_pairs={{64,0},{17,1},{66,2},{19,3},{68,4},{21,5},{70,6},{23,7},{72,8},{25... | collective-permute-start | bytes 1966088 | tf_op jit(solution)/shard_map/ppermute | solution.py:31
  5.5 3.1 %collective-permute-start.1 = (bf16[256,512]{1,0:T(8,128)(2,1)S(1)}, bf16[256,512]{1,0:T(8,128)(2,1)S(1)}, u32[]{:S(2)}, u32[]{:S(2)}) collective-permute-start(bf16[256,512]{1,0:T(8,128)(2,1)S(1)} %bitcast_multiply_fusion.own), channel_id=1, source_target_pairs={{4,0},{13,1},{6,2},{15,3},{8,4},{1,5},{10,6},{3,7},{12,8},{5,9},{1... | collective-permute-start | bytes 786440 | tf_op jit(solution)/shard_map/ppermute | solution.py:31
  8.6 1.6 %collective-permute-start = (bf16[256,512]{1,0:T(8,128)(2,1)S(1)}, bf16[256,512]{1,0:T(8,128)(2,1)S(1)}, u32[]{:S(2)}, u32[]{:S(2)}) collective-permute-start(bf16[256,512]{1,0:T(8,128)(2,1)S(1)} %bitcast_multiply_fusion.own), channel_id=1, source_target_pairs={{2,0},{15,1},{4,2},{1,3},{6,4},{3,5},{8,6},{5,7},{10,8},{7,9},{12,... | collective-permute-start | bytes 786440 | tf_op jit(solution)/shard_map/ppermute | solution.py:31
  10.3 1.5 %collective-permute-start.4 = (bf16[256,256]{1,0:T(8,128)(2,1)S(1)}, bf16[256,256]{1,0:T(8,128)(2,1)S(1)}, u32[]{:S(2)}, u32[]{:S(2)}) collective-permute-start(bf16[256,256]{1,0:T(8,128)(2,1)S(1)} %constant_dynamic-slice_fusion.1), channel_id=1, source_target_pairs={{128,0},{33,1},{130,2},{35,3},{132,4},{37,5},{134,6},{39,7},{136,8... | collective-permute-start | bytes 393224 | tf_op jit(solution)/shard_map/ppermute | solution.py:31
  11.9 4.1 %collective-permute-done.1 = bf16[256,512]{1,0:T(8,128)(2,1)S(1)} collective-permute-done((bf16[256,512]{1,0:T(8,128)(2,1)S(1)}, bf16[256,512]{1,0:T(8,128)(2,1)S(1)}, u32[]{:S(2)}, u32[]{:S(2)}) %collective-permute-start.1) | collective-permute-done | bytes 262176 | tf_op jit(solution)/shard_map/ppermute | solution.py:31
  16.0 4.6 %collective-permute-done = bf16[256,512]{1,0:T(8,128)(2,1)S(1)} collective-permute-done((bf16[256,512]{1,0:T(8,128)(2,1)S(1)}, bf16[256,512]{1,0:T(8,128)(2,1)S(1)}, u32[]{:S(2)}, u32[]{:S(2)}) %collective-permute-start) | collective-permute-done | bytes 262176 | tf_op jit(solution)/shard_map/ppermute | solution.py:31
  20.6 0.1 pad_maximum_fusion.4
  20.7 0.0 collective-permute-done.4
  20.7 1.9 %collective-permute-start.15 = (bf16[256,1024]{1,0:T(8,128)(2,1)S(1)}, bf16[256,1024]{1,0:T(8,128)(2,1)S(1)}, u32[]{:S(2)}, u32[]{:S(2)}) collective-permute-start(bf16[256,1024]{1,0:T(8,128)(2,1)S(1)} %constant_dynamic-slice_fusion), channel_id=1, source_target_pairs={{128,0},{33,1},{130,2},{35,3},{132,4},{37,5},{134,6},{39,7},{136,8... | collective-permute-start | bytes 1572872 | tf_op jit(solution)/shard_map/ppermute | solution.py:31
  22.6 0.1 pad_maximum_fusion.5.refs_0_
  22.7 1.1 %collective-permute-start.8 = (bf16[4,256,256]{2,1,0:T(8,128)(2,1)S(1)}, bf16[4,256,256]{2,1,0:T(8,128)(2,1)S(1)}, u32[]{:S(2)}, u32[]{:S(2)}) collective-permute-start(bf16[4,256,256]{2,1,0:T(8,128)(2,1)S(1)} %pad_maximum_fusion.5.refs_0_), channel_id=1, source_target_pairs={{48,0},{193,1},{50,2},{195,3},{52,4},{197,5},{54,6},{199,7},{56,8}... | collective-permute-start | bytes 1572872 | tf_op jit(solution)/shard_map/ppermute | solution.py:31
  23.8 2.6 %collective-permute-start.7 = (bf16[4,256,256]{2,1,0:T(8,128)(2,1)S(1)}, bf16[4,256,256]{2,1,0:T(8,128)(2,1)S(1)}, u32[]{:S(2)}, u32[]{:S(2)}) collective-permute-start(bf16[4,256,256]{2,1,0:T(8,128)(2,1)S(1)} %pad_maximum_fusion.5.refs_0_), channel_id=1, source_target_pairs={{32,0},{129,1},{34,2},{131,3},{36,4},{133,5},{38,6},{135,7},{40,8}... | collective-permute-start | bytes 1572872 | tf_op jit(solution)/shard_map/ppermute | solution.py:31
  26.4 1.1 %collective-permute-start.6 = (bf16[4,256,256]{2,1,0:T(8,128)(2,1)S(1)}, bf16[4,256,256]{2,1,0:T(8,128)(2,1)S(1)}, u32[]{:S(2)}, u32[]{:S(2)}) collective-permute-start(bf16[4,256,256]{2,1,0:T(8,128)(2,1)S(1)} %pad_maximum_fusion.5.refs_0_), channel_id=1, source_target_pairs={{16,0},{65,1},{18,2},{67,3},{20,4},{69,5},{22,6},{71,7},{24,8},{73... | collective-permute-start | bytes 1572872 | tf_op jit(solution)/shard_map/ppermute | solution.py:31
  27.5 1.1 %collective-permute-start.5 = (bf16[2,256,512]{2,1,0:T(8,128)(2,1)S(1)}, bf16[2,256,512]{2,1,0:T(8,128)(2,1)S(1)}, u32[]{:S(2)}, u32[]{:S(2)}) collective-permute-start(bf16[2,256,512]{2,1,0:T(8,128)(2,1)S(1)} %pad_maximum_fusion.4), channel_id=1, source_target_pairs={{4,0},{13,1},{6,2},{15,3},{8,4},{1,5},{10,6},{3,7},{12,8},{5,9},{1... | collective-permute-start | bytes 1572872 | tf_op jit(solution)/shard_map/ppermute | solution.py:31
  28.6 0.1 slice_bitcast_fusion
  28.7 0.1 slice_bitcast_fusion.1
  28.7 2.0 %collective-permute-done.15 = bf16[256,1024]{1,0:T(8,128)(2,1)S(1)} collective-permute-done((bf16[256,1024]{1,0:T(8,128)(2,1)S(1)}, bf16[256,1024]{1,0:T(8,128)(2,1)S(1)}, u32[]{:S(2)}, u32[]{:S(2)}) %collective-permute-start.15) | collective-permute-done | bytes 524320 | tf_op jit(solution)/shard_map/ppermute | solution.py:31
  30.7 0.3 pad_maximum_fusion.refs_0_
  31.0 4.7 %collective-permute-done.8.refs_3_ = bf16[4,256,256]{2,1,0:T(8,128)(2,1)S(1)} collective-permute-done((bf16[4,256,256]{2,1,0:T(8,128)(2,1)S(1)}, bf16[4,256,256]{2,1,0:T(8,128)(2,1)S(1)}, u32[]{:S(2)}, u32[]{:S(2)}) %collective-permute-start.8) | collective-permute-done | bytes 524320 | tf_op jit(solution)/shard_map/ppermute | solution.py:31
  35.7 8.6 %collective-permute-done.7.refs_2_ = bf16[4,256,256]{2,1,0:T(8,128)(2,1)S(1)} collective-permute-done((bf16[4,256,256]{2,1,0:T(8,128)(2,1)S(1)}, bf16[4,256,256]{2,1,0:T(8,128)(2,1)S(1)}, u32[]{:S(2)}, u32[]{:S(2)}) %collective-permute-start.7) | collective-permute-done | bytes 524320 | tf_op jit(solution)/shard_map/ppermute | solution.py:31
  44.2 0.0 collective-permute-done.6.refs_1_
  44.2 2.7 %collective-permute-start.16 = (bf16[4,256,1024]{2,1,0:T(8,128)(2,1)S(1)}, bf16[4,256,1024]{2,1,0:T(8,128)(2,1)S(1)}, u32[]{:S(2)}, u32[]{:S(2)}) collective-permute-start(bf16[4,256,1024]{2,1,0:T(8,128)(2,1)S(1)} %pad_maximum_fusion.refs_0_), channel_id=1, source_target_pairs={{16,0},{65,1},{18,2},{67,3},{20,4},{69,5},{22,6},{71,7},{24,8},{73... | collective-permute-start | bytes 6291464 | tf_op jit(solution)/shard_map/ppermute | solution.py:31
  46.9 0.0 collective-permute-done.5
  46.9 0.1 pad_maximum_fusion.1.mine
  47.0 0.1 collective-permute-start.9
  47.1 2.6 %collective-permute-done.9.other = bf16[4,256,512]{2,1,0:T(8,128)(2,1)S(1)} collective-permute-done((bf16[4,256,512]{2,1,0:T(8,128)(2,1)S(1)}, bf16[4,256,512]{2,1,0:T(8,128)(2,1)S(1)}, u32[]{:S(2)}, u32[]{:S(2)}) %collective-permute-start.9) | collective-permute-done | bytes 1048608 | tf_op jit(solution)/shard_map/ppermute | solution.py:31
  49.7 1.1 %shard_map.37 = (bf16[256,4096]{1,0:T(8,128)(2,1)S(1)}, bf16[256,256]{1,0:T(8,128)(2,1)S(1)}) custom-call(bf16[256,512]{1,0:T(8,128)(2,1)S(1)} %bitcast_multiply_fusion.own, bf16[4,256,512]{2,1,0:T(8,128)(2,1)S(1)} %pad_maximum_fusion.1.mine, bf16[4,256,512]{2,1,0:T(8,128)(2,1)S(1)} %collective-permute-done.9.other, ...), custom_call_target="tpu_custom_call" | custom-call | flops 536870912 | bytes 1048576 | tf_op jit(solution)/shard_map/pallas_call | solution.py:148
  50.8 0.2 collective-permute-start.10
  51.0 1.2 %collective-permute-done.10 = bf16[256,256]{1,0:T(8,128)(2,1)S(1)} collective-permute-done((bf16[256,256]{1,0:T(8,128)(2,1)S(1)}, bf16[256,256]{1,0:T(8,128)(2,1)S(1)}, u32[]{:S(2)}, u32[]{:S(2)}) %collective-permute-start.10) | collective-permute-done | bytes 131104 | tf_op jit(solution)/shard_map/ppermute | solution.py:31
  52.3 0.3 collective-permute-start.12
  52.5 2.1 %collective-permute-start.11 = (bf16[2,256,256]{2,1,0:T(8,128)(2,1)S(1)}, bf16[2,256,256]{2,1,0:T(8,128)(2,1)S(1)}, u32[]{:S(2)}, u32[]{:S(2)}) collective-permute-start(bf16[2,256,256]{2,1,0:T(8,128)(2,1)S(1)} %pad_maximum_fusion.6.own), channel_id=1, source_target_pairs={{2,0},{15,1},{4,2},{1,3},{6,4},{3,5},{8,6},{5,7},{10,8},{7,9},{12,... | collective-permute-start | bytes 786440 | tf_op jit(solution)/shard_map/ppermute | solution.py:31
  54.7 8.2 %collective-permute-done.12 = bf16[2,256,256]{2,1,0:T(8,128)(2,1)S(1)} collective-permute-done((bf16[2,256,256]{2,1,0:T(8,128)(2,1)S(1)}, bf16[2,256,256]{2,1,0:T(8,128)(2,1)S(1)}, u32[]{:S(2)}, u32[]{:S(2)}) %collective-permute-start.12) | collective-permute-done | bytes 262176 | tf_op jit(solution)/shard_map/ppermute | solution.py:31
  62.8 0.7 collective-permute-start.14
  63.5 0.1 collective-permute-start.13
  63.6 6.9 %collective-permute-done.17.refs_2_ = bf16[4,256,1024]{2,1,0:T(8,128)(2,1)S(1)} collective-permute-done((bf16[4,256,1024]{2,1,0:T(8,128)(2,1)S(1)}, bf16[4,256,1024]{2,1,0:T(8,128)(2,1)S(1)}, u32[]{:S(2)}, u32[]{:S(2)}) %collective-permute-start.17) | collective-permute-done | bytes 2097184 | tf_op jit(solution)/shard_map/ppermute | solution.py:31
  70.5 0.1 slice.29
  70.5 0.1 collective-permute-start.20
  70.6 0.1 slice.28
  70.7 2.7 %collective-permute-start.19 = (bf16[2,256,1024]{2,1,0:T(8,128)(2,1)S(1)}, bf16[2,256,1024]{2,1,0:T(8,128)(2,1)S(1)}, u32[]{:S(2)}, u32[]{:S(2)}) collective-permute-start(bf16[2,256,1024]{2,1,0:T(8,128)(2,1)S(1)} %slice.28), channel_id=1, source_target_pairs={{16,0},{65,1},{18,2},{67,3},{20,4},{69,5},{22,6},{71,7},{24,8},{73... | collective-permute-start | bytes 3145736 | tf_op jit(solution)/shard_map/ppermute | solution.py:31
  73.4 0.1 pad_maximum_fusion.2.mine
  73.6 5.5 %collective-permute-start.18 = (bf16[4,2,256,256]{3,2,1,0:T(8,128)(2,1)S(1)}, bf16[4,2,256,256]{3,2,1,0:T(8,128)(2,1)S(1)}, u32[]{:S(2)}, u32[]{:S(2)}) collective-permute-start(bf16[4,2,256,256]{3,2,1,0:T(8,128)(2,1)S(1)} %pad_maximum_fusion.2.mine), channel_id=1, source_target_pairs={{1,0},{0,1},{3,2},{2,3},{5,4},{4,5},{7,6},{6,7},{9,8},{8,9},{11,10... | collective-permute-start | bytes 3145736 | tf_op jit(solution)/shard_map/ppermute | solution.py:31
  79.1 6.3 %collective-permute-done.20.refs_4_ = bf16[2,256,1024]{2,1,0:T(8,128)(2,1)S(1)} collective-permute-done((bf16[2,256,1024]{2,1,0:T(8,128)(2,1)S(1)}, bf16[2,256,1024]{2,1,0:T(8,128)(2,1)S(1)}, u32[]{:S(2)}, u32[]{:S(2)}) %collective-permute-start.20) | collective-permute-done | bytes 1048608 | tf_op jit(solution)/shard_map/ppermute | solution.py:31
  85.5 2.3 %shard_map.38.one = f32[256,1024]{1,0:T(8,128)S(1)} custom-call(bf16[256,4096]{1,0:T(8,128)(2,1)S(1)} %get-tuple-element.20.row_ref, bf16[4,256,1024]{2,1,0:T(8,128)(2,1)S(1)} %pad_maximum_fusion.refs_0_, bf16[4,256,1024]{2,1,0:T(8,128)(2,1)S(1)} %collective-permute-done.16.refs_1_, bf16[4,256,1024]{2,1,0:T(8,128)(2,1)S(1)} %collective-permute-done.17.refs_2_, ...), custom_call_target="tpu_custom_call" | custom-call | flops 2147483648 | bytes 1048576 | tf_op jit(solution)/shard_map/pallas_call | solution.py:148
  87.8 3.5 %shard_map.39 = bf16[256,1024]{1,0:T(8,128)(2,1)} custom-call(bf16[2,256,256]{2,1,0:T(8,128)(2,1)S(1)} %pad_maximum_fusion.6.own, bf16[4,2,256,256]{3,2,1,0:T(8,128)(2,1)S(1)} %pad_maximum_fusion.2.mine, bf16[4,2,256,256]{3,2,1,0:T(8,128)(2,1)S(1)} %collective-permute-done.18.other, f32[256,1024]{1,0:T(8,128)S(1)} %shard_map.38.one, ...), custom_call_target="tpu_custom_call" | custom-call | flops 2147483648 | bytes 1048576 | tf_op jit(solution)/shard_map/pallas_call | solution.py:148
  (19 shorter events, 0.2 us)
Async XLA Ops:
  0.0 1.9 %copy-start = (bf16[256,2048]{1,0:T(8,128)(2,1)S(1)}, bf16[256,2048]{1,0:T(8,128)(2,1)}, u32[]{:S(2)}) copy-start(bf16[256,2048]{1,0:T(8,128)(2,1)} %param.4) | copy-start | bytes 3145732
  2.1 18.6 %collective-permute-start.3 = (bf16[256,1280]{1,0:T(8,128)(2,1)S(1)}, bf16[256,1280]{1,0:T(8,128)(2,1)S(1)}, u32[]{:S(2)}, u32[]{:S(2)}) collective-permute-start(bf16[256,1280]{1,0:T(8,128)(2,1)S(1)} %pad_maximum_fusion.3), channel_id=1, source_target_pairs={{192,0},{49,1},{194,2},{51,3},{196,4},{53,5},{198,6},{55,7},{200,8... | collective-permute-start | bytes 1966088 | tf_op jit(solution)/shard_map/ppermute | solution.py:31
  4.2 16.5 %collective-permute-start.2 = (bf16[256,1280]{1,0:T(8,128)(2,1)S(1)}, bf16[256,1280]{1,0:T(8,128)(2,1)S(1)}, u32[]{:S(2)}, u32[]{:S(2)}) collective-permute-start(bf16[256,1280]{1,0:T(8,128)(2,1)S(1)} %pad_maximum_fusion.3), channel_id=1, source_target_pairs={{64,0},{17,1},{66,2},{19,3},{68,4},{21,5},{70,6},{23,7},{72,8},{25... | collective-permute-start | bytes 1966088 | tf_op jit(solution)/shard_map/ppermute | solution.py:31
  5.5 10.5 %collective-permute-start.1 = (bf16[256,512]{1,0:T(8,128)(2,1)S(1)}, bf16[256,512]{1,0:T(8,128)(2,1)S(1)}, u32[]{:S(2)}, u32[]{:S(2)}) collective-permute-start(bf16[256,512]{1,0:T(8,128)(2,1)S(1)} %bitcast_multiply_fusion.own), channel_id=1, source_target_pairs={{4,0},{13,1},{6,2},{15,3},{8,4},{1,5},{10,6},{3,7},{12,8},{5,9},{1... | collective-permute-start | bytes 786440 | tf_op jit(solution)/shard_map/ppermute | solution.py:31
  8.6 12.0 %collective-permute-start = (bf16[256,512]{1,0:T(8,128)(2,1)S(1)}, bf16[256,512]{1,0:T(8,128)(2,1)S(1)}, u32[]{:S(2)}, u32[]{:S(2)}) collective-permute-start(bf16[256,512]{1,0:T(8,128)(2,1)S(1)} %bitcast_multiply_fusion.own), channel_id=1, source_target_pairs={{2,0},{15,1},{4,2},{1,3},{6,4},{3,5},{8,6},{5,7},{10,8},{7,9},{12,... | collective-permute-start | bytes 786440 | tf_op jit(solution)/shard_map/ppermute | solution.py:31
  10.3 10.4 %collective-permute-start.4 = (bf16[256,256]{1,0:T(8,128)(2,1)S(1)}, bf16[256,256]{1,0:T(8,128)(2,1)S(1)}, u32[]{:S(2)}, u32[]{:S(2)}) collective-permute-start(bf16[256,256]{1,0:T(8,128)(2,1)S(1)} %constant_dynamic-slice_fusion.1), channel_id=1, source_target_pairs={{128,0},{33,1},{130,2},{35,3},{132,4},{37,5},{134,6},{39,7},{136,8... | collective-permute-start | bytes 393224 | tf_op jit(solution)/shard_map/ppermute | solution.py:31
  20.7 10.0 %collective-permute-start.15 = (bf16[256,1024]{1,0:T(8,128)(2,1)S(1)}, bf16[256,1024]{1,0:T(8,128)(2,1)S(1)}, u32[]{:S(2)}, u32[]{:S(2)}) collective-permute-start(bf16[256,1024]{1,0:T(8,128)(2,1)S(1)} %constant_dynamic-slice_fusion), channel_id=1, source_target_pairs={{128,0},{33,1},{130,2},{35,3},{132,4},{37,5},{134,6},{39,7},{136,8... | collective-permute-start | bytes 1572872 | tf_op jit(solution)/shard_map/ppermute | solution.py:31
  22.7 12.9 %collective-permute-start.8 = (bf16[4,256,256]{2,1,0:T(8,128)(2,1)S(1)}, bf16[4,256,256]{2,1,0:T(8,128)(2,1)S(1)}, u32[]{:S(2)}, u32[]{:S(2)}) collective-permute-start(bf16[4,256,256]{2,1,0:T(8,128)(2,1)S(1)} %pad_maximum_fusion.5.refs_0_), channel_id=1, source_target_pairs={{48,0},{193,1},{50,2},{195,3},{52,4},{197,5},{54,6},{199,7},{56,8}... | collective-permute-start | bytes 1572872 | tf_op jit(solution)/shard_map/ppermute | solution.py:31
  23.8 20.4 %collective-permute-start.7 = (bf16[4,256,256]{2,1,0:T(8,128)(2,1)S(1)}, bf16[4,256,256]{2,1,0:T(8,128)(2,1)S(1)}, u32[]{:S(2)}, u32[]{:S(2)}) collective-permute-start(bf16[4,256,256]{2,1,0:T(8,128)(2,1)S(1)} %pad_maximum_fusion.5.refs_0_), channel_id=1, source_target_pairs={{32,0},{129,1},{34,2},{131,3},{36,4},{133,5},{38,6},{135,7},{40,8}... | collective-permute-start | bytes 1572872 | tf_op jit(solution)/shard_map/ppermute | solution.py:31
  26.4 17.8 %collective-permute-start.6 = (bf16[4,256,256]{2,1,0:T(8,128)(2,1)S(1)}, bf16[4,256,256]{2,1,0:T(8,128)(2,1)S(1)}, u32[]{:S(2)}, u32[]{:S(2)}) collective-permute-start(bf16[4,256,256]{2,1,0:T(8,128)(2,1)S(1)} %pad_maximum_fusion.5.refs_0_), channel_id=1, source_target_pairs={{16,0},{65,1},{18,2},{67,3},{20,4},{69,5},{22,6},{71,7},{24,8},{73... | collective-permute-start | bytes 1572872 | tf_op jit(solution)/shard_map/ppermute | solution.py:31
  27.5 19.4 %collective-permute-start.5 = (bf16[2,256,512]{2,1,0:T(8,128)(2,1)S(1)}, bf16[2,256,512]{2,1,0:T(8,128)(2,1)S(1)}, u32[]{:S(2)}, u32[]{:S(2)}) collective-permute-start(bf16[2,256,512]{2,1,0:T(8,128)(2,1)S(1)} %pad_maximum_fusion.4), channel_id=1, source_target_pairs={{4,0},{13,1},{6,2},{15,3},{8,4},{1,5},{10,6},{3,7},{12,8},{5,9},{1... | collective-permute-start | bytes 1572872 | tf_op jit(solution)/shard_map/ppermute | solution.py:31
  44.2 26.2 %collective-permute-start.17 = (bf16[4,256,1024]{2,1,0:T(8,128)(2,1)S(1)}, bf16[4,256,1024]{2,1,0:T(8,128)(2,1)S(1)}, u32[]{:S(2)}, u32[]{:S(2)}) collective-permute-start(bf16[4,256,1024]{2,1,0:T(8,128)(2,1)S(1)} %pad_maximum_fusion.refs_0_), channel_id=1, source_target_pairs={{48,0},{193,1},{50,2},{195,3},{52,4},{197,5},{54,6},{199,7},{56,8}... | collective-permute-start | bytes 6291464 | tf_op jit(solution)/shard_map/ppermute | solution.py:31
  44.2 26.4 %collective-permute-start.16 = (bf16[4,256,1024]{2,1,0:T(8,128)(2,1)S(1)}, bf16[4,256,1024]{2,1,0:T(8,128)(2,1)S(1)}, u32[]{:S(2)}, u32[]{:S(2)}) collective-permute-start(bf16[4,256,1024]{2,1,0:T(8,128)(2,1)S(1)} %pad_maximum_fusion.refs_0_), channel_id=1, source_target_pairs={{16,0},{65,1},{18,2},{67,3},{20,4},{69,5},{22,6},{71,7},{24,8},{73... | collective-permute-start | bytes 6291464 | tf_op jit(solution)/shard_map/ppermute | solution.py:31
  47.0 2.7 %collective-permute-start.9 = (bf16[4,256,512]{2,1,0:T(8,128)(2,1)S(1)}, bf16[4,256,512]{2,1,0:T(8,128)(2,1)S(1)}, u32[]{:S(2)}, u32[]{:S(2)}) collective-permute-start(bf16[4,256,512]{2,1,0:T(8,128)(2,1)S(1)} %pad_maximum_fusion.1.mine), channel_id=1, source_target_pairs={{1,0},{0,1},{3,2},{2,3},{5,4},{4,5},{7,6},{6,7},{9,8},{8,9},{11,10... | collective-permute-start | bytes 3145736 | tf_op jit(solution)/shard_map/ppermute | solution.py:31
  50.8 1.4 %collective-permute-start.10 = (bf16[256,256]{1,0:T(8,128)(2,1)S(1)}, bf16[256,256]{1,0:T(8,128)(2,1)S(1)}, u32[]{:S(2)}, u32[]{:S(2)}) collective-permute-start(bf16[256,256]{1,0:T(8,128)(2,1)S(1)} %get-tuple-element.16), channel_id=1, source_target_pairs={{1,0},{0,1},{3,2},{2,3},{5,4},{4,5},{7,6},{6,7},{9,8},{8,9},{11,10... | collective-permute-start | bytes 393224 | tf_op jit(solution)/shard_map/ppermute | solution.py:31
  52.3 10.6 %collective-permute-start.12 = (bf16[2,256,256]{2,1,0:T(8,128)(2,1)S(1)}, bf16[2,256,256]{2,1,0:T(8,128)(2,1)S(1)}, u32[]{:S(2)}, u32[]{:S(2)}) collective-permute-start(bf16[2,256,256]{2,1,0:T(8,128)(2,1)S(1)} %pad_maximum_fusion.6.own), channel_id=1, source_target_pairs={{4,0},{13,1},{6,2},{15,3},{8,4},{1,5},{10,6},{3,7},{12,8},{5,9},{1... | collective-permute-start | bytes 786440 | tf_op jit(solution)/shard_map/ppermute | solution.py:31
  52.5 20.9 %collective-permute-start.11 = (bf16[2,256,256]{2,1,0:T(8,128)(2,1)S(1)}, bf16[2,256,256]{2,1,0:T(8,128)(2,1)S(1)}, u32[]{:S(2)}, u32[]{:S(2)}) collective-permute-start(bf16[2,256,256]{2,1,0:T(8,128)(2,1)S(1)} %pad_maximum_fusion.6.own), channel_id=1, source_target_pairs={{2,0},{15,1},{4,2},{1,3},{6,4},{3,5},{8,6},{5,7},{10,8},{7,9},{12,... | collective-permute-start | bytes 786440 | tf_op jit(solution)/shard_map/ppermute | solution.py:31
  62.8 10.6 %collective-permute-start.14 = (bf16[2,256,256]{2,1,0:T(8,128)(2,1)S(1)}, bf16[2,256,256]{2,1,0:T(8,128)(2,1)S(1)}, u32[]{:S(2)}, u32[]{:S(2)}) collective-permute-start(bf16[2,256,256]{2,1,0:T(8,128)(2,1)S(1)} %collective-permute-done.12), channel_id=1, source_target_pairs={{4,0},{6,2},{8,4},{10,6},{12,8},{14,10},{0,12},{2,14},{20,16},{22,... | collective-permute-start | bytes 786440 | tf_op jit(solution)/shard_map/ppermute | solution.py:31
  63.5 9.9 %collective-permute-start.13 = (bf16[2,256,256]{2,1,0:T(8,128)(2,1)S(1)}, bf16[2,256,256]{2,1,0:T(8,128)(2,1)S(1)}, u32[]{:S(2)}, u32[]{:S(2)}) collective-permute-start(bf16[2,256,256]{2,1,0:T(8,128)(2,1)S(1)} %collective-permute-done.12), channel_id=1, source_target_pairs={{2,0},{15,1},{4,2},{1,3},{6,4},{3,5},{8,6},{5,7},{10,8},{7,9},{12,... | collective-permute-start | bytes 786440 | tf_op jit(solution)/shard_map/ppermute | solution.py:31
  70.5 14.9 %collective-permute-start.20 = (bf16[2,256,1024]{2,1,0:T(8,128)(2,1)S(1)}, bf16[2,256,1024]{2,1,0:T(8,128)(2,1)S(1)}, u32[]{:S(2)}, u32[]{:S(2)}) collective-permute-start(bf16[2,256,1024]{2,1,0:T(8,128)(2,1)S(1)} %slice.29), channel_id=1, source_target_pairs={{48,0},{193,1},{50,2},{195,3},{52,4},{197,5},{54,6},{199,7},{56,8}... | collective-permute-start | bytes 3145736 | tf_op jit(solution)/shard_map/ppermute | solution.py:31
  70.7 14.8 %collective-permute-start.19 = (bf16[2,256,1024]{2,1,0:T(8,128)(2,1)S(1)}, bf16[2,256,1024]{2,1,0:T(8,128)(2,1)S(1)}, u32[]{:S(2)}, u32[]{:S(2)}) collective-permute-start(bf16[2,256,1024]{2,1,0:T(8,128)(2,1)S(1)} %slice.28), channel_id=1, source_target_pairs={{16,0},{65,1},{18,2},{67,3},{20,4},{69,5},{22,6},{71,7},{24,8},{73... | collective-permute-start | bytes 3145736 | tf_op jit(solution)/shard_map/ppermute | solution.py:31
  73.6 14.2 %collective-permute-start.18 = (bf16[4,2,256,256]{3,2,1,0:T(8,128)(2,1)S(1)}, bf16[4,2,256,256]{3,2,1,0:T(8,128)(2,1)S(1)}, u32[]{:S(2)}, u32[]{:S(2)}) collective-permute-start(bf16[4,2,256,256]{3,2,1,0:T(8,128)(2,1)S(1)} %pad_maximum_fusion.2.mine), channel_id=1, source_target_pairs={{1,0},{0,1},{3,2},{2,3},{5,4},{4,5},{7,6},{6,7},{9,8},{8,9},{11,10... | collective-permute-start | bytes 3145736 | tf_op jit(solution)/shard_map/ppermute | solution.py:31

commit v4 on v3

--- a/solution.py
+++ b/solution.py
@@ -127,26 +127,31 @@
 
 def single_kernel(places, row_ref, *refs):
     stacks, (out_ref,) = refs[: len(places)], refs[len(places) :]
-    out_ref[...] = contract(row_ref, places, stacks)
-
-
-def final_kernel(places, own, mine, other, one, *refs):
-    stacks, (out_ref, row_ref) = refs[: len(places)], refs[len(places) :]
+    out_ref[...] = 3.0 * contract(row_ref, places, stacks)
+
+
+def more_kernel(places, single, row_ref, *refs):
+    stacks, (out_ref,) = refs[: len(places)], refs[len(places) :]
+    out_ref[...] = single[...] + 3.0 * contract(row_ref, places, stacks)
+
+
+def last_kernel(places, own, mine, other, single, *refs):
+    stacks, (out_ref, squared_ref) = refs[: len(places)], refs[len(places) :]
     reorder(
         lambda h: own[h],
         lambda k, h: mine[k, h],
         lambda k, h: other[k, h],
-        row_ref,
+        squared_ref,
         lambda core, h: core if h == 0 else 1 - core,
     )
-    two = contract(row_ref, places, stacks)
-    out_ref[...] = (3.0 * one[...] - 2.0 * two).astype(BF16)
-
-
-def call(kernel, out_shape, scratch, flops, *operands):
+    out_ref[...] = (single[...] - 2.0 * contract(squared_ref, places, stacks)).astype(BF16)
+
+
+def call(kernel, parts, scratch, out_shape, flops, *operands):
+    operands += tuple(blocks for _, blocks in parts)
     vmem = pl.BlockSpec(memory_space=pltpu.VMEM)
     return pl.pallas_call(
-        kernel,
+        functools.partial(kernel, [place for place, _ in parts]),
         out_shape=out_shape,
         in_specs=[vmem] * len(operands),
         out_specs=jax.tree.map(lambda _: vmem, out_shape),
@@ -157,6 +162,8 @@
 
 
 def shards(density, panel, pattern):
+    panel_f32 = jax.ShapeDtypeStruct((ROWS, WIDTH), F32)
+    row_bf16 = jax.ShapeDtypeStruct((ROWS, DEPTH), BF16)
     core = lax.axis_index("c")
     mask = pattern.astype(BF16)
     filtered = (
@@ -173,7 +180,7 @@
 
     near_columns = after(near_columns, one_on, two_on)
     pair = after(joined([one_on, two_on]), both_one, both_three, columns_two)
-    panel_two = first(after(own_panel, both_one, both_three, columns_two), 2)
+    panel_two = first(after(own_panel, one_on), 2)
     near_panel = joined([own_panel, both_one[:, PART:], panel_two, both_three[:, PART:]])
     columns = [near_columns] + [second(near_columns, e) for e in (1, 2, 3)]
     filtered_mine = jnp.concatenate([pair, along(pair, 2)], 0)
@@ -183,42 +190,31 @@
     near_panel = after(near_panel, *columns[1:])
     plus, minus = second(near_panel, 1), second(near_panel, 3)
     row, squared = call(
-        functools.partial(square_kernel, [(e, 0) for e in range(NX)]),
-        (jax.ShapeDtypeStruct((ROWS, DEPTH), BF16), jax.ShapeDtypeStruct((ROWS, PART), BF16)),
+        square_kernel,
+        [((e, 0), blocks) for e, blocks in enumerate(columns)],
         [],
+        (row_bf16, jax.ShapeDtypeStruct((ROWS, PART), BF16)),
         2 * ROWS * DEPTH * PART,
         *filtered_line,
-        *columns,
     )
     squared = joined([squared, swapped(squared)])
     one_on, two_on = along(squared, 1), along(squared, 2)
     squared_mine = joined([one_on, two_on, *farther(two_on)])
     squared_mine = after(squared_mine, plus, minus)
     squared_line = (squared, squared_mine, swapped(squared_mine))
-    parts = [
-        (0, 0, near_panel),
-        (1, 0, plus),
-        (3, 0, minus),
-        (2, 0, second(plus[:2], 1)),
-        (2, 2, second(minus[2:], 3)),
-    ]
-    places, stacks = [(e, d) for e, d, _ in parts], [blocks for _, _, blocks in parts]
-    one = call(
-        functools.partial(single_kernel, places),
-        jax.ShapeDtypeStruct((ROWS, WIDTH), F32),
-        [],
-        2 * ROWS * DEPTH * WIDTH,
-        row,
-        *stacks,
-    )
+    early = [((0, 0), near_panel), ((1, 0), plus), ((3, 0), minus)]
+    late = [((2, 0), second(plus[:2], 1)), ((2, 2), second(minus[2:], 3))]
+    flops = 2 * ROWS * DEPTH * WIDTH
+    single = call(single_kernel, early, [], panel_f32, flops // 64, row)
+    single = call(more_kernel, late, [], panel_f32, flops, single, row)
     return call(
-        functools.partial(final_kernel, places),
+        last_kernel,
+        early + late,
+        [pltpu.VMEM((ROWS, DEPTH), BF16)],
         jax.ShapeDtypeStruct((ROWS, WIDTH), BF16),
-        [pltpu.VMEM((ROWS, DEPTH), BF16)],
-        2 * ROWS * DEPTH * WIDTH,
+        flops,
         *squared_line,
-        one,
-        *stacks,
+        single,
     )
 
 

time: 91.4 us -> 88.6 us (0.969)
  waiting for transfers between devices: 49.2 us -> 47 us
    ppermute x21, waiting for transfers between devices: 49.2 us -> 47 us  [moved(): return lax.ppermute(block, AXES, route)]
    pallas_call x3 -> x4, Pallas kernels: 6.84 us -> 7.03 us  [call(): pl.pallas_call(functools.partial(kernel, [place for place, _ in parts]),...]
  transfers between devices with their start and end apart: 21 -> 21, of which waited for: 10 -> 11; matrix products, arithmetic and copies ran while one was open for 1% -> 1% of each run, Pallas kernels for 4% -> 4%
where the time goes in v4:
time: 88.6 us; the launch traced here: 88.4 us
  waiting for transfers between devices  47 us (53%)
  starting transfers between devices  31.1 us (35%)
  Pallas kernels  7.03 us (8%)
  other arithmetic  2.45 us (3%)
    ppermute x21, waiting for transfers between devices, moved(): return lax.ppermute(block, AXES, route)  47 us
    ppermute x21, starting transfers between devices, moved(): return lax.ppermute(block, AXES, route)  31.1 us
    pallas_call x4, Pallas kernels, call(): pl.pallas_call(functools.partial(kernel, [place for place, _ in parts]),...  7.03 us
  transfers between devices with their start and end apart: 21, of which 11 were waited for; matrix products, arithmetic and copies ran while one was open for 1% of the time, Pallas kernels for 4%

profile of v4, /device:TPU:1, one launch (start us, length us, event | category | flops | bytes accessed | tf_op | source)
XLA Modules:
  0.0 88.4 jit_solution(9829315977119810426)
XLA Ops:
  0.0 0.8 convert_element_type.3
  0.8 0.1 mul.17
  0.9 1.0 %bitcast_multiply_fusion.own = bf16[256,512]{1,0:T(8,128)(2,1)S(1)} fusion(bf16[256,512]{1,0:T(8,128)(2,1)} %param.3, bf16[32,8,4,128]{3,2,1,0:T(4,128)(2,1)S(1)} %bitcast.27), kind=kLoop, calls=%fused_computation.8 | loop fusion | flops 131072 | bytes 786432 | tf_op jit(solution)/shard_map/mul | solution.py:170
  2.1 2.1 %collective-permute-start.3 = (bf16[256,1280]{1,0:T(8,128)(2,1)S(1)}, bf16[256,1280]{1,0:T(8,128)(2,1)S(1)}, u32[]{:S(2)}, u32[]{:S(2)}) collective-permute-start(bf16[256,1280]{1,0:T(8,128)(2,1)S(1)} %pad_maximum_fusion.3), channel_id=1, source_target_pairs={{192,0},{49,1},{194,2},{51,3},{196,4},{53,5},{198,6},{55,7},{200,8... | collective-permute-start | bytes 1966088 | tf_op jit(solution)/shard_map/ppermute | solution.py:31
  4.2 1.4 %collective-permute-start.2 = (bf16[256,1280]{1,0:T(8,128)(2,1)S(1)}, bf16[256,1280]{1,0:T(8,128)(2,1)S(1)}, u32[]{:S(2)}, u32[]{:S(2)}) collective-permute-start(bf16[256,1280]{1,0:T(8,128)(2,1)S(1)} %pad_maximum_fusion.3), channel_id=1, source_target_pairs={{64,0},{17,1},{66,2},{19,3},{68,4},{21,5},{70,6},{23,7},{72,8},{25... | collective-permute-start | bytes 1966088 | tf_op jit(solution)/shard_map/ppermute | solution.py:31
  5.5 1.7 %collective-permute-start = (bf16[256,512]{1,0:T(8,128)(2,1)S(1)}, bf16[256,512]{1,0:T(8,128)(2,1)S(1)}, u32[]{:S(2)}, u32[]{:S(2)}) collective-permute-start(bf16[256,512]{1,0:T(8,128)(2,1)S(1)} %bitcast_multiply_fusion.own), channel_id=1, source_target_pairs={{2,0},{15,1},{4,2},{1,3},{6,4},{3,5},{8,6},{5,7},{10,8},{7,9},{12,... | collective-permute-start | bytes 786440 | tf_op jit(solution)/shard_map/ppermute | solution.py:31
  7.3 3.0 %collective-permute-start.1 = (bf16[256,512]{1,0:T(8,128)(2,1)S(1)}, bf16[256,512]{1,0:T(8,128)(2,1)S(1)}, u32[]{:S(2)}, u32[]{:S(2)}) collective-permute-start(bf16[256,512]{1,0:T(8,128)(2,1)S(1)} %bitcast_multiply_fusion.own), channel_id=1, source_target_pairs={{4,0},{13,1},{6,2},{15,3},{8,4},{1,5},{10,6},{3,7},{12,8},{5,9},{1... | collective-permute-start | bytes 786440 | tf_op jit(solution)/shard_map/ppermute | solution.py:31
  10.3 1.5 %collective-permute-start.4 = (bf16[256,256]{1,0:T(8,128)(2,1)S(1)}, bf16[256,256]{1,0:T(8,128)(2,1)S(1)}, u32[]{:S(2)}, u32[]{:S(2)}) collective-permute-start(bf16[256,256]{1,0:T(8,128)(2,1)S(1)} %constant_dynamic-slice_fusion.1), channel_id=1, source_target_pairs={{128,0},{33,1},{130,2},{35,3},{132,4},{37,5},{134,6},{39,7},{136,8... | collective-permute-start | bytes 393224 | tf_op jit(solution)/shard_map/ppermute | solution.py:31
  11.9 3.4 %collective-permute-done = bf16[256,512]{1,0:T(8,128)(2,1)S(1)} collective-permute-done((bf16[256,512]{1,0:T(8,128)(2,1)S(1)}, bf16[256,512]{1,0:T(8,128)(2,1)S(1)}, u32[]{:S(2)}, u32[]{:S(2)}) %collective-permute-start) | collective-permute-done | bytes 262176 | tf_op jit(solution)/shard_map/ppermute | solution.py:31
  15.3 1.5 %collective-permute-start.15 = (bf16[256,1024]{1,0:T(8,128)(2,1)S(1)}, bf16[256,1024]{1,0:T(8,128)(2,1)S(1)}, u32[]{:S(2)}, u32[]{:S(2)}) collective-permute-start(bf16[256,1024]{1,0:T(8,128)(2,1)S(1)} %constant_dynamic-slice_fusion), channel_id=1, source_target_pairs={{128,0},{33,1},{130,2},{35,3},{132,4},{37,5},{134,6},{39,7},{136,8... | collective-permute-start | bytes 1572872 | tf_op jit(solution)/shard_map/ppermute | solution.py:31
  16.8 3.0 %collective-permute-done.1 = bf16[256,512]{1,0:T(8,128)(2,1)S(1)} collective-permute-done((bf16[256,512]{1,0:T(8,128)(2,1)S(1)}, bf16[256,512]{1,0:T(8,128)(2,1)S(1)}, u32[]{:S(2)}, u32[]{:S(2)}) %collective-permute-start.1) | collective-permute-done | bytes 262176 | tf_op jit(solution)/shard_map/ppermute | solution.py:31
  19.8 0.1 pad_maximum_fusion.4
  19.9 0.0 collective-permute-done.2
  19.9 0.1 pad_maximum_fusion.5.refs_0_
  20.0 2.5 %collective-permute-start.6 = (bf16[4,256,256]{2,1,0:T(8,128)(2,1)S(1)}, bf16[4,256,256]{2,1,0:T(8,128)(2,1)S(1)}, u32[]{:S(2)}, u32[]{:S(2)}) collective-permute-start(bf16[4,256,256]{2,1,0:T(8,128)(2,1)S(1)} %pad_maximum_fusion.5.refs_0_), channel_id=1, source_target_pairs={{16,0},{65,1},{18,2},{67,3},{20,4},{69,5},{22,6},{71,7},{24,8},{73... | collective-permute-start | bytes 1572872 | tf_op jit(solution)/shard_map/ppermute | solution.py:31
  22.5 0.3 collective-permute-start.7
  22.9 0.7 collective-permute-start.8
  23.6 0.2 collective-permute-start.5
  23.8 0.1 slice_bitcast_fusion
  23.9 0.1 slice_bitcast_fusion.1
  23.9 1.2 %collective-permute-done.15 = bf16[256,1024]{1,0:T(8,128)(2,1)S(1)} collective-permute-done((bf16[256,1024]{1,0:T(8,128)(2,1)S(1)}, bf16[256,1024]{1,0:T(8,128)(2,1)S(1)}, u32[]{:S(2)}, u32[]{:S(2)}) %collective-permute-start.15) | collective-permute-done | bytes 524320 | tf_op jit(solution)/shard_map/ppermute | solution.py:31
  25.1 0.3 pad_maximum_fusion.refs_0_
  25.4 13.6 %collective-permute-done.6.refs_1_ = bf16[4,256,256]{2,1,0:T(8,128)(2,1)S(1)} collective-permute-done((bf16[4,256,256]{2,1,0:T(8,128)(2,1)S(1)}, bf16[4,256,256]{2,1,0:T(8,128)(2,1)S(1)}, u32[]{:S(2)}, u32[]{:S(2)}) %collective-permute-start.6) | collective-permute-done | bytes 524320 | tf_op jit(solution)/shard_map/ppermute | solution.py:31
  39.0 0.0 collective-permute-done.7.refs_2_
  39.0 1.2 %collective-permute-done.8.refs_3_ = bf16[4,256,256]{2,1,0:T(8,128)(2,1)S(1)} collective-permute-done((bf16[4,256,256]{2,1,0:T(8,128)(2,1)S(1)}, bf16[4,256,256]{2,1,0:T(8,128)(2,1)S(1)}, u32[]{:S(2)}, u32[]{:S(2)}) %collective-permute-start.8) | collective-permute-done | bytes 524320 | tf_op jit(solution)/shard_map/ppermute | solution.py:31
  40.2 2.2 %collective-permute-start.16 = (bf16[4,256,1024]{2,1,0:T(8,128)(2,1)S(1)}, bf16[4,256,1024]{2,1,0:T(8,128)(2,1)S(1)}, u32[]{:S(2)}, u32[]{:S(2)}) collective-permute-start(bf16[4,256,1024]{2,1,0:T(8,128)(2,1)S(1)} %pad_maximum_fusion.refs_0_), channel_id=1, source_target_pairs={{16,0},{65,1},{18,2},{67,3},{20,4},{69,5},{22,6},{71,7},{24,8},{73... | collective-permute-start | bytes 6291464 | tf_op jit(solution)/shard_map/ppermute | solution.py:31
  42.4 0.1 pad_maximum_fusion.1.mine
  42.5 1.3 %collective-permute-start.9 = (bf16[4,256,512]{2,1,0:T(8,128)(2,1)S(1)}, bf16[4,256,512]{2,1,0:T(8,128)(2,1)S(1)}, u32[]{:S(2)}, u32[]{:S(2)}) collective-permute-start(bf16[4,256,512]{2,1,0:T(8,128)(2,1)S(1)} %pad_maximum_fusion.1.mine), channel_id=1, source_target_pairs={{1,0},{0,1},{3,2},{2,3},{5,4},{4,5},{7,6},{6,7},{9,8},{8,9},{11,10... | collective-permute-start | bytes 3145736 | tf_op jit(solution)/shard_map/ppermute | solution.py:31
  43.8 2.3 %collective-permute-done.9.other = bf16[4,256,512]{2,1,0:T(8,128)(2,1)S(1)} collective-permute-done((bf16[4,256,512]{2,1,0:T(8,128)(2,1)S(1)}, bf16[4,256,512]{2,1,0:T(8,128)(2,1)S(1)}, u32[]{:S(2)}, u32[]{:S(2)}) %collective-permute-start.9) | collective-permute-done | bytes 1048608 | tf_op jit(solution)/shard_map/ppermute | solution.py:31
  46.1 1.1 %shard_map.37 = (bf16[256,4096]{1,0:T(8,128)(2,1)S(1)}, bf16[256,256]{1,0:T(8,128)(2,1)S(1)}) custom-call(bf16[256,512]{1,0:T(8,128)(2,1)S(1)} %bitcast_multiply_fusion.own, bf16[4,256,512]{2,1,0:T(8,128)(2,1)S(1)} %pad_maximum_fusion.1.mine, bf16[4,256,512]{2,1,0:T(8,128)(2,1)S(1)} %collective-permute-done.9.other, ...), custom_call_target="tpu_custom_call" | custom-call | flops 536870912 | bytes 1048576 | tf_op jit(solution)/shard_map/pallas_call | solution.py:153
  47.2 0.4 collective-permute-start.10
  47.6 1.0 %collective-permute-done.10 = bf16[256,256]{1,0:T(8,128)(2,1)S(1)} collective-permute-done((bf16[256,256]{1,0:T(8,128)(2,1)S(1)}, bf16[256,256]{1,0:T(8,128)(2,1)S(1)}, u32[]{:S(2)}, u32[]{:S(2)}) %collective-permute-start.10) | collective-permute-done | bytes 131104 | tf_op jit(solution)/shard_map/ppermute | solution.py:31
  48.7 2.4 %collective-permute-start.12 = (bf16[2,256,256]{2,1,0:T(8,128)(2,1)S(1)}, bf16[2,256,256]{2,1,0:T(8,128)(2,1)S(1)}, u32[]{:S(2)}, u32[]{:S(2)}) collective-permute-start(bf16[2,256,256]{2,1,0:T(8,128)(2,1)S(1)} %pad_maximum_fusion.6.own), channel_id=1, source_target_pairs={{4,0},{13,1},{6,2},{15,3},{8,4},{1,5},{10,6},{3,7},{12,8},{5,9},{1... | collective-permute-start | bytes 786440 | tf_op jit(solution)/shard_map/ppermute | solution.py:31
  51.1 0.0 collective-permute-start.11
  51.1 8.8 %collective-permute-done.12 = bf16[2,256,256]{2,1,0:T(8,128)(2,1)S(1)} collective-permute-done((bf16[2,256,256]{2,1,0:T(8,128)(2,1)S(1)}, bf16[2,256,256]{2,1,0:T(8,128)(2,1)S(1)}, u32[]{:S(2)}, u32[]{:S(2)}) %collective-permute-start.12) | collective-permute-done | bytes 262176 | tf_op jit(solution)/shard_map/ppermute | solution.py:31
  59.8 0.7 collective-permute-start.14
  60.5 4.9 %collective-permute-done.16.refs_1_ = bf16[4,256,1024]{2,1,0:T(8,128)(2,1)S(1)} collective-permute-done((bf16[4,256,1024]{2,1,0:T(8,128)(2,1)S(1)}, bf16[4,256,1024]{2,1,0:T(8,128)(2,1)S(1)}, u32[]{:S(2)}, u32[]{:S(2)}) %collective-permute-start.16) | collective-permute-done | bytes 2097184 | tf_op jit(solution)/shard_map/ppermute | solution.py:31
  65.4 0.1 slice.28
  65.4 3.5 %collective-permute-start.19 = (bf16[2,256,1024]{2,1,0:T(8,128)(2,1)S(1)}, bf16[2,256,1024]{2,1,0:T(8,128)(2,1)S(1)}, u32[]{:S(2)}, u32[]{:S(2)}) collective-permute-start(bf16[2,256,1024]{2,1,0:T(8,128)(2,1)S(1)} %slice.28), channel_id=1, source_target_pairs={{16,0},{65,1},{18,2},{67,3},{20,4},{69,5},{22,6},{71,7},{24,8},{73... | collective-permute-start | bytes 3145736 | tf_op jit(solution)/shard_map/ppermute | solution.py:31
  68.9 0.1 slice.29
  69.0 0.1 collective-permute-start.20
  69.1 0.1 pad_maximum_fusion.2.mine
  69.3 5.4 %collective-permute-start.18 = (bf16[4,2,256,256]{3,2,1,0:T(8,128)(2,1)S(1)}, bf16[4,2,256,256]{3,2,1,0:T(8,128)(2,1)S(1)}, u32[]{:S(2)}, u32[]{:S(2)}) collective-permute-start(bf16[4,2,256,256]{3,2,1,0:T(8,128)(2,1)S(1)} %pad_maximum_fusion.2.mine), channel_id=1, source_target_pairs={{1,0},{0,1},{3,2},{2,3},{5,4},{4,5},{7,6},{6,7},{9,8},{8,9},{11,10... | collective-permute-start | bytes 3145736 | tf_op jit(solution)/shard_map/ppermute | solution.py:31
  74.7 1.8 %shard_map.38.single = f32[256,1024]{1,0:T(8,128)S(1)} custom-call(bf16[256,4096]{1,0:T(8,128)(2,1)S(1)} %get-tuple-element.20.row_ref, bf16[4,256,1024]{2,1,0:T(8,128)(2,1)S(1)} %pad_maximum_fusion.refs_0_, bf16[4,256,1024]{2,1,0:T(8,128)(2,1)S(1)} %collective-permute-done.16.refs_1_, bf16[4,256,1024]{2,1,0:T(8,128)(2,1)S(1)} %collective-permute-done.17.refs_2_), custom_call_target="tpu_custom_call" | custom-call | flops 33554432 | bytes 1048576 | tf_op jit(solution)/shard_map/pallas_call | solution.py:153
  76.5 4.2 %collective-permute-done.19.refs_0_.refs_3_ = bf16[2,256,1024]{2,1,0:T(8,128)(2,1)S(1)} collective-permute-done((bf16[2,256,1024]{2,1,0:T(8,128)(2,1)S(1)}, bf16[2,256,1024]{2,1,0:T(8,128)(2,1)S(1)}, u32[]{:S(2)}, u32[]{:S(2)}) %collective-permute-start.19) | collective-permute-done | bytes 1048608 | tf_op jit(solution)/shard_map/ppermute | solution.py:31
  80.7 3.6 %collective-permute-done.20.refs_1_.refs_4_ = bf16[2,256,1024]{2,1,0:T(8,128)(2,1)S(1)} collective-permute-done((bf16[2,256,1024]{2,1,0:T(8,128)(2,1)S(1)}, bf16[2,256,1024]{2,1,0:T(8,128)(2,1)S(1)}, u32[]{:S(2)}, u32[]{:S(2)}) %collective-permute-start.20) | collective-permute-done | bytes 1048608 | tf_op jit(solution)/shard_map/ppermute | solution.py:31
  84.2 0.7 shard_map.39.single
  85.0 3.5 %shard_map.40 = bf16[256,1024]{1,0:T(8,128)(2,1)} custom-call(bf16[2,256,256]{2,1,0:T(8,128)(2,1)S(1)} %pad_maximum_fusion.6.own, bf16[4,2,256,256]{3,2,1,0:T(8,128)(2,1)S(1)} %pad_maximum_fusion.2.mine, bf16[4,2,256,256]{3,2,1,0:T(8,128)(2,1)S(1)} %collective-permute-done.18.other, f32[256,1024]{1,0:T(8,128)S(1)} %shard_map.39.single, ...), custom_call_target="tpu_custom_call" | custom-call | flops 2147483648 | bytes 1048576 | tf_op jit(solution)/shard_map/pallas_call | solution.py:153
  (20 shorter events, 0.2 us)
Async XLA Ops:
  0.0 1.9 %copy-start = (bf16[256,2048]{1,0:T(8,128)(2,1)S(1)}, bf16[256,2048]{1,0:T(8,128)(2,1)}, u32[]{:S(2)}) copy-start(bf16[256,2048]{1,0:T(8,128)(2,1)} %param.4) | copy-start | bytes 3145732
  2.1 17.8 %collective-permute-start.3 = (bf16[256,1280]{1,0:T(8,128)(2,1)S(1)}, bf16[256,1280]{1,0:T(8,128)(2,1)S(1)}, u32[]{:S(2)}, u32[]{:S(2)}) collective-permute-start(bf16[256,1280]{1,0:T(8,128)(2,1)S(1)} %pad_maximum_fusion.3), channel_id=1, source_target_pairs={{192,0},{49,1},{194,2},{51,3},{196,4},{53,5},{198,6},{55,7},{200,8... | collective-permute-start | bytes 1966088 | tf_op jit(solution)/shard_map/ppermute | solution.py:31
  4.2 15.7 %collective-permute-start.2 = (bf16[256,1280]{1,0:T(8,128)(2,1)S(1)}, bf16[256,1280]{1,0:T(8,128)(2,1)S(1)}, u32[]{:S(2)}, u32[]{:S(2)}) collective-permute-start(bf16[256,1280]{1,0:T(8,128)(2,1)S(1)} %pad_maximum_fusion.3), channel_id=1, source_target_pairs={{64,0},{17,1},{66,2},{19,3},{68,4},{21,5},{70,6},{23,7},{72,8},{25... | collective-permute-start | bytes 1966088 | tf_op jit(solution)/shard_map/ppermute | solution.py:31
  5.5 9.7 %collective-permute-start = (bf16[256,512]{1,0:T(8,128)(2,1)S(1)}, bf16[256,512]{1,0:T(8,128)(2,1)S(1)}, u32[]{:S(2)}, u32[]{:S(2)}) collective-permute-start(bf16[256,512]{1,0:T(8,128)(2,1)S(1)} %bitcast_multiply_fusion.own), channel_id=1, source_target_pairs={{2,0},{15,1},{4,2},{1,3},{6,4},{3,5},{8,6},{5,7},{10,8},{7,9},{12,... | collective-permute-start | bytes 786440 | tf_op jit(solution)/shard_map/ppermute | solution.py:31
  7.3 12.5 %collective-permute-start.1 = (bf16[256,512]{1,0:T(8,128)(2,1)S(1)}, bf16[256,512]{1,0:T(8,128)(2,1)S(1)}, u32[]{:S(2)}, u32[]{:S(2)}) collective-permute-start(bf16[256,512]{1,0:T(8,128)(2,1)S(1)} %bitcast_multiply_fusion.own), channel_id=1, source_target_pairs={{4,0},{13,1},{6,2},{15,3},{8,4},{1,5},{10,6},{3,7},{12,8},{5,9},{1... | collective-permute-start | bytes 786440 | tf_op jit(solution)/shard_map/ppermute | solution.py:31
  10.3 9.6 %collective-permute-start.4 = (bf16[256,256]{1,0:T(8,128)(2,1)S(1)}, bf16[256,256]{1,0:T(8,128)(2,1)S(1)}, u32[]{:S(2)}, u32[]{:S(2)}) collective-permute-start(bf16[256,256]{1,0:T(8,128)(2,1)S(1)} %constant_dynamic-slice_fusion.1), channel_id=1, source_target_pairs={{128,0},{33,1},{130,2},{35,3},{132,4},{37,5},{134,6},{39,7},{136,8... | collective-permute-start | bytes 393224 | tf_op jit(solution)/shard_map/ppermute | solution.py:31
  15.3 9.8 %collective-permute-start.15 = (bf16[256,1024]{1,0:T(8,128)(2,1)S(1)}, bf16[256,1024]{1,0:T(8,128)(2,1)S(1)}, u32[]{:S(2)}, u32[]{:S(2)}) collective-permute-start(bf16[256,1024]{1,0:T(8,128)(2,1)S(1)} %constant_dynamic-slice_fusion), channel_id=1, source_target_pairs={{128,0},{33,1},{130,2},{35,3},{132,4},{37,5},{134,6},{39,7},{136,8... | collective-permute-start | bytes 1572872 | tf_op jit(solution)/shard_map/ppermute | solution.py:31
  20.0 19.0 %collective-permute-start.6 = (bf16[4,256,256]{2,1,0:T(8,128)(2,1)S(1)}, bf16[4,256,256]{2,1,0:T(8,128)(2,1)S(1)}, u32[]{:S(2)}, u32[]{:S(2)}) collective-permute-start(bf16[4,256,256]{2,1,0:T(8,128)(2,1)S(1)} %pad_maximum_fusion.5.refs_0_), channel_id=1, source_target_pairs={{16,0},{65,1},{18,2},{67,3},{20,4},{69,5},{22,6},{71,7},{24,8},{73... | collective-permute-start | bytes 1572872 | tf_op jit(solution)/shard_map/ppermute | solution.py:31
  22.5 16.4 %collective-permute-start.7 = (bf16[4,256,256]{2,1,0:T(8,128)(2,1)S(1)}, bf16[4,256,256]{2,1,0:T(8,128)(2,1)S(1)}, u32[]{:S(2)}, u32[]{:S(2)}) collective-permute-start(bf16[4,256,256]{2,1,0:T(8,128)(2,1)S(1)} %pad_maximum_fusion.5.refs_0_), channel_id=1, source_target_pairs={{32,0},{129,1},{34,2},{131,3},{36,4},{133,5},{38,6},{135,7},{40,8}... | collective-permute-start | bytes 1572872 | tf_op jit(solution)/shard_map/ppermute | solution.py:31
  22.9 17.3 %collective-permute-start.8 = (bf16[4,256,256]{2,1,0:T(8,128)(2,1)S(1)}, bf16[4,256,256]{2,1,0:T(8,128)(2,1)S(1)}, u32[]{:S(2)}, u32[]{:S(2)}) collective-permute-start(bf16[4,256,256]{2,1,0:T(8,128)(2,1)S(1)} %pad_maximum_fusion.5.refs_0_), channel_id=1, source_target_pairs={{48,0},{193,1},{50,2},{195,3},{52,4},{197,5},{54,6},{199,7},{56,8}... | collective-permute-start | bytes 1572872 | tf_op jit(solution)/shard_map/ppermute | solution.py:31
  23.6 18.8 %collective-permute-start.5 = (bf16[2,256,512]{2,1,0:T(8,128)(2,1)S(1)}, bf16[2,256,512]{2,1,0:T(8,128)(2,1)S(1)}, u32[]{:S(2)}, u32[]{:S(2)}) collective-permute-start(bf16[2,256,512]{2,1,0:T(8,128)(2,1)S(1)} %pad_maximum_fusion.4), channel_id=1, source_target_pairs={{4,0},{13,1},{6,2},{15,3},{8,4},{1,5},{10,6},{3,7},{12,8},{5,9},{1... | collective-permute-start | bytes 1572872 | tf_op jit(solution)/shard_map/ppermute | solution.py:31
  40.2 25.2 %collective-permute-start.16 = (bf16[4,256,1024]{2,1,0:T(8,128)(2,1)S(1)}, bf16[4,256,1024]{2,1,0:T(8,128)(2,1)S(1)}, u32[]{:S(2)}, u32[]{:S(2)}) collective-permute-start(bf16[4,256,1024]{2,1,0:T(8,128)(2,1)S(1)} %pad_maximum_fusion.refs_0_), channel_id=1, source_target_pairs={{16,0},{65,1},{18,2},{67,3},{20,4},{69,5},{22,6},{71,7},{24,8},{73... | collective-permute-start | bytes 6291464 | tf_op jit(solution)/shard_map/ppermute | solution.py:31
  42.4 26.5 %collective-permute-start.17 = (bf16[4,256,1024]{2,1,0:T(8,128)(2,1)S(1)}, bf16[4,256,1024]{2,1,0:T(8,128)(2,1)S(1)}, u32[]{:S(2)}, u32[]{:S(2)}) collective-permute-start(bf16[4,256,1024]{2,1,0:T(8,128)(2,1)S(1)} %pad_maximum_fusion.refs_0_), channel_id=1, source_target_pairs={{48,0},{193,1},{50,2},{195,3},{52,4},{197,5},{54,6},{199,7},{56,8}... | collective-permute-start | bytes 6291464 | tf_op jit(solution)/shard_map/ppermute | solution.py:31
  42.5 3.6 %collective-permute-start.9 = (bf16[4,256,512]{2,1,0:T(8,128)(2,1)S(1)}, bf16[4,256,512]{2,1,0:T(8,128)(2,1)S(1)}, u32[]{:S(2)}, u32[]{:S(2)}) collective-permute-start(bf16[4,256,512]{2,1,0:T(8,128)(2,1)S(1)} %pad_maximum_fusion.1.mine), channel_id=1, source_target_pairs={{1,0},{0,1},{3,2},{2,3},{5,4},{4,5},{7,6},{6,7},{9,8},{8,9},{11,10... | collective-permute-start | bytes 3145736 | tf_op jit(solution)/shard_map/ppermute | solution.py:31
  47.2 1.4 %collective-permute-start.10 = (bf16[256,256]{1,0:T(8,128)(2,1)S(1)}, bf16[256,256]{1,0:T(8,128)(2,1)S(1)}, u32[]{:S(2)}, u32[]{:S(2)}) collective-permute-start(bf16[256,256]{1,0:T(8,128)(2,1)S(1)} %get-tuple-element.16), channel_id=1, source_target_pairs={{1,0},{0,1},{3,2},{2,3},{5,4},{4,5},{7,6},{6,7},{9,8},{8,9},{11,10... | collective-permute-start | bytes 393224 | tf_op jit(solution)/shard_map/ppermute | solution.py:31
  48.7 11.2 %collective-permute-start.12 = (bf16[2,256,256]{2,1,0:T(8,128)(2,1)S(1)}, bf16[2,256,256]{2,1,0:T(8,128)(2,1)S(1)}, u32[]{:S(2)}, u32[]{:S(2)}) collective-permute-start(bf16[2,256,256]{2,1,0:T(8,128)(2,1)S(1)} %pad_maximum_fusion.6.own), channel_id=1, source_target_pairs={{4,0},{13,1},{6,2},{15,3},{8,4},{1,5},{10,6},{3,7},{12,8},{5,9},{1... | collective-permute-start | bytes 786440 | tf_op jit(solution)/shard_map/ppermute | solution.py:31
  51.1 18.0 %collective-permute-start.11 = (bf16[2,256,256]{2,1,0:T(8,128)(2,1)S(1)}, bf16[2,256,256]{2,1,0:T(8,128)(2,1)S(1)}, u32[]{:S(2)}, u32[]{:S(2)}) collective-permute-start(bf16[2,256,256]{2,1,0:T(8,128)(2,1)S(1)} %pad_maximum_fusion.6.own), channel_id=1, source_target_pairs={{2,0},{15,1},{4,2},{1,3},{6,4},{3,5},{8,6},{5,7},{10,8},{7,9},{12,... | collective-permute-start | bytes 786440 | tf_op jit(solution)/shard_map/ppermute | solution.py:31
  59.8 9.3 %collective-permute-start.13 = (bf16[2,256,256]{2,1,0:T(8,128)(2,1)S(1)}, bf16[2,256,256]{2,1,0:T(8,128)(2,1)S(1)}, u32[]{:S(2)}, u32[]{:S(2)}) collective-permute-start(bf16[2,256,256]{2,1,0:T(8,128)(2,1)S(1)} %collective-permute-done.12), channel_id=1, source_target_pairs={{2,0},{15,1},{4,2},{1,3},{6,4},{3,5},{8,6},{5,7},{10,8},{7,9},{12,... | collective-permute-start | bytes 786440 | tf_op jit(solution)/shard_map/ppermute | solution.py:31
  59.8 9.3 %collective-permute-start.14 = (bf16[2,256,256]{2,1,0:T(8,128)(2,1)S(1)}, bf16[2,256,256]{2,1,0:T(8,128)(2,1)S(1)}, u32[]{:S(2)}, u32[]{:S(2)}) collective-permute-start(bf16[2,256,256]{2,1,0:T(8,128)(2,1)S(1)} %collective-permute-done.12), channel_id=1, source_target_pairs={{4,0},{6,2},{8,4},{10,6},{12,8},{14,10},{0,12},{2,14},{20,16},{22,... | collective-permute-start | bytes 786440 | tf_op jit(solution)/shard_map/ppermute | solution.py:31
  65.4 15.2 %collective-permute-start.19 = (bf16[2,256,1024]{2,1,0:T(8,128)(2,1)S(1)}, bf16[2,256,1024]{2,1,0:T(8,128)(2,1)S(1)}, u32[]{:S(2)}, u32[]{:S(2)}) collective-permute-start(bf16[2,256,1024]{2,1,0:T(8,128)(2,1)S(1)} %slice.28), channel_id=1, source_target_pairs={{16,0},{65,1},{18,2},{67,3},{20,4},{69,5},{22,6},{71,7},{24,8},{73... | collective-permute-start | bytes 3145736 | tf_op jit(solution)/shard_map/ppermute | solution.py:31
  69.0 15.2 %collective-permute-start.20 = (bf16[2,256,1024]{2,1,0:T(8,128)(2,1)S(1)}, bf16[2,256,1024]{2,1,0:T(8,128)(2,1)S(1)}, u32[]{:S(2)}, u32[]{:S(2)}) collective-permute-start(bf16[2,256,1024]{2,1,0:T(8,128)(2,1)S(1)} %slice.29), channel_id=1, source_target_pairs={{48,0},{193,1},{50,2},{195,3},{52,4},{197,5},{54,6},{199,7},{56,8}... | collective-permute-start | bytes 3145736 | tf_op jit(solution)/shard_map/ppermute | solution.py:31
  69.3 15.7 %collective-permute-start.18 = (bf16[4,2,256,256]{3,2,1,0:T(8,128)(2,1)S(1)}, bf16[4,2,256,256]{3,2,1,0:T(8,128)(2,1)S(1)}, u32[]{:S(2)}, u32[]{:S(2)}) collective-permute-start(bf16[4,2,256,256]{3,2,1,0:T(8,128)(2,1)S(1)} %pad_maximum_fusion.2.mine), channel_id=1, source_target_pairs={{1,0},{0,1},{3,2},{2,3},{5,4},{4,5},{7,6},{6,7},{9,8},{8,9},{11,10... | collective-permute-start | bytes 3145736 | tf_op jit(solution)/shard_map/ppermute | solution.py:31

commit v5 on v4

--- a/solution.py
+++ b/solution.py
@@ -130,21 +130,27 @@
     out_ref[...] = 3.0 * contract(row_ref, places, stacks)
 
 
-def more_kernel(places, single, row_ref, *refs):
-    stacks, (out_ref,) = refs[: len(places)], refs[len(places) :]
-    out_ref[...] = single[...] + 3.0 * contract(row_ref, places, stacks)
-
-
-def last_kernel(places, own, mine, other, single, *refs):
-    stacks, (out_ref, squared_ref) = refs[: len(places)], refs[len(places) :]
+def double_kernel(places, own, mine, far, other, other_far, single, *refs):
+    stacks, (row_ref, out_ref) = refs[: len(places)], refs[len(places) :]
+
+    def read(near, beyond):
+        return lambda k, h: near[k, h] if k < 2 else beyond[k - 2, h]
+
     reorder(
         lambda h: own[h],
-        lambda k, h: mine[k, h],
-        lambda k, h: other[k, h],
-        squared_ref,
+        read(mine, far),
+        read(other, other_far),
+        row_ref,
         lambda core, h: core if h == 0 else 1 - core,
     )
-    out_ref[...] = (single[...] - 2.0 * contract(squared_ref, places, stacks)).astype(BF16)
+    out_ref[...] = single[...] - 2.0 * contract(row_ref, places, stacks)
+
+
+def last_kernel(places, row_ref, squared_ref, total, *refs):
+    stacks, (out_ref,) = refs[: len(places)], refs[len(places) :]
+    once = contract(row_ref, places, stacks)
+    twice = contract(squared_ref, places, stacks)
+    out_ref[...] = (total[...] + (3.0 * once - 2.0 * twice)).astype(BF16)
 
 
 def call(kernel, parts, scratch, out_shape, flops, *operands):
@@ -187,8 +193,8 @@
     filtered_mine = after(filtered_mine, *columns[1:])
     filtered_line = (filtered, filtered_mine, swapped(filtered_mine))
 
-    near_panel = after(near_panel, *columns[1:])
-    plus, minus = second(near_panel, 1), second(near_panel, 3)
+    plus = second(after(near_panel, columns[1], columns[2]), 1)
+    minus = second(after(near_panel, *columns[1:]), 3)
     row, squared = call(
         square_kernel,
         [((e, 0), blocks) for e, blocks in enumerate(columns)],
@@ -199,22 +205,35 @@
     )
     squared = joined([squared, swapped(squared)])
     one_on, two_on = along(squared, 1), along(squared, 2)
-    squared_mine = joined([one_on, two_on, *farther(two_on)])
-    squared_mine = after(squared_mine, plus, minus)
-    squared_line = (squared, squared_mine, swapped(squared_mine))
+    mine = joined([one_on, two_on])
+    far = joined(list(farther(two_on)))
     early = [((0, 0), near_panel), ((1, 0), plus), ((3, 0), minus)]
-    late = [((2, 0), second(plus[:2], 1)), ((2, 2), second(minus[2:], 3))]
+    plus_part = after(plus[:2], one_on, two_on)
+    late = [((2, 0), second(plus_part, 1)), ((2, 2), second(minus[2:], 3))]
     flops = 2 * ROWS * DEPTH * WIDTH
-    single = call(single_kernel, early, [], panel_f32, flops // 64, row)
-    single = call(more_kernel, late, [], panel_f32, flops, single, row)
+    single = call(single_kernel, early, [], panel_f32, flops, row)
+    squared_row, total = call(
+        double_kernel,
+        early,
+        [],
+        (row_bf16, panel_f32),
+        flops // 1,
+        squared,
+        mine,
+        far,
+        swapped(mine),
+        swapped(far),
+        single,
+    )
     return call(
         last_kernel,
-        early + late,
-        [pltpu.VMEM((ROWS, DEPTH), BF16)],
+        late,
+        [],
         jax.ShapeDtypeStruct((ROWS, WIDTH), BF16),
-        flops,
-        *squared_line,
-        single,
+        flops // 64,
+        row,
+        squared_row,
+        total,
     )
 
 

time: 88.6 us -> 86.4 us (0.975)
  waiting for transfers between devices: 47 us -> 42 us
  starting transfers between devices: 31.1 us -> 34.1 us
    ppermute x21 -> x22, waiting for transfers between devices: 47 us -> 42 us  [moved(): return lax.ppermute(block, AXES, route)]
    ppermute x21 -> x22, starting transfers between devices: 31.1 us -> 34.1 us  [moved(): return lax.ppermute(block, AXES, route)]
  transfers between devices with their start and end apart: 21 -> 22, of which waited for: 11 -> 10; matrix products, arithmetic and copies ran while one was open for 1% -> 1% of each run, Pallas kernels for 4% -> 6%
where the time goes in v5:
time: 86.4 us; the launch traced here: 86.3 us
  waiting for transfers between devices  42 us (49%)
  starting transfers between devices  34.1 us (39%)
  Pallas kernels  7.05 us (8%)
  other arithmetic  2.42 us (3%)
    ppermute x22, waiting for transfers between devices, moved(): return lax.ppermute(block, AXES, route)  42 us
    ppermute x22, starting transfers between devices, moved(): return lax.ppermute(block, AXES, route)  34.1 us
    pallas_call x4, Pallas kernels, call(): pl.pallas_call(functools.partial(kernel, [place for place, _ in parts]),...  7.05 us
  transfers between devices with their start and end apart: 22, of which 10 were waited for; matrix products, arithmetic and copies ran while one was open for 1% of the time, Pallas kernels for 6%

profile of v5, /device:TPU:1, one launch (start us, length us, event | category | flops | bytes accessed | tf_op | source)
XLA Modules:
  0.0 86.3 jit_solution(2292657806254544007)
XLA Ops:
  0.0 0.8 convert_element_type.3
  0.8 0.1 mul.17
  0.9 1.0 %bitcast_multiply_fusion.own = bf16[256,512]{1,0:T(8,128)(2,1)S(1)} fusion(bf16[256,512]{1,0:T(8,128)(2,1)} %param.3, bf16[32,8,4,128]{3,2,1,0:T(4,128)(2,1)S(1)} %bitcast.27), kind=kLoop, calls=%fused_computation.9 | loop fusion | flops 131072 | bytes 786432 | tf_op jit(solution)/shard_map/mul | solution.py:176
  2.1 2.1 %collective-permute-start.3 = (bf16[256,1280]{1,0:T(8,128)(2,1)S(1)}, bf16[256,1280]{1,0:T(8,128)(2,1)S(1)}, u32[]{:S(2)}, u32[]{:S(2)}) collective-permute-start(bf16[256,1280]{1,0:T(8,128)(2,1)S(1)} %pad_maximum_fusion.2), channel_id=1, source_target_pairs={{192,0},{49,1},{194,2},{51,3},{196,4},{53,5},{198,6},{55,7},{200,8... | collective-permute-start | bytes 1966088 | tf_op jit(solution)/shard_map/ppermute | solution.py:31
  4.2 1.4 %collective-permute-start.2 = (bf16[256,1280]{1,0:T(8,128)(2,1)S(1)}, bf16[256,1280]{1,0:T(8,128)(2,1)S(1)}, u32[]{:S(2)}, u32[]{:S(2)}) collective-permute-start(bf16[256,1280]{1,0:T(8,128)(2,1)S(1)} %pad_maximum_fusion.2), channel_id=1, source_target_pairs={{64,0},{17,1},{66,2},{19,3},{68,4},{21,5},{70,6},{23,7},{72,8},{25... | collective-permute-start | bytes 1966088 | tf_op jit(solution)/shard_map/ppermute | solution.py:31
  5.5 1.7 %collective-permute-start = (bf16[256,512]{1,0:T(8,128)(2,1)S(1)}, bf16[256,512]{1,0:T(8,128)(2,1)S(1)}, u32[]{:S(2)}, u32[]{:S(2)}) collective-permute-start(bf16[256,512]{1,0:T(8,128)(2,1)S(1)} %bitcast_multiply_fusion.own), channel_id=1, source_target_pairs={{2,0},{15,1},{4,2},{1,3},{6,4},{3,5},{8,6},{5,7},{10,8},{7,9},{12,... | collective-permute-start | bytes 786440 | tf_op jit(solution)/shard_map/ppermute | solution.py:31
  7.3 3.0 %collective-permute-start.1 = (bf16[256,512]{1,0:T(8,128)(2,1)S(1)}, bf16[256,512]{1,0:T(8,128)(2,1)S(1)}, u32[]{:S(2)}, u32[]{:S(2)}) collective-permute-start(bf16[256,512]{1,0:T(8,128)(2,1)S(1)} %bitcast_multiply_fusion.own), channel_id=1, source_target_pairs={{4,0},{13,1},{6,2},{15,3},{8,4},{1,5},{10,6},{3,7},{12,8},{5,9},{1... | collective-permute-start | bytes 786440 | tf_op jit(solution)/shard_map/ppermute | solution.py:31
  10.3 1.5 %collective-permute-start.4 = (bf16[256,256]{1,0:T(8,128)(2,1)S(1)}, bf16[256,256]{1,0:T(8,128)(2,1)S(1)}, u32[]{:S(2)}, u32[]{:S(2)}) collective-permute-start(bf16[256,256]{1,0:T(8,128)(2,1)S(1)} %constant_dynamic-slice_fusion.1), channel_id=1, source_target_pairs={{128,0},{33,1},{130,2},{35,3},{132,4},{37,5},{134,6},{39,7},{136,8... | collective-permute-start | bytes 393224 | tf_op jit(solution)/shard_map/ppermute | solution.py:31
  11.9 3.4 %collective-permute-done = bf16[256,512]{1,0:T(8,128)(2,1)S(1)} collective-permute-done((bf16[256,512]{1,0:T(8,128)(2,1)S(1)}, bf16[256,512]{1,0:T(8,128)(2,1)S(1)}, u32[]{:S(2)}, u32[]{:S(2)}) %collective-permute-start) | collective-permute-done | bytes 262176 | tf_op jit(solution)/shard_map/ppermute | solution.py:31
  15.3 1.5 %collective-permute-start.17 = (bf16[256,1024]{1,0:T(8,128)(2,1)S(1)}, bf16[256,1024]{1,0:T(8,128)(2,1)S(1)}, u32[]{:S(2)}, u32[]{:S(2)}) collective-permute-start(bf16[256,1024]{1,0:T(8,128)(2,1)S(1)} %constant_dynamic-slice_fusion), channel_id=1, source_target_pairs={{128,0},{33,1},{130,2},{35,3},{132,4},{37,5},{134,6},{39,7},{136,8... | collective-permute-start | bytes 1572872 | tf_op jit(solution)/shard_map/ppermute | solution.py:31
  16.8 3.0 %collective-permute-done.1 = bf16[256,512]{1,0:T(8,128)(2,1)S(1)} collective-permute-done((bf16[256,512]{1,0:T(8,128)(2,1)S(1)}, bf16[256,512]{1,0:T(8,128)(2,1)S(1)}, u32[]{:S(2)}, u32[]{:S(2)}) %collective-permute-start.1) | collective-permute-done | bytes 262176 | tf_op jit(solution)/shard_map/ppermute | solution.py:31
  19.8 0.1 pad_maximum_fusion.3
  19.9 0.0 collective-permute-done.3
  19.9 0.1 pad_maximum_fusion.4.refs_0_
  20.0 2.5 %collective-permute-start.6 = (bf16[4,256,256]{2,1,0:T(8,128)(2,1)S(1)}, bf16[4,256,256]{2,1,0:T(8,128)(2,1)S(1)}, u32[]{:S(2)}, u32[]{:S(2)}) collective-permute-start(bf16[4,256,256]{2,1,0:T(8,128)(2,1)S(1)} %pad_maximum_fusion.4.refs_0_), channel_id=1, source_target_pairs={{16,0},{65,1},{18,2},{67,3},{20,4},{69,5},{22,6},{71,7},{24,8},{73... | collective-permute-start | bytes 1572872 | tf_op jit(solution)/shard_map/ppermute | solution.py:31
  22.5 0.3 collective-permute-start.7
  22.9 0.7 collective-permute-start.8
  23.6 0.2 collective-permute-start.5
  23.8 0.1 slice_bitcast_fusion
  23.9 0.1 slice_bitcast_fusion.1
  23.9 1.2 %collective-permute-done.17 = bf16[256,1024]{1,0:T(8,128)(2,1)S(1)} collective-permute-done((bf16[256,1024]{1,0:T(8,128)(2,1)S(1)}, bf16[256,1024]{1,0:T(8,128)(2,1)S(1)}, u32[]{:S(2)}, u32[]{:S(2)}) %collective-permute-start.17) | collective-permute-done | bytes 524320 | tf_op jit(solution)/shard_map/ppermute | solution.py:31
  25.1 0.3 pad_maximum_fusion.refs_0_
  25.4 13.6 %collective-permute-done.6.refs_1_ = bf16[4,256,256]{2,1,0:T(8,128)(2,1)S(1)} collective-permute-done((bf16[4,256,256]{2,1,0:T(8,128)(2,1)S(1)}, bf16[4,256,256]{2,1,0:T(8,128)(2,1)S(1)}, u32[]{:S(2)}, u32[]{:S(2)}) %collective-permute-start.6) | collective-permute-done | bytes 524320 | tf_op jit(solution)/shard_map/ppermute | solution.py:31
  39.0 3.4 %collective-permute-start.18 = (bf16[4,256,1024]{2,1,0:T(8,128)(2,1)S(1)}, bf16[4,256,1024]{2,1,0:T(8,128)(2,1)S(1)}, u32[]{:S(2)}, u32[]{:S(2)}) collective-permute-start(bf16[4,256,1024]{2,1,0:T(8,128)(2,1)S(1)} %pad_maximum_fusion.refs_0_), channel_id=1, source_target_pairs={{16,0},{65,1},{18,2},{67,3},{20,4},{69,5},{22,6},{71,7},{24,8},{73... | collective-permute-start | bytes 6291464 | tf_op jit(solution)/shard_map/ppermute | solution.py:31
  42.4 0.1 pad_maximum_fusion.1.mine
  42.5 0.1 collective-permute-start.9
  42.6 2.6 %collective-permute-done.9.other = bf16[4,256,512]{2,1,0:T(8,128)(2,1)S(1)} collective-permute-done((bf16[4,256,512]{2,1,0:T(8,128)(2,1)S(1)}, bf16[4,256,512]{2,1,0:T(8,128)(2,1)S(1)}, u32[]{:S(2)}, u32[]{:S(2)}) %collective-permute-start.9) | collective-permute-done | bytes 1048608 | tf_op jit(solution)/shard_map/ppermute | solution.py:31
  45.2 1.1 %shard_map.37 = (bf16[256,4096]{1,0:T(8,128)(2,1)S(1)}, bf16[256,256]{1,0:T(8,128)(2,1)S(1)}) custom-call(bf16[256,512]{1,0:T(8,128)(2,1)S(1)} %bitcast_multiply_fusion.own, bf16[4,256,512]{2,1,0:T(8,128)(2,1)S(1)} %pad_maximum_fusion.1.mine, bf16[4,256,512]{2,1,0:T(8,128)(2,1)S(1)} %collective-permute-done.9.other, ...), custom_call_target="tpu_custom_call" | custom-call | flops 536870912 | bytes 1048576 | tf_op jit(solution)/shard_map/pallas_call | solution.py:159
  46.3 0.2 collective-permute-start.10
  46.5 1.2 %collective-permute-done.10 = bf16[256,256]{1,0:T(8,128)(2,1)S(1)} collective-permute-done((bf16[256,256]{1,0:T(8,128)(2,1)S(1)}, bf16[256,256]{1,0:T(8,128)(2,1)S(1)}, u32[]{:S(2)}, u32[]{:S(2)}) %collective-permute-start.10) | collective-permute-done | bytes 131104 | tf_op jit(solution)/shard_map/ppermute | solution.py:31
  47.8 2.6 %collective-permute-start.12 = (bf16[2,256,256]{2,1,0:T(8,128)(2,1)S(1)}, bf16[2,256,256]{2,1,0:T(8,128)(2,1)S(1)}, u32[]{:S(2)}, u32[]{:S(2)}) collective-permute-start(bf16[2,256,256]{2,1,0:T(8,128)(2,1)S(1)} %pad_maximum_fusion.7.own), channel_id=1, source_target_pairs={{4,0},{13,1},{6,2},{15,3},{8,4},{1,5},{10,6},{3,7},{12,8},{5,9},{1... | collective-permute-start | bytes 786440 | tf_op jit(solution)/shard_map/ppermute | solution.py:31
  50.4 6.7 %collective-permute-done.12 = bf16[2,256,256]{2,1,0:T(8,128)(2,1)S(1)} collective-permute-done((bf16[2,256,256]{2,1,0:T(8,128)(2,1)S(1)}, bf16[2,256,256]{2,1,0:T(8,128)(2,1)S(1)}, u32[]{:S(2)}, u32[]{:S(2)}) %collective-permute-start.12) | collective-permute-done | bytes 262176 | tf_op jit(solution)/shard_map/ppermute | solution.py:31
  57.1 0.7 collective-permute-start.14
  57.8 2.4 %collective-permute-start.13 = (bf16[2,256,256]{2,1,0:T(8,128)(2,1)S(1)}, bf16[2,256,256]{2,1,0:T(8,128)(2,1)S(1)}, u32[]{:S(2)}, u32[]{:S(2)}) collective-permute-start(bf16[2,256,256]{2,1,0:T(8,128)(2,1)S(1)} %collective-permute-done.12), channel_id=1, source_target_pairs={{2,0},{15,1},{4,2},{1,3},{6,4},{3,5},{8,6},{5,7},{10,8},{7,9},{12,... | collective-permute-start | bytes 786440 | tf_op jit(solution)/shard_map/ppermute | solution.py:31
  60.2 5.2 %collective-permute-done.18.refs_1_ = bf16[4,256,1024]{2,1,0:T(8,128)(2,1)S(1)} collective-permute-done((bf16[4,256,1024]{2,1,0:T(8,128)(2,1)S(1)}, bf16[4,256,1024]{2,1,0:T(8,128)(2,1)S(1)}, u32[]{:S(2)}, u32[]{:S(2)}) %collective-permute-start.18) | collective-permute-done | bytes 2097184 | tf_op jit(solution)/shard_map/ppermute | solution.py:31
  65.4 0.1 slice.28
  65.4 3.5 %collective-permute-start.20 = (bf16[2,256,1024]{2,1,0:T(8,128)(2,1)S(1)}, bf16[2,256,1024]{2,1,0:T(8,128)(2,1)S(1)}, u32[]{:S(2)}, u32[]{:S(2)}) collective-permute-start(bf16[2,256,1024]{2,1,0:T(8,128)(2,1)S(1)} %slice.28), channel_id=1, source_target_pairs={{16,0},{65,1},{18,2},{67,3},{20,4},{69,5},{22,6},{71,7},{24,8},{73... | collective-permute-start | bytes 3145736 | tf_op jit(solution)/shard_map/ppermute | solution.py:31
  68.9 0.1 slice.29
  69.0 0.1 collective-permute-start.21
  69.1 0.1 pad_maximum_fusion.5.mine
  69.2 0.1 collective-permute-start.15
  69.3 0.1 pad_maximum_fusion.6.far
  69.3 5.9 %collective-permute-start.16 = (bf16[2,2,256,256]{3,2,1,0:T(8,128)(2,1)S(1)}, bf16[2,2,256,256]{3,2,1,0:T(8,128)(2,1)S(1)}, u32[]{:S(2)}, u32[]{:S(2)}) collective-permute-start(bf16[2,2,256,256]{3,2,1,0:T(8,128)(2,1)S(1)} %pad_maximum_fusion.6.far), channel_id=1, source_target_pairs={{1,0},{0,1},{3,2},{2,3},{5,4},{4,5},{7,6},{6,7},{9,8},{8,9},{11,10... | collective-permute-start | bytes 1572872 | tf_op jit(solution)/shard_map/ppermute | solution.py:31
  75.3 1.8 %shard_map.38.single = f32[256,1024]{1,0:T(8,128)S(1)} custom-call(bf16[256,4096]{1,0:T(8,128)(2,1)S(1)} %get-tuple-element.19.row_ref, bf16[4,256,1024]{2,1,0:T(8,128)(2,1)S(1)} %pad_maximum_fusion.refs_0_, bf16[4,256,1024]{2,1,0:T(8,128)(2,1)S(1)} %collective-permute-done.18.refs_1_, bf16[4,256,1024]{2,1,0:T(8,128)(2,1)S(1)} %collective-permute-done.19.refs_2_), custom_call_target="tpu_custom_call" | custom-call | flops 2147483648 | bytes 1048576 | tf_op jit(solution)/shard_map/pallas_call | solution.py:159
  77.1 2.1 %shard_map.39 = (bf16[256,4096]{1,0:T(8,128)(2,1)S(1)}, f32[256,1024]{1,0:T(8,128)S(1)}) custom-call(bf16[2,256,256]{2,1,0:T(8,128)(2,1)S(1)} %pad_maximum_fusion.7.own, bf16[2,2,256,256]{3,2,1,0:T(8,128)(2,1)S(1)} %pad_maximum_fusion.5.mine, bf16[2,2,256,256]{3,2,1,0:T(8,128)(2,1)S(1)} %pad_maximum_fusion.6.far, ...), custom_call_target="tpu_custom_call" | custom-call | flops 2147483648 | bytes 1048576 | tf_op jit(solution)/shard_map/pallas_call | solution.py:159
  79.2 1.4 %collective-permute-done.20.refs_0_ = bf16[2,256,1024]{2,1,0:T(8,128)(2,1)S(1)} collective-permute-done((bf16[2,256,1024]{2,1,0:T(8,128)(2,1)S(1)}, bf16[2,256,1024]{2,1,0:T(8,128)(2,1)S(1)}, u32[]{:S(2)}, u32[]{:S(2)}) %collective-permute-start.20) | collective-permute-done | bytes 1048608 | tf_op jit(solution)/shard_map/ppermute | solution.py:31
  80.7 3.6 %collective-permute-done.21.refs_1_ = bf16[2,256,1024]{2,1,0:T(8,128)(2,1)S(1)} collective-permute-done((bf16[2,256,1024]{2,1,0:T(8,128)(2,1)S(1)}, bf16[2,256,1024]{2,1,0:T(8,128)(2,1)S(1)}, u32[]{:S(2)}, u32[]{:S(2)}) %collective-permute-start.21) | collective-permute-done | bytes 1048608 | tf_op jit(solution)/shard_map/ppermute | solution.py:31
  84.2 2.1 %shard_map.40 = bf16[256,1024]{1,0:T(8,128)(2,1)} custom-call(bf16[256,4096]{1,0:T(8,128)(2,1)S(1)} %get-tuple-element.19.row_ref, bf16[256,4096]{1,0:T(8,128)(2,1)S(1)} %get-tuple-element.24.squared_ref, f32[256,1024]{1,0:T(8,128)S(1)} %get-tuple-element.25.total, bf16[2,256,1024]{2,1,0:T(8,128)(2,1)S(1)} %collective-permute-done.20.refs_0_, ...), custom_call_target="tpu_custom_call" | custom-call | flops 33554432 | bytes 1048576 | tf_op jit(solution)/shard_map/pallas_call | solution.py:159
  (23 shorter events, 0.3 us)
Async XLA Ops:
  0.0 1.9 %copy-start = (bf16[256,2048]{1,0:T(8,128)(2,1)S(1)}, bf16[256,2048]{1,0:T(8,128)(2,1)}, u32[]{:S(2)}) copy-start(bf16[256,2048]{1,0:T(8,128)(2,1)} %param.4) | copy-start | bytes 3145732
  2.1 17.8 %collective-permute-start.3 = (bf16[256,1280]{1,0:T(8,128)(2,1)S(1)}, bf16[256,1280]{1,0:T(8,128)(2,1)S(1)}, u32[]{:S(2)}, u32[]{:S(2)}) collective-permute-start(bf16[256,1280]{1,0:T(8,128)(2,1)S(1)} %pad_maximum_fusion.2), channel_id=1, source_target_pairs={{192,0},{49,1},{194,2},{51,3},{196,4},{53,5},{198,6},{55,7},{200,8... | collective-permute-start | bytes 1966088 | tf_op jit(solution)/shard_map/ppermute | solution.py:31
  4.2 15.7 %collective-permute-start.2 = (bf16[256,1280]{1,0:T(8,128)(2,1)S(1)}, bf16[256,1280]{1,0:T(8,128)(2,1)S(1)}, u32[]{:S(2)}, u32[]{:S(2)}) collective-permute-start(bf16[256,1280]{1,0:T(8,128)(2,1)S(1)} %pad_maximum_fusion.2), channel_id=1, source_target_pairs={{64,0},{17,1},{66,2},{19,3},{68,4},{21,5},{70,6},{23,7},{72,8},{25... | collective-permute-start | bytes 1966088 | tf_op jit(solution)/shard_map/ppermute | solution.py:31
  5.5 9.7 %collective-permute-start = (bf16[256,512]{1,0:T(8,128)(2,1)S(1)}, bf16[256,512]{1,0:T(8,128)(2,1)S(1)}, u32[]{:S(2)}, u32[]{:S(2)}) collective-permute-start(bf16[256,512]{1,0:T(8,128)(2,1)S(1)} %bitcast_multiply_fusion.own), channel_id=1, source_target_pairs={{2,0},{15,1},{4,2},{1,3},{6,4},{3,5},{8,6},{5,7},{10,8},{7,9},{12,... | collective-permute-start | bytes 786440 | tf_op jit(solution)/shard_map/ppermute | solution.py:31
  7.3 12.5 %collective-permute-start.1 = (bf16[256,512]{1,0:T(8,128)(2,1)S(1)}, bf16[256,512]{1,0:T(8,128)(2,1)S(1)}, u32[]{:S(2)}, u32[]{:S(2)}) collective-permute-start(bf16[256,512]{1,0:T(8,128)(2,1)S(1)} %bitcast_multiply_fusion.own), channel_id=1, source_target_pairs={{4,0},{13,1},{6,2},{15,3},{8,4},{1,5},{10,6},{3,7},{12,8},{5,9},{1... | collective-permute-start | bytes 786440 | tf_op jit(solution)/shard_map/ppermute | solution.py:31
  10.3 9.6 %collective-permute-start.4 = (bf16[256,256]{1,0:T(8,128)(2,1)S(1)}, bf16[256,256]{1,0:T(8,128)(2,1)S(1)}, u32[]{:S(2)}, u32[]{:S(2)}) collective-permute-start(bf16[256,256]{1,0:T(8,128)(2,1)S(1)} %constant_dynamic-slice_fusion.1), channel_id=1, source_target_pairs={{128,0},{33,1},{130,2},{35,3},{132,4},{37,5},{134,6},{39,7},{136,8... | collective-permute-start | bytes 393224 | tf_op jit(solution)/shard_map/ppermute | solution.py:31
  15.3 9.8 %collective-permute-start.17 = (bf16[256,1024]{1,0:T(8,128)(2,1)S(1)}, bf16[256,1024]{1,0:T(8,128)(2,1)S(1)}, u32[]{:S(2)}, u32[]{:S(2)}) collective-permute-start(bf16[256,1024]{1,0:T(8,128)(2,1)S(1)} %constant_dynamic-slice_fusion), channel_id=1, source_target_pairs={{128,0},{33,1},{130,2},{35,3},{132,4},{37,5},{134,6},{39,7},{136,8... | collective-permute-start | bytes 1572872 | tf_op jit(solution)/shard_map/ppermute | solution.py:31
  20.0 19.0 %collective-permute-start.6 = (bf16[4,256,256]{2,1,0:T(8,128)(2,1)S(1)}, bf16[4,256,256]{2,1,0:T(8,128)(2,1)S(1)}, u32[]{:S(2)}, u32[]{:S(2)}) collective-permute-start(bf16[4,256,256]{2,1,0:T(8,128)(2,1)S(1)} %pad_maximum_fusion.4.refs_0_), channel_id=1, source_target_pairs={{16,0},{65,1},{18,2},{67,3},{20,4},{69,5},{22,6},{71,7},{24,8},{73... | collective-permute-start | bytes 1572872 | tf_op jit(solution)/shard_map/ppermute | solution.py:31
  22.5 16.4 %collective-permute-start.7 = (bf16[4,256,256]{2,1,0:T(8,128)(2,1)S(1)}, bf16[4,256,256]{2,1,0:T(8,128)(2,1)S(1)}, u32[]{:S(2)}, u32[]{:S(2)}) collective-permute-start(bf16[4,256,256]{2,1,0:T(8,128)(2,1)S(1)} %pad_maximum_fusion.4.refs_0_), channel_id=1, source_target_pairs={{32,0},{129,1},{34,2},{131,3},{36,4},{133,5},{38,6},{135,7},{40,8}... | collective-permute-start | bytes 1572872 | tf_op jit(solution)/shard_map/ppermute | solution.py:31
  22.9 19.5 %collective-permute-start.8 = (bf16[4,256,256]{2,1,0:T(8,128)(2,1)S(1)}, bf16[4,256,256]{2,1,0:T(8,128)(2,1)S(1)}, u32[]{:S(2)}, u32[]{:S(2)}) collective-permute-start(bf16[4,256,256]{2,1,0:T(8,128)(2,1)S(1)} %pad_maximum_fusion.4.refs_0_), channel_id=1, source_target_pairs={{48,0},{193,1},{50,2},{195,3},{52,4},{197,5},{54,6},{199,7},{56,8}... | collective-permute-start | bytes 1572872 | tf_op jit(solution)/shard_map/ppermute | solution.py:31
  23.6 18.8 %collective-permute-start.5 = (bf16[2,256,512]{2,1,0:T(8,128)(2,1)S(1)}, bf16[2,256,512]{2,1,0:T(8,128)(2,1)S(1)}, u32[]{:S(2)}, u32[]{:S(2)}) collective-permute-start(bf16[2,256,512]{2,1,0:T(8,128)(2,1)S(1)} %pad_maximum_fusion.3), channel_id=1, source_target_pairs={{4,0},{13,1},{6,2},{15,3},{8,4},{1,5},{10,6},{3,7},{12,8},{5,9},{1... | collective-permute-start | bytes 1572872 | tf_op jit(solution)/shard_map/ppermute | solution.py:31
  39.0 26.4 %collective-permute-start.18 = (bf16[4,256,1024]{2,1,0:T(8,128)(2,1)S(1)}, bf16[4,256,1024]{2,1,0:T(8,128)(2,1)S(1)}, u32[]{:S(2)}, u32[]{:S(2)}) collective-permute-start(bf16[4,256,1024]{2,1,0:T(8,128)(2,1)S(1)} %pad_maximum_fusion.refs_0_), channel_id=1, source_target_pairs={{16,0},{65,1},{18,2},{67,3},{20,4},{69,5},{22,6},{71,7},{24,8},{73... | collective-permute-start | bytes 6291464 | tf_op jit(solution)/shard_map/ppermute | solution.py:31
  42.4 26.6 %collective-permute-start.19 = (bf16[4,256,1024]{2,1,0:T(8,128)(2,1)S(1)}, bf16[4,256,1024]{2,1,0:T(8,128)(2,1)S(1)}, u32[]{:S(2)}, u32[]{:S(2)}) collective-permute-start(bf16[4,256,1024]{2,1,0:T(8,128)(2,1)S(1)} %pad_maximum_fusion.refs_0_), channel_id=1, source_target_pairs={{48,0},{193,1},{50,2},{195,3},{52,4},{197,5},{54,6},{199,7},{56,8}... | collective-permute-start | bytes 6291464 | tf_op jit(solution)/shard_map/ppermute | solution.py:31
  42.5 2.7 %collective-permute-start.9 = (bf16[4,256,512]{2,1,0:T(8,128)(2,1)S(1)}, bf16[4,256,512]{2,1,0:T(8,128)(2,1)S(1)}, u32[]{:S(2)}, u32[]{:S(2)}) collective-permute-start(bf16[4,256,512]{2,1,0:T(8,128)(2,1)S(1)} %pad_maximum_fusion.1.mine), channel_id=1, source_target_pairs={{1,0},{0,1},{3,2},{2,3},{5,4},{4,5},{7,6},{6,7},{9,8},{8,9},{11,10... | collective-permute-start | bytes 3145736 | tf_op jit(solution)/shard_map/ppermute | solution.py:31
  46.3 1.4 %collective-permute-start.10 = (bf16[256,256]{1,0:T(8,128)(2,1)S(1)}, bf16[256,256]{1,0:T(8,128)(2,1)S(1)}, u32[]{:S(2)}, u32[]{:S(2)}) collective-permute-start(bf16[256,256]{1,0:T(8,128)(2,1)S(1)} %get-tuple-element.20), channel_id=1, source_target_pairs={{1,0},{0,1},{3,2},{2,3},{5,4},{4,5},{7,6},{6,7},{9,8},{8,9},{11,10... | collective-permute-start | bytes 393224 | tf_op jit(solution)/shard_map/ppermute | solution.py:31
  47.8 9.3 %collective-permute-start.12 = (bf16[2,256,256]{2,1,0:T(8,128)(2,1)S(1)}, bf16[2,256,256]{2,1,0:T(8,128)(2,1)S(1)}, u32[]{:S(2)}, u32[]{:S(2)}) collective-permute-start(bf16[2,256,256]{2,1,0:T(8,128)(2,1)S(1)} %pad_maximum_fusion.7.own), channel_id=1, source_target_pairs={{4,0},{13,1},{6,2},{15,3},{8,4},{1,5},{10,6},{3,7},{12,8},{5,9},{1... | collective-permute-start | bytes 786440 | tf_op jit(solution)/shard_map/ppermute | solution.py:31
  50.4 15.0 %collective-permute-start.11 = (bf16[2,256,256]{2,1,0:T(8,128)(2,1)S(1)}, bf16[2,256,256]{2,1,0:T(8,128)(2,1)S(1)}, u32[]{:S(2)}, u32[]{:S(2)}) collective-permute-start(bf16[2,256,256]{2,1,0:T(8,128)(2,1)S(1)} %pad_maximum_fusion.7.own), channel_id=1, source_target_pairs={{2,0},{15,1},{4,2},{1,3},{6,4},{3,5},{8,6},{5,7},{10,8},{7,9},{12,... | collective-permute-start | bytes 786440 | tf_op jit(solution)/shard_map/ppermute | solution.py:31
  57.1 12.2 %collective-permute-start.14 = (bf16[2,256,256]{2,1,0:T(8,128)(2,1)S(1)}, bf16[2,256,256]{2,1,0:T(8,128)(2,1)S(1)}, u32[]{:S(2)}, u32[]{:S(2)}) collective-permute-start(bf16[2,256,256]{2,1,0:T(8,128)(2,1)S(1)} %collective-permute-done.12), channel_id=1, source_target_pairs={{4,0},{6,2},{8,4},{10,6},{12,8},{14,10},{0,12},{2,14},{20,16},{22,... | collective-permute-start | bytes 786440 | tf_op jit(solution)/shard_map/ppermute | solution.py:31
  57.8 11.5 %collective-permute-start.13 = (bf16[2,256,256]{2,1,0:T(8,128)(2,1)S(1)}, bf16[2,256,256]{2,1,0:T(8,128)(2,1)S(1)}, u32[]{:S(2)}, u32[]{:S(2)}) collective-permute-start(bf16[2,256,256]{2,1,0:T(8,128)(2,1)S(1)} %collective-permute-done.12), channel_id=1, source_target_pairs={{2,0},{15,1},{4,2},{1,3},{6,4},{3,5},{8,6},{5,7},{10,8},{7,9},{12,... | collective-permute-start | bytes 786440 | tf_op jit(solution)/shard_map/ppermute | solution.py:31
  65.4 15.2 %collective-permute-start.20 = (bf16[2,256,1024]{2,1,0:T(8,128)(2,1)S(1)}, bf16[2,256,1024]{2,1,0:T(8,128)(2,1)S(1)}, u32[]{:S(2)}, u32[]{:S(2)}) collective-permute-start(bf16[2,256,1024]{2,1,0:T(8,128)(2,1)S(1)} %slice.28), channel_id=1, source_target_pairs={{16,0},{65,1},{18,2},{67,3},{20,4},{69,5},{22,6},{71,7},{24,8},{73... | collective-permute-start | bytes 3145736 | tf_op jit(solution)/shard_map/ppermute | solution.py:31
  69.0 15.2 %collective-permute-start.21 = (bf16[2,256,1024]{2,1,0:T(8,128)(2,1)S(1)}, bf16[2,256,1024]{2,1,0:T(8,128)(2,1)S(1)}, u32[]{:S(2)}, u32[]{:S(2)}) collective-permute-start(bf16[2,256,1024]{2,1,0:T(8,128)(2,1)S(1)} %slice.29), channel_id=1, source_target_pairs={{48,0},{193,1},{50,2},{195,3},{52,4},{197,5},{54,6},{199,7},{56,8}... | collective-permute-start | bytes 3145736 | tf_op jit(solution)/shard_map/ppermute | solution.py:31
  69.2 7.9 %collective-permute-start.15 = (bf16[2,2,256,256]{3,2,1,0:T(8,128)(2,1)S(1)}, bf16[2,2,256,256]{3,2,1,0:T(8,128)(2,1)S(1)}, u32[]{:S(2)}, u32[]{:S(2)}) collective-permute-start(bf16[2,2,256,256]{3,2,1,0:T(8,128)(2,1)S(1)} %pad_maximum_fusion.5.mine), channel_id=1, source_target_pairs={{1,0},{0,1},{3,2},{2,3},{5,4},{4,5},{7,6},{6,7},{9,8},{8,9},{11,10... | collective-permute-start | bytes 1572872 | tf_op jit(solution)/shard_map/ppermute | solution.py:31
  69.3 7.7 %collective-permute-start.16 = (bf16[2,2,256,256]{3,2,1,0:T(8,128)(2,1)S(1)}, bf16[2,2,256,256]{3,2,1,0:T(8,128)(2,1)S(1)}, u32[]{:S(2)}, u32[]{:S(2)}) collective-permute-start(bf16[2,2,256,256]{3,2,1,0:T(8,128)(2,1)S(1)} %pad_maximum_fusion.6.far), channel_id=1, source_target_pairs={{1,0},{0,1},{3,2},{2,3},{5,4},{4,5},{7,6},{6,7},{9,8},{8,9},{11,10... | collective-permute-start | bytes 1572872 | tf_op jit(solution)/shard_map/ppermute | solution.py:31

commit v6 on v5

--- a/solution.py
+++ b/solution.py
@@ -150,7 +150,7 @@
     stacks, (out_ref,) = refs[: len(places)], refs[len(places) :]
     once = contract(row_ref, places, stacks)
     twice = contract(squared_ref, places, stacks)
-    out_ref[...] = (total[...] + (3.0 * once - 2.0 * twice)).astype(BF16)
+    out_ref[...] = (total[...] + (3.0 * once - 2.0 * twice)).astype(out_ref.dtype)
 
 
 def call(kernel, parts, scratch, out_shape, flops, *operands):
@@ -188,7 +188,7 @@
     pair = after(joined([one_on, two_on]), both_one, both_three, columns_two)
     panel_two = first(after(own_panel, one_on), 2)
     near_panel = joined([own_panel, both_one[:, PART:], panel_two, both_three[:, PART:]])
-    columns = [near_columns] + [second(near_columns, e) for e in (1, 2, 3)]
+    columns = [near_columns] + [second(near_columns, e) for e in (1, 3, 2)]
     filtered_mine = jnp.concatenate([pair, along(pair, 2)], 0)
     filtered_mine = after(filtered_mine, *columns[1:])
     filtered_line = (filtered, filtered_mine, swapped(filtered_mine))
@@ -197,7 +197,7 @@
     minus = second(after(near_panel, *columns[1:]), 3)
     row, squared = call(
         square_kernel,
-        [((e, 0), blocks) for e, blocks in enumerate(columns)],
+        [((e, 0), blocks) for e, blocks in zip((0, 1, 3, 2), columns)],
         [],
         (row_bf16, jax.ShapeDtypeStruct((ROWS, PART), BF16)),
         2 * ROWS * DEPTH * PART,
@@ -225,9 +225,10 @@
         swapped(far),
         single,
     )
+    total = call(last_kernel, late[:1], [], panel_f32, flops // 64, row, squared_row, total)
     return call(
         last_kernel,
-        late,
+        late[1:],
         [],
         jax.ShapeDtypeStruct((ROWS, WIDTH), BF16),
         flops // 64,

time: 86.4 us -> 85.9 us (level)
    pallas_call x4 -> x5, Pallas kernels: 7.05 us -> 7.23 us  [call(): pl.pallas_call(functools.partial(kernel, [place for place, _ in parts]),...]
  transfers between devices with their start and end apart: 22 -> 22, of which waited for: 10 -> 11; matrix products, arithmetic and copies ran while one was open for 1% -> 1% of each run, Pallas kernels for 6% -> 7%
where the time goes in v6:
time: 85.9 us; the launch traced here: 85.8 us
  waiting for transfers between devices  42 us (49%)
  starting transfers between devices  33.3 us (39%)
  Pallas kernels  7.23 us (8%)
  other arithmetic  2.42 us (3%)
    ppermute x22, waiting for transfers between devices, moved(): return lax.ppermute(block, AXES, route)  42 us
    ppermute x22, starting transfers between devices, moved(): return lax.ppermute(block, AXES, route)  33.3 us
    pallas_call x5, Pallas kernels, call(): pl.pallas_call(functools.partial(kernel, [place for place, _ in parts]),...  7.23 us
  transfers between devices with their start and end apart: 22, of which 11 were waited for; matrix products, arithmetic and copies ran while one was open for 1% of the time, Pallas kernels for 7%

profile of v6, /device:TPU:1, one launch (start us, length us, event | category | flops | bytes accessed | tf_op | source)
XLA Modules:
  0.0 85.8 jit_solution(13698060314894511994)
XLA Ops:
  0.0 0.8 convert_element_type.3
  0.8 0.1 mul.17
  0.9 1.0 %bitcast_multiply_fusion.own = bf16[256,512]{1,0:T(8,128)(2,1)S(1)} fusion(bf16[256,512]{1,0:T(8,128)(2,1)} %param.3, bf16[32,8,4,128]{3,2,1,0:T(4,128)(2,1)S(1)} %bitcast.27), kind=kLoop, calls=%fused_computation.9 | loop fusion | flops 131072 | bytes 786432 | tf_op jit(solution)/shard_map/mul | solution.py:176
  2.1 2.1 %collective-permute-start.3 = (bf16[256,1280]{1,0:T(8,128)(2,1)S(1)}, bf16[256,1280]{1,0:T(8,128)(2,1)S(1)}, u32[]{:S(2)}, u32[]{:S(2)}) collective-permute-start(bf16[256,1280]{1,0:T(8,128)(2,1)S(1)} %pad_maximum_fusion.2), channel_id=1, source_target_pairs={{192,0},{49,1},{194,2},{51,3},{196,4},{53,5},{198,6},{55,7},{200,8... | collective-permute-start | bytes 1966088 | tf_op jit(solution)/shard_map/ppermute | solution.py:31
  4.2 1.4 %collective-permute-start.2 = (bf16[256,1280]{1,0:T(8,128)(2,1)S(1)}, bf16[256,1280]{1,0:T(8,128)(2,1)S(1)}, u32[]{:S(2)}, u32[]{:S(2)}) collective-permute-start(bf16[256,1280]{1,0:T(8,128)(2,1)S(1)} %pad_maximum_fusion.2), channel_id=1, source_target_pairs={{64,0},{17,1},{66,2},{19,3},{68,4},{21,5},{70,6},{23,7},{72,8},{25... | collective-permute-start | bytes 1966088 | tf_op jit(solution)/shard_map/ppermute | solution.py:31
  5.5 1.7 %collective-permute-start = (bf16[256,512]{1,0:T(8,128)(2,1)S(1)}, bf16[256,512]{1,0:T(8,128)(2,1)S(1)}, u32[]{:S(2)}, u32[]{:S(2)}) collective-permute-start(bf16[256,512]{1,0:T(8,128)(2,1)S(1)} %bitcast_multiply_fusion.own), channel_id=1, source_target_pairs={{2,0},{15,1},{4,2},{1,3},{6,4},{3,5},{8,6},{5,7},{10,8},{7,9},{12,... | collective-permute-start | bytes 786440 | tf_op jit(solution)/shard_map/ppermute | solution.py:31
  7.3 3.0 %collective-permute-start.1 = (bf16[256,512]{1,0:T(8,128)(2,1)S(1)}, bf16[256,512]{1,0:T(8,128)(2,1)S(1)}, u32[]{:S(2)}, u32[]{:S(2)}) collective-permute-start(bf16[256,512]{1,0:T(8,128)(2,1)S(1)} %bitcast_multiply_fusion.own), channel_id=1, source_target_pairs={{4,0},{13,1},{6,2},{15,3},{8,4},{1,5},{10,6},{3,7},{12,8},{5,9},{1... | collective-permute-start | bytes 786440 | tf_op jit(solution)/shard_map/ppermute | solution.py:31
  10.3 1.5 %collective-permute-start.4 = (bf16[256,256]{1,0:T(8,128)(2,1)S(1)}, bf16[256,256]{1,0:T(8,128)(2,1)S(1)}, u32[]{:S(2)}, u32[]{:S(2)}) collective-permute-start(bf16[256,256]{1,0:T(8,128)(2,1)S(1)} %constant_dynamic-slice_fusion.1), channel_id=1, source_target_pairs={{128,0},{33,1},{130,2},{35,3},{132,4},{37,5},{134,6},{39,7},{136,8... | collective-permute-start | bytes 393224 | tf_op jit(solution)/shard_map/ppermute | solution.py:31
  11.9 3.4 %collective-permute-done = bf16[256,512]{1,0:T(8,128)(2,1)S(1)} collective-permute-done((bf16[256,512]{1,0:T(8,128)(2,1)S(1)}, bf16[256,512]{1,0:T(8,128)(2,1)S(1)}, u32[]{:S(2)}, u32[]{:S(2)}) %collective-permute-start) | collective-permute-done | bytes 262176 | tf_op jit(solution)/shard_map/ppermute | solution.py:31
  15.3 1.5 %collective-permute-start.17 = (bf16[256,1024]{1,0:T(8,128)(2,1)S(1)}, bf16[256,1024]{1,0:T(8,128)(2,1)S(1)}, u32[]{:S(2)}, u32[]{:S(2)}) collective-permute-start(bf16[256,1024]{1,0:T(8,128)(2,1)S(1)} %constant_dynamic-slice_fusion), channel_id=1, source_target_pairs={{128,0},{33,1},{130,2},{35,3},{132,4},{37,5},{134,6},{39,7},{136,8... | collective-permute-start | bytes 1572872 | tf_op jit(solution)/shard_map/ppermute | solution.py:31
  16.8 3.0 %collective-permute-done.1 = bf16[256,512]{1,0:T(8,128)(2,1)S(1)} collective-permute-done((bf16[256,512]{1,0:T(8,128)(2,1)S(1)}, bf16[256,512]{1,0:T(8,128)(2,1)S(1)}, u32[]{:S(2)}, u32[]{:S(2)}) %collective-permute-start.1) | collective-permute-done | bytes 262176 | tf_op jit(solution)/shard_map/ppermute | solution.py:31
  19.8 0.1 pad_maximum_fusion.3
  19.9 0.1 pad_maximum_fusion.4.refs_0_
  20.0 2.5 %collective-permute-start.6 = (bf16[4,256,256]{2,1,0:T(8,128)(2,1)S(1)}, bf16[4,256,256]{2,1,0:T(8,128)(2,1)S(1)}, u32[]{:S(2)}, u32[]{:S(2)}) collective-permute-start(bf16[4,256,256]{2,1,0:T(8,128)(2,1)S(1)} %pad_maximum_fusion.4.refs_0_), channel_id=1, source_target_pairs={{16,0},{65,1},{18,2},{67,3},{20,4},{69,5},{22,6},{71,7},{24,8},{73... | collective-permute-start | bytes 1572872 | tf_op jit(solution)/shard_map/ppermute | solution.py:31
  22.5 1.6 %collective-permute-start.8 = (bf16[4,256,256]{2,1,0:T(8,128)(2,1)S(1)}, bf16[4,256,256]{2,1,0:T(8,128)(2,1)S(1)}, u32[]{:S(2)}, u32[]{:S(2)}) collective-permute-start(bf16[4,256,256]{2,1,0:T(8,128)(2,1)S(1)} %pad_maximum_fusion.4.refs_0_), channel_id=1, source_target_pairs={{32,0},{129,1},{34,2},{131,3},{36,4},{133,5},{38,6},{135,7},{40,8}... | collective-permute-start | bytes 1572872 | tf_op jit(solution)/shard_map/ppermute | solution.py:31
  24.2 0.2 collective-permute-start.5
  24.4 0.1 slice_bitcast_fusion
  24.5 0.1 slice_bitcast_fusion.1
  24.5 0.6 collective-permute-done.17
  25.1 0.3 pad_maximum_fusion.refs_0_
  25.4 13.6 %collective-permute-done.6.refs_1_ = bf16[4,256,256]{2,1,0:T(8,128)(2,1)S(1)} collective-permute-done((bf16[4,256,256]{2,1,0:T(8,128)(2,1)S(1)}, bf16[4,256,256]{2,1,0:T(8,128)(2,1)S(1)}, u32[]{:S(2)}, u32[]{:S(2)}) %collective-permute-start.6) | collective-permute-done | bytes 524320 | tf_op jit(solution)/shard_map/ppermute | solution.py:31
  39.0 1.7 %collective-permute-done.7.refs_2_ = bf16[4,256,256]{2,1,0:T(8,128)(2,1)S(1)} collective-permute-done((bf16[4,256,256]{2,1,0:T(8,128)(2,1)S(1)}, bf16[4,256,256]{2,1,0:T(8,128)(2,1)S(1)}, u32[]{:S(2)}, u32[]{:S(2)}) %collective-permute-start.7) | collective-permute-done | bytes 524320 | tf_op jit(solution)/shard_map/ppermute | solution.py:31
  40.7 1.7 %collective-permute-start.18 = (bf16[4,256,1024]{2,1,0:T(8,128)(2,1)S(1)}, bf16[4,256,1024]{2,1,0:T(8,128)(2,1)S(1)}, u32[]{:S(2)}, u32[]{:S(2)}) collective-permute-start(bf16[4,256,1024]{2,1,0:T(8,128)(2,1)S(1)} %pad_maximum_fusion.refs_0_), channel_id=1, source_target_pairs={{16,0},{65,1},{18,2},{67,3},{20,4},{69,5},{22,6},{71,7},{24,8},{73... | collective-permute-start | bytes 6291464 | tf_op jit(solution)/shard_map/ppermute | solution.py:31
  42.4 0.1 pad_maximum_fusion.1.mine
  42.5 1.1 %collective-permute-start.9 = (bf16[4,256,512]{2,1,0:T(8,128)(2,1)S(1)}, bf16[4,256,512]{2,1,0:T(8,128)(2,1)S(1)}, u32[]{:S(2)}, u32[]{:S(2)}) collective-permute-start(bf16[4,256,512]{2,1,0:T(8,128)(2,1)S(1)} %pad_maximum_fusion.1.mine), channel_id=1, source_target_pairs={{1,0},{0,1},{3,2},{2,3},{5,4},{4,5},{7,6},{6,7},{9,8},{8,9},{11,10... | collective-permute-start | bytes 3145736 | tf_op jit(solution)/shard_map/ppermute | solution.py:31
  43.5 2.3 %collective-permute-done.9.other = bf16[4,256,512]{2,1,0:T(8,128)(2,1)S(1)} collective-permute-done((bf16[4,256,512]{2,1,0:T(8,128)(2,1)S(1)}, bf16[4,256,512]{2,1,0:T(8,128)(2,1)S(1)}, u32[]{:S(2)}, u32[]{:S(2)}) %collective-permute-start.9) | collective-permute-done | bytes 1048608 | tf_op jit(solution)/shard_map/ppermute | solution.py:31
  45.8 1.1 %shard_map.37 = (bf16[256,4096]{1,0:T(8,128)(2,1)S(1)}, bf16[256,256]{1,0:T(8,128)(2,1)S(1)}) custom-call(bf16[256,512]{1,0:T(8,128)(2,1)S(1)} %bitcast_multiply_fusion.own, bf16[4,256,512]{2,1,0:T(8,128)(2,1)S(1)} %pad_maximum_fusion.1.mine, bf16[4,256,512]{2,1,0:T(8,128)(2,1)S(1)} %collective-permute-done.9.other, ...), custom_call_target="tpu_custom_call" | custom-call | flops 536870912 | bytes 1048576 | tf_op jit(solution)/shard_map/pallas_call | solution.py:159
  46.9 0.4 collective-permute-start.10
  47.3 1.0 %collective-permute-done.10 = bf16[256,256]{1,0:T(8,128)(2,1)S(1)} collective-permute-done((bf16[256,256]{1,0:T(8,128)(2,1)S(1)}, bf16[256,256]{1,0:T(8,128)(2,1)S(1)}, u32[]{:S(2)}, u32[]{:S(2)}) %collective-permute-start.10) | collective-permute-done | bytes 131104 | tf_op jit(solution)/shard_map/ppermute | solution.py:31
  48.4 2.7 %collective-permute-start.12 = (bf16[2,256,256]{2,1,0:T(8,128)(2,1)S(1)}, bf16[2,256,256]{2,1,0:T(8,128)(2,1)S(1)}, u32[]{:S(2)}, u32[]{:S(2)}) collective-permute-start(bf16[2,256,256]{2,1,0:T(8,128)(2,1)S(1)} %pad_maximum_fusion.7.own), channel_id=1, source_target_pairs={{4,0},{13,1},{6,2},{15,3},{8,4},{1,5},{10,6},{3,7},{12,8},{5,9},{1... | collective-permute-start | bytes 786440 | tf_op jit(solution)/shard_map/ppermute | solution.py:31
  51.0 8.3 %collective-permute-done.12 = bf16[2,256,256]{2,1,0:T(8,128)(2,1)S(1)} collective-permute-done((bf16[2,256,256]{2,1,0:T(8,128)(2,1)S(1)}, bf16[2,256,256]{2,1,0:T(8,128)(2,1)S(1)}, u32[]{:S(2)}, u32[]{:S(2)}) %collective-permute-start.12) | collective-permute-done | bytes 262176 | tf_op jit(solution)/shard_map/ppermute | solution.py:31
  59.3 0.7 collective-permute-start.14
  59.9 0.9 %collective-permute-start.13 = (bf16[2,256,256]{2,1,0:T(8,128)(2,1)S(1)}, bf16[2,256,256]{2,1,0:T(8,128)(2,1)S(1)}, u32[]{:S(2)}, u32[]{:S(2)}) collective-permute-start(bf16[2,256,256]{2,1,0:T(8,128)(2,1)S(1)} %collective-permute-done.12), channel_id=1, source_target_pairs={{2,0},{15,1},{4,2},{1,3},{6,4},{3,5},{8,6},{5,7},{10,8},{7,9},{12,... | collective-permute-start | bytes 786440 | tf_op jit(solution)/shard_map/ppermute | solution.py:31
  60.9 5.0 %collective-permute-done.18.refs_1_ = bf16[4,256,1024]{2,1,0:T(8,128)(2,1)S(1)} collective-permute-done((bf16[4,256,1024]{2,1,0:T(8,128)(2,1)S(1)}, bf16[4,256,1024]{2,1,0:T(8,128)(2,1)S(1)}, u32[]{:S(2)}, u32[]{:S(2)}) %collective-permute-start.18) | collective-permute-done | bytes 2097184 | tf_op jit(solution)/shard_map/ppermute | solution.py:31
  65.8 0.1 slice.28
  65.9 3.0 %collective-permute-start.20 = (bf16[2,256,1024]{2,1,0:T(8,128)(2,1)S(1)}, bf16[2,256,1024]{2,1,0:T(8,128)(2,1)S(1)}, u32[]{:S(2)}, u32[]{:S(2)}) collective-permute-start(bf16[2,256,1024]{2,1,0:T(8,128)(2,1)S(1)} %slice.28), channel_id=1, source_target_pairs={{16,0},{65,1},{18,2},{67,3},{20,4},{69,5},{22,6},{71,7},{24,8},{73... | collective-permute-start | bytes 3145736 | tf_op jit(solution)/shard_map/ppermute | solution.py:31
  68.9 0.1 slice.29
  69.0 0.1 collective-permute-start.21
  69.1 0.1 pad_maximum_fusion.5.mine
  69.2 0.7 collective-permute-start.15
  69.8 0.1 pad_maximum_fusion.6.far
  69.9 6.4 %collective-permute-start.16 = (bf16[2,2,256,256]{3,2,1,0:T(8,128)(2,1)S(1)}, bf16[2,2,256,256]{3,2,1,0:T(8,128)(2,1)S(1)}, u32[]{:S(2)}, u32[]{:S(2)}) collective-permute-start(bf16[2,2,256,256]{3,2,1,0:T(8,128)(2,1)S(1)} %pad_maximum_fusion.6.far), channel_id=1, source_target_pairs={{1,0},{0,1},{3,2},{2,3},{5,4},{4,5},{7,6},{6,7},{9,8},{8,9},{11,10... | collective-permute-start | bytes 1572872 | tf_op jit(solution)/shard_map/ppermute | solution.py:31
  76.3 1.8 %shard_map.38.single = f32[256,1024]{1,0:T(8,128)S(1)} custom-call(bf16[256,4096]{1,0:T(8,128)(2,1)S(1)} %get-tuple-element.19.row_ref, bf16[4,256,1024]{2,1,0:T(8,128)(2,1)S(1)} %pad_maximum_fusion.refs_0_, bf16[4,256,1024]{2,1,0:T(8,128)(2,1)S(1)} %collective-permute-done.18.refs_1_, bf16[4,256,1024]{2,1,0:T(8,128)(2,1)S(1)} %collective-permute-done.19.refs_2_), custom_call_target="tpu_custom_call" | custom-call | flops 2147483648 | bytes 1048576 | tf_op jit(solution)/shard_map/pallas_call | solution.py:159
  78.1 2.1 %shard_map.39 = (bf16[256,4096]{1,0:T(8,128)(2,1)S(1)}, f32[256,1024]{1,0:T(8,128)S(1)}) custom-call(bf16[2,256,256]{2,1,0:T(8,128)(2,1)S(1)} %pad_maximum_fusion.7.own, bf16[2,2,256,256]{3,2,1,0:T(8,128)(2,1)S(1)} %pad_maximum_fusion.5.mine, bf16[2,2,256,256]{3,2,1,0:T(8,128)(2,1)S(1)} %pad_maximum_fusion.6.far, ...), custom_call_target="tpu_custom_call" | custom-call | flops 2147483648 | bytes 1048576 | tf_op jit(solution)/shard_map/pallas_call | solution.py:159
  80.3 0.4 collective-permute-done.20.refs_0_
  80.7 0.7 shard_map.40.total
  81.4 2.8 %collective-permute-done.21.refs_0_ = bf16[2,256,1024]{2,1,0:T(8,128)(2,1)S(1)} collective-permute-done((bf16[2,256,1024]{2,1,0:T(8,128)(2,1)S(1)}, bf16[2,256,1024]{2,1,0:T(8,128)(2,1)S(1)}, u32[]{:S(2)}, u32[]{:S(2)}) %collective-permute-start.21) | collective-permute-done | bytes 1048608 | tf_op jit(solution)/shard_map/ppermute | solution.py:31
  84.2 1.5 %shard_map.41 = bf16[256,1024]{1,0:T(8,128)(2,1)} custom-call(bf16[256,4096]{1,0:T(8,128)(2,1)S(1)} %get-tuple-element.19.row_ref, bf16[256,4096]{1,0:T(8,128)(2,1)S(1)} %get-tuple-element.24.squared_ref, f32[256,1024]{1,0:T(8,128)S(1)} %shard_map.40.total, bf16[2,256,1024]{2,1,0:T(8,128)(2,1)S(1)} %collective-permute-done.21.refs_0_), custom_call_target="tpu_custom_call" | custom-call | flops 33554432 | bytes 1048576 | tf_op jit(solution)/shard_map/pallas_call | solution.py:159
  (24 shorter events, 0.3 us)
Async XLA Ops:
  0.0 1.9 %copy-start = (bf16[256,2048]{1,0:T(8,128)(2,1)S(1)}, bf16[256,2048]{1,0:T(8,128)(2,1)}, u32[]{:S(2)}) copy-start(bf16[256,2048]{1,0:T(8,128)(2,1)} %param.4) | copy-start | bytes 3145732
  2.1 17.8 %collective-permute-start.3 = (bf16[256,1280]{1,0:T(8,128)(2,1)S(1)}, bf16[256,1280]{1,0:T(8,128)(2,1)S(1)}, u32[]{:S(2)}, u32[]{:S(2)}) collective-permute-start(bf16[256,1280]{1,0:T(8,128)(2,1)S(1)} %pad_maximum_fusion.2), channel_id=1, source_target_pairs={{192,0},{49,1},{194,2},{51,3},{196,4},{53,5},{198,6},{55,7},{200,8... | collective-permute-start | bytes 1966088 | tf_op jit(solution)/shard_map/ppermute | solution.py:31
  4.2 15.7 %collective-permute-start.2 = (bf16[256,1280]{1,0:T(8,128)(2,1)S(1)}, bf16[256,1280]{1,0:T(8,128)(2,1)S(1)}, u32[]{:S(2)}, u32[]{:S(2)}) collective-permute-start(bf16[256,1280]{1,0:T(8,128)(2,1)S(1)} %pad_maximum_fusion.2), channel_id=1, source_target_pairs={{64,0},{17,1},{66,2},{19,3},{68,4},{21,5},{70,6},{23,7},{72,8},{25... | collective-permute-start | bytes 1966088 | tf_op jit(solution)/shard_map/ppermute | solution.py:31
  5.5 9.7 %collective-permute-start = (bf16[256,512]{1,0:T(8,128)(2,1)S(1)}, bf16[256,512]{1,0:T(8,128)(2,1)S(1)}, u32[]{:S(2)}, u32[]{:S(2)}) collective-permute-start(bf16[256,512]{1,0:T(8,128)(2,1)S(1)} %bitcast_multiply_fusion.own), channel_id=1, source_target_pairs={{2,0},{15,1},{4,2},{1,3},{6,4},{3,5},{8,6},{5,7},{10,8},{7,9},{12,... | collective-permute-start | bytes 786440 | tf_op jit(solution)/shard_map/ppermute | solution.py:31
  7.3 12.5 %collective-permute-start.1 = (bf16[256,512]{1,0:T(8,128)(2,1)S(1)}, bf16[256,512]{1,0:T(8,128)(2,1)S(1)}, u32[]{:S(2)}, u32[]{:S(2)}) collective-permute-start(bf16[256,512]{1,0:T(8,128)(2,1)S(1)} %bitcast_multiply_fusion.own), channel_id=1, source_target_pairs={{4,0},{13,1},{6,2},{15,3},{8,4},{1,5},{10,6},{3,7},{12,8},{5,9},{1... | collective-permute-start | bytes 786440 | tf_op jit(solution)/shard_map/ppermute | solution.py:31
  10.3 9.6 %collective-permute-start.4 = (bf16[256,256]{1,0:T(8,128)(2,1)S(1)}, bf16[256,256]{1,0:T(8,128)(2,1)S(1)}, u32[]{:S(2)}, u32[]{:S(2)}) collective-permute-start(bf16[256,256]{1,0:T(8,128)(2,1)S(1)} %constant_dynamic-slice_fusion.1), channel_id=1, source_target_pairs={{128,0},{33,1},{130,2},{35,3},{132,4},{37,5},{134,6},{39,7},{136,8... | collective-permute-start | bytes 393224 | tf_op jit(solution)/shard_map/ppermute | solution.py:31
  15.3 9.8 %collective-permute-start.17 = (bf16[256,1024]{1,0:T(8,128)(2,1)S(1)}, bf16[256,1024]{1,0:T(8,128)(2,1)S(1)}, u32[]{:S(2)}, u32[]{:S(2)}) collective-permute-start(bf16[256,1024]{1,0:T(8,128)(2,1)S(1)} %constant_dynamic-slice_fusion), channel_id=1, source_target_pairs={{128,0},{33,1},{130,2},{35,3},{132,4},{37,5},{134,6},{39,7},{136,8... | collective-permute-start | bytes 1572872 | tf_op jit(solution)/shard_map/ppermute | solution.py:31
  20.0 19.0 %collective-permute-start.6 = (bf16[4,256,256]{2,1,0:T(8,128)(2,1)S(1)}, bf16[4,256,256]{2,1,0:T(8,128)(2,1)S(1)}, u32[]{:S(2)}, u32[]{:S(2)}) collective-permute-start(bf16[4,256,256]{2,1,0:T(8,128)(2,1)S(1)} %pad_maximum_fusion.4.refs_0_), channel_id=1, source_target_pairs={{16,0},{65,1},{18,2},{67,3},{20,4},{69,5},{22,6},{71,7},{24,8},{73... | collective-permute-start | bytes 1572872 | tf_op jit(solution)/shard_map/ppermute | solution.py:31
  22.5 18.1 %collective-permute-start.7 = (bf16[4,256,256]{2,1,0:T(8,128)(2,1)S(1)}, bf16[4,256,256]{2,1,0:T(8,128)(2,1)S(1)}, u32[]{:S(2)}, u32[]{:S(2)}) collective-permute-start(bf16[4,256,256]{2,1,0:T(8,128)(2,1)S(1)} %pad_maximum_fusion.4.refs_0_), channel_id=1, source_target_pairs={{48,0},{193,1},{50,2},{195,3},{52,4},{197,5},{54,6},{199,7},{56,8}... | collective-permute-start | bytes 1572872 | tf_op jit(solution)/shard_map/ppermute | solution.py:31
  22.5 19.8 %collective-permute-start.8 = (bf16[4,256,256]{2,1,0:T(8,128)(2,1)S(1)}, bf16[4,256,256]{2,1,0:T(8,128)(2,1)S(1)}, u32[]{:S(2)}, u32[]{:S(2)}) collective-permute-start(bf16[4,256,256]{2,1,0:T(8,128)(2,1)S(1)} %pad_maximum_fusion.4.refs_0_), channel_id=1, source_target_pairs={{32,0},{129,1},{34,2},{131,3},{36,4},{133,5},{38,6},{135,7},{40,8}... | collective-permute-start | bytes 1572872 | tf_op jit(solution)/shard_map/ppermute | solution.py:31
  24.2 18.2 %collective-permute-start.5 = (bf16[2,256,512]{2,1,0:T(8,128)(2,1)S(1)}, bf16[2,256,512]{2,1,0:T(8,128)(2,1)S(1)}, u32[]{:S(2)}, u32[]{:S(2)}) collective-permute-start(bf16[2,256,512]{2,1,0:T(8,128)(2,1)S(1)} %pad_maximum_fusion.3), channel_id=1, source_target_pairs={{4,0},{13,1},{6,2},{15,3},{8,4},{1,5},{10,6},{3,7},{12,8},{5,9},{1... | collective-permute-start | bytes 1572872 | tf_op jit(solution)/shard_map/ppermute | solution.py:31
  40.7 25.2 %collective-permute-start.18 = (bf16[4,256,1024]{2,1,0:T(8,128)(2,1)S(1)}, bf16[4,256,1024]{2,1,0:T(8,128)(2,1)S(1)}, u32[]{:S(2)}, u32[]{:S(2)}) collective-permute-start(bf16[4,256,1024]{2,1,0:T(8,128)(2,1)S(1)} %pad_maximum_fusion.refs_0_), channel_id=1, source_target_pairs={{16,0},{65,1},{18,2},{67,3},{20,4},{69,5},{22,6},{71,7},{24,8},{73... | collective-permute-start | bytes 6291464 | tf_op jit(solution)/shard_map/ppermute | solution.py:31
  42.4 26.6 %collective-permute-start.19 = (bf16[4,256,1024]{2,1,0:T(8,128)(2,1)S(1)}, bf16[4,256,1024]{2,1,0:T(8,128)(2,1)S(1)}, u32[]{:S(2)}, u32[]{:S(2)}) collective-permute-start(bf16[4,256,1024]{2,1,0:T(8,128)(2,1)S(1)} %pad_maximum_fusion.refs_0_), channel_id=1, source_target_pairs={{48,0},{193,1},{50,2},{195,3},{52,4},{197,5},{54,6},{199,7},{56,8}... | collective-permute-start | bytes 6291464 | tf_op jit(solution)/shard_map/ppermute | solution.py:31
  42.5 3.3 %collective-permute-start.9 = (bf16[4,256,512]{2,1,0:T(8,128)(2,1)S(1)}, bf16[4,256,512]{2,1,0:T(8,128)(2,1)S(1)}, u32[]{:S(2)}, u32[]{:S(2)}) collective-permute-start(bf16[4,256,512]{2,1,0:T(8,128)(2,1)S(1)} %pad_maximum_fusion.1.mine), channel_id=1, source_target_pairs={{1,0},{0,1},{3,2},{2,3},{5,4},{4,5},{7,6},{6,7},{9,8},{8,9},{11,10... | collective-permute-start | bytes 3145736 | tf_op jit(solution)/shard_map/ppermute | solution.py:31
  46.9 1.4 %collective-permute-start.10 = (bf16[256,256]{1,0:T(8,128)(2,1)S(1)}, bf16[256,256]{1,0:T(8,128)(2,1)S(1)}, u32[]{:S(2)}, u32[]{:S(2)}) collective-permute-start(bf16[256,256]{1,0:T(8,128)(2,1)S(1)} %get-tuple-element.20), channel_id=1, source_target_pairs={{1,0},{0,1},{3,2},{2,3},{5,4},{4,5},{7,6},{6,7},{9,8},{8,9},{11,10... | collective-permute-start | bytes 393224 | tf_op jit(solution)/shard_map/ppermute | solution.py:31
  48.4 10.9 %collective-permute-start.12 = (bf16[2,256,256]{2,1,0:T(8,128)(2,1)S(1)}, bf16[2,256,256]{2,1,0:T(8,128)(2,1)S(1)}, u32[]{:S(2)}, u32[]{:S(2)}) collective-permute-start(bf16[2,256,256]{2,1,0:T(8,128)(2,1)S(1)} %pad_maximum_fusion.7.own), channel_id=1, source_target_pairs={{4,0},{13,1},{6,2},{15,3},{8,4},{1,5},{10,6},{3,7},{12,8},{5,9},{1... | collective-permute-start | bytes 786440 | tf_op jit(solution)/shard_map/ppermute | solution.py:31
  51.0 14.9 %collective-permute-start.11 = (bf16[2,256,256]{2,1,0:T(8,128)(2,1)S(1)}, bf16[2,256,256]{2,1,0:T(8,128)(2,1)S(1)}, u32[]{:S(2)}, u32[]{:S(2)}) collective-permute-start(bf16[2,256,256]{2,1,0:T(8,128)(2,1)S(1)} %pad_maximum_fusion.7.own), channel_id=1, source_target_pairs={{2,0},{15,1},{4,2},{1,3},{6,4},{3,5},{8,6},{5,7},{10,8},{7,9},{12,... | collective-permute-start | bytes 786440 | tf_op jit(solution)/shard_map/ppermute | solution.py:31
  59.3 10.6 %collective-permute-start.14 = (bf16[2,256,256]{2,1,0:T(8,128)(2,1)S(1)}, bf16[2,256,256]{2,1,0:T(8,128)(2,1)S(1)}, u32[]{:S(2)}, u32[]{:S(2)}) collective-permute-start(bf16[2,256,256]{2,1,0:T(8,128)(2,1)S(1)} %collective-permute-done.12), channel_id=1, source_target_pairs={{4,0},{6,2},{8,4},{10,6},{12,8},{14,10},{0,12},{2,14},{20,16},{22,... | collective-permute-start | bytes 786440 | tf_op jit(solution)/shard_map/ppermute | solution.py:31
  59.9 9.9 %collective-permute-start.13 = (bf16[2,256,256]{2,1,0:T(8,128)(2,1)S(1)}, bf16[2,256,256]{2,1,0:T(8,128)(2,1)S(1)}, u32[]{:S(2)}, u32[]{:S(2)}) collective-permute-start(bf16[2,256,256]{2,1,0:T(8,128)(2,1)S(1)} %collective-permute-done.12), channel_id=1, source_target_pairs={{2,0},{15,1},{4,2},{1,3},{6,4},{3,5},{8,6},{5,7},{10,8},{7,9},{12,... | collective-permute-start | bytes 786440 | tf_op jit(solution)/shard_map/ppermute | solution.py:31
  65.9 14.8 %collective-permute-start.20 = (bf16[2,256,1024]{2,1,0:T(8,128)(2,1)S(1)}, bf16[2,256,1024]{2,1,0:T(8,128)(2,1)S(1)}, u32[]{:S(2)}, u32[]{:S(2)}) collective-permute-start(bf16[2,256,1024]{2,1,0:T(8,128)(2,1)S(1)} %slice.28), channel_id=1, source_target_pairs={{16,0},{65,1},{18,2},{67,3},{20,4},{69,5},{22,6},{71,7},{24,8},{73... | collective-permute-start | bytes 3145736 | tf_op jit(solution)/shard_map/ppermute | solution.py:31
  69.0 15.2 %collective-permute-start.21 = (bf16[2,256,1024]{2,1,0:T(8,128)(2,1)S(1)}, bf16[2,256,1024]{2,1,0:T(8,128)(2,1)S(1)}, u32[]{:S(2)}, u32[]{:S(2)}) collective-permute-start(bf16[2,256,1024]{2,1,0:T(8,128)(2,1)S(1)} %slice.29), channel_id=1, source_target_pairs={{48,0},{193,1},{50,2},{195,3},{52,4},{197,5},{54,6},{199,7},{56,8}... | collective-permute-start | bytes 3145736 | tf_op jit(solution)/shard_map/ppermute | solution.py:31
  69.2 8.9 %collective-permute-start.15 = (bf16[2,2,256,256]{3,2,1,0:T(8,128)(2,1)S(1)}, bf16[2,2,256,256]{3,2,1,0:T(8,128)(2,1)S(1)}, u32[]{:S(2)}, u32[]{:S(2)}) collective-permute-start(bf16[2,2,256,256]{3,2,1,0:T(8,128)(2,1)S(1)} %pad_maximum_fusion.5.mine), channel_id=1, source_target_pairs={{1,0},{0,1},{3,2},{2,3},{5,4},{4,5},{7,6},{6,7},{9,8},{8,9},{11,10... | collective-permute-start | bytes 1572872 | tf_op jit(solution)/shard_map/ppermute | solution.py:31
  69.9 8.2 %collective-permute-start.16 = (bf16[2,2,256,256]{3,2,1,0:T(8,128)(2,1)S(1)}, bf16[2,2,256,256]{3,2,1,0:T(8,128)(2,1)S(1)}, u32[]{:S(2)}, u32[]{:S(2)}) collective-permute-start(bf16[2,2,256,256]{3,2,1,0:T(8,128)(2,1)S(1)} %pad_maximum_fusion.6.far), channel_id=1, source_target_pairs={{1,0},{0,1},{3,2},{2,3},{5,4},{4,5},{7,6},{6,7},{9,8},{8,9},{11,10... | collective-permute-start | bytes 1572872 | tf_op jit(solution)/shard_map/ppermute | solution.py:31

commit v7 on v6

--- a/solution.py
+++ b/solution.py
@@ -222,7 +222,7 @@
         mine,
         far,
         swapped(mine),
-        swapped(far),
+        swapped(after(far, single)),
         single,
     )
     total = call(last_kernel, late[:1], [], panel_f32, flops // 64, row, squared_row, total)

time: 85.9 us -> 85.9 us (level)
  starting transfers between devices: 33.3 us -> 37.1 us
  waiting for transfers between devices: 42 us -> 38.2 us
    ppermute x22, waiting for transfers between devices: 42 us -> 38.2 us  [moved(): return lax.ppermute(block, AXES, route)]
    ppermute x22, starting transfers between devices: 33.3 us -> 37.1 us  [moved(): return lax.ppermute(block, AXES, route)]
where the time goes in v7:
time: 85.9 us; the launch traced here: 85.8 us
  waiting for transfers between devices  38.2 us (44%)
  starting transfers between devices  37.1 us (43%)
  Pallas kernels  7.23 us (8%)
  other arithmetic  2.42 us (3%)
    ppermute x22, waiting for transfers between devices, moved(): return lax.ppermute(block, AXES, route)  38.2 us
    ppermute x22, starting transfers between devices, moved(): return lax.ppermute(block, AXES, route)  37.1 us
    pallas_call x5, Pallas kernels, call(): pl.pallas_call(functools.partial(kernel, [place for place, _ in parts]),...  7.23 us
  transfers between devices with their start and end apart: 22, of which 11 were waited for; matrix products, arithmetic and copies ran while one was open for 1% of the time, Pallas kernels for 7%

profile of v7, /device:TPU:1, one launch (start us, length us, event | category | flops | bytes accessed | tf_op | source)
XLA Modules:
  0.0 85.8 jit_solution(1564140799460162953)
XLA Ops:
  0.0 0.8 convert_element_type.3
  0.8 0.1 mul.17
  0.9 1.0 %bitcast_multiply_fusion.own = bf16[256,512]{1,0:T(8,128)(2,1)S(1)} fusion(bf16[256,512]{1,0:T(8,128)(2,1)} %param.3, bf16[32,8,4,128]{3,2,1,0:T(4,128)(2,1)S(1)} %bitcast.27), kind=kLoop, calls=%fused_computation.9 | loop fusion | flops 131072 | bytes 786432 | tf_op jit(solution)/shard_map/mul | solution.py:176
  2.1 2.1 %collective-permute-start.3 = (bf16[256,1280]{1,0:T(8,128)(2,1)S(1)}, bf16[256,1280]{1,0:T(8,128)(2,1)S(1)}, u32[]{:S(2)}, u32[]{:S(2)}) collective-permute-start(bf16[256,1280]{1,0:T(8,128)(2,1)S(1)} %pad_maximum_fusion.2), channel_id=1, source_target_pairs={{192,0},{49,1},{194,2},{51,3},{196,4},{53,5},{198,6},{55,7},{200,8... | collective-permute-start | bytes 1966088 | tf_op jit(solution)/shard_map/ppermute | solution.py:31
  4.2 1.4 %collective-permute-start.2 = (bf16[256,1280]{1,0:T(8,128)(2,1)S(1)}, bf16[256,1280]{1,0:T(8,128)(2,1)S(1)}, u32[]{:S(2)}, u32[]{:S(2)}) collective-permute-start(bf16[256,1280]{1,0:T(8,128)(2,1)S(1)} %pad_maximum_fusion.2), channel_id=1, source_target_pairs={{64,0},{17,1},{66,2},{19,3},{68,4},{21,5},{70,6},{23,7},{72,8},{25... | collective-permute-start | bytes 1966088 | tf_op jit(solution)/shard_map/ppermute | solution.py:31
  5.5 1.7 %collective-permute-start = (bf16[256,512]{1,0:T(8,128)(2,1)S(1)}, bf16[256,512]{1,0:T(8,128)(2,1)S(1)}, u32[]{:S(2)}, u32[]{:S(2)}) collective-permute-start(bf16[256,512]{1,0:T(8,128)(2,1)S(1)} %bitcast_multiply_fusion.own), channel_id=1, source_target_pairs={{2,0},{15,1},{4,2},{1,3},{6,4},{3,5},{8,6},{5,7},{10,8},{7,9},{12,... | collective-permute-start | bytes 786440 | tf_op jit(solution)/shard_map/ppermute | solution.py:31
  7.3 3.0 %collective-permute-start.1 = (bf16[256,512]{1,0:T(8,128)(2,1)S(1)}, bf16[256,512]{1,0:T(8,128)(2,1)S(1)}, u32[]{:S(2)}, u32[]{:S(2)}) collective-permute-start(bf16[256,512]{1,0:T(8,128)(2,1)S(1)} %bitcast_multiply_fusion.own), channel_id=1, source_target_pairs={{4,0},{13,1},{6,2},{15,3},{8,4},{1,5},{10,6},{3,7},{12,8},{5,9},{1... | collective-permute-start | bytes 786440 | tf_op jit(solution)/shard_map/ppermute | solution.py:31
  10.3 1.5 %collective-permute-start.4 = (bf16[256,256]{1,0:T(8,128)(2,1)S(1)}, bf16[256,256]{1,0:T(8,128)(2,1)S(1)}, u32[]{:S(2)}, u32[]{:S(2)}) collective-permute-start(bf16[256,256]{1,0:T(8,128)(2,1)S(1)} %constant_dynamic-slice_fusion.1), channel_id=1, source_target_pairs={{128,0},{33,1},{130,2},{35,3},{132,4},{37,5},{134,6},{39,7},{136,8... | collective-permute-start | bytes 393224 | tf_op jit(solution)/shard_map/ppermute | solution.py:31
  11.9 3.4 %collective-permute-done = bf16[256,512]{1,0:T(8,128)(2,1)S(1)} collective-permute-done((bf16[256,512]{1,0:T(8,128)(2,1)S(1)}, bf16[256,512]{1,0:T(8,128)(2,1)S(1)}, u32[]{:S(2)}, u32[]{:S(2)}) %collective-permute-start) | collective-permute-done | bytes 262176 | tf_op jit(solution)/shard_map/ppermute | solution.py:31
  15.3 1.5 %collective-permute-start.16 = (bf16[256,1024]{1,0:T(8,128)(2,1)S(1)}, bf16[256,1024]{1,0:T(8,128)(2,1)S(1)}, u32[]{:S(2)}, u32[]{:S(2)}) collective-permute-start(bf16[256,1024]{1,0:T(8,128)(2,1)S(1)} %constant_dynamic-slice_fusion), channel_id=1, source_target_pairs={{128,0},{33,1},{130,2},{35,3},{132,4},{37,5},{134,6},{39,7},{136,8... | collective-permute-start | bytes 1572872 | tf_op jit(solution)/shard_map/ppermute | solution.py:31
  16.8 3.0 %collective-permute-done.1 = bf16[256,512]{1,0:T(8,128)(2,1)S(1)} collective-permute-done((bf16[256,512]{1,0:T(8,128)(2,1)S(1)}, bf16[256,512]{1,0:T(8,128)(2,1)S(1)}, u32[]{:S(2)}, u32[]{:S(2)}) %collective-permute-start.1) | collective-permute-done | bytes 262176 | tf_op jit(solution)/shard_map/ppermute | solution.py:31
  19.8 0.1 pad_maximum_fusion.3
  19.9 0.1 pad_maximum_fusion.4.refs_0_
  20.0 2.5 %collective-permute-start.6 = (bf16[4,256,256]{2,1,0:T(8,128)(2,1)S(1)}, bf16[4,256,256]{2,1,0:T(8,128)(2,1)S(1)}, u32[]{:S(2)}, u32[]{:S(2)}) collective-permute-start(bf16[4,256,256]{2,1,0:T(8,128)(2,1)S(1)} %pad_maximum_fusion.4.refs_0_), channel_id=1, source_target_pairs={{16,0},{65,1},{18,2},{67,3},{20,4},{69,5},{22,6},{71,7},{24,8},{73... | collective-permute-start | bytes 1572872 | tf_op jit(solution)/shard_map/ppermute | solution.py:31
  22.5 1.6 %collective-permute-start.8 = (bf16[4,256,256]{2,1,0:T(8,128)(2,1)S(1)}, bf16[4,256,256]{2,1,0:T(8,128)(2,1)S(1)}, u32[]{:S(2)}, u32[]{:S(2)}) collective-permute-start(bf16[4,256,256]{2,1,0:T(8,128)(2,1)S(1)} %pad_maximum_fusion.4.refs_0_), channel_id=1, source_target_pairs={{32,0},{129,1},{34,2},{131,3},{36,4},{133,5},{38,6},{135,7},{40,8}... | collective-permute-start | bytes 1572872 | tf_op jit(solution)/shard_map/ppermute | solution.py:31
  24.2 0.2 collective-permute-start.5
  24.4 0.1 slice_bitcast_fusion
  24.5 0.1 slice_bitcast_fusion.1
  24.5 0.6 collective-permute-done.16
  25.1 0.3 pad_maximum_fusion.refs_0_
  25.4 13.6 %collective-permute-done.6.refs_1_ = bf16[4,256,256]{2,1,0:T(8,128)(2,1)S(1)} collective-permute-done((bf16[4,256,256]{2,1,0:T(8,128)(2,1)S(1)}, bf16[4,256,256]{2,1,0:T(8,128)(2,1)S(1)}, u32[]{:S(2)}, u32[]{:S(2)}) %collective-permute-start.6) | collective-permute-done | bytes 524320 | tf_op jit(solution)/shard_map/ppermute | solution.py:31
  39.0 1.7 %collective-permute-done.7.refs_2_ = bf16[4,256,256]{2,1,0:T(8,128)(2,1)S(1)} collective-permute-done((bf16[4,256,256]{2,1,0:T(8,128)(2,1)S(1)}, bf16[4,256,256]{2,1,0:T(8,128)(2,1)S(1)}, u32[]{:S(2)}, u32[]{:S(2)}) %collective-permute-start.7) | collective-permute-done | bytes 524320 | tf_op jit(solution)/shard_map/ppermute | solution.py:31
  40.7 1.7 %collective-permute-start.17 = (bf16[4,256,1024]{2,1,0:T(8,128)(2,1)S(1)}, bf16[4,256,1024]{2,1,0:T(8,128)(2,1)S(1)}, u32[]{:S(2)}, u32[]{:S(2)}) collective-permute-start(bf16[4,256,1024]{2,1,0:T(8,128)(2,1)S(1)} %pad_maximum_fusion.refs_0_), channel_id=1, source_target_pairs={{16,0},{65,1},{18,2},{67,3},{20,4},{69,5},{22,6},{71,7},{24,8},{73... | collective-permute-start | bytes 6291464 | tf_op jit(solution)/shard_map/ppermute | solution.py:31
  42.4 0.1 pad_maximum_fusion.1.mine
  42.5 1.1 %collective-permute-start.9 = (bf16[4,256,512]{2,1,0:T(8,128)(2,1)S(1)}, bf16[4,256,512]{2,1,0:T(8,128)(2,1)S(1)}, u32[]{:S(2)}, u32[]{:S(2)}) collective-permute-start(bf16[4,256,512]{2,1,0:T(8,128)(2,1)S(1)} %pad_maximum_fusion.1.mine), channel_id=1, source_target_pairs={{1,0},{0,1},{3,2},{2,3},{5,4},{4,5},{7,6},{6,7},{9,8},{8,9},{11,10... | collective-permute-start | bytes 3145736 | tf_op jit(solution)/shard_map/ppermute | solution.py:31
  43.5 2.3 %collective-permute-done.9.other = bf16[4,256,512]{2,1,0:T(8,128)(2,1)S(1)} collective-permute-done((bf16[4,256,512]{2,1,0:T(8,128)(2,1)S(1)}, bf16[4,256,512]{2,1,0:T(8,128)(2,1)S(1)}, u32[]{:S(2)}, u32[]{:S(2)}) %collective-permute-start.9) | collective-permute-done | bytes 1048608 | tf_op jit(solution)/shard_map/ppermute | solution.py:31
  45.8 1.1 %shard_map.37 = (bf16[256,4096]{1,0:T(8,128)(2,1)S(1)}, bf16[256,256]{1,0:T(8,128)(2,1)S(1)}) custom-call(bf16[256,512]{1,0:T(8,128)(2,1)S(1)} %bitcast_multiply_fusion.own, bf16[4,256,512]{2,1,0:T(8,128)(2,1)S(1)} %pad_maximum_fusion.1.mine, bf16[4,256,512]{2,1,0:T(8,128)(2,1)S(1)} %collective-permute-done.9.other, ...), custom_call_target="tpu_custom_call" | custom-call | flops 536870912 | bytes 1048576 | tf_op jit(solution)/shard_map/pallas_call | solution.py:159
  46.9 0.4 collective-permute-start.10
  47.3 1.0 %collective-permute-done.10 = bf16[256,256]{1,0:T(8,128)(2,1)S(1)} collective-permute-done((bf16[256,256]{1,0:T(8,128)(2,1)S(1)}, bf16[256,256]{1,0:T(8,128)(2,1)S(1)}, u32[]{:S(2)}, u32[]{:S(2)}) %collective-permute-start.10) | collective-permute-done | bytes 131104 | tf_op jit(solution)/shard_map/ppermute | solution.py:31
  48.4 2.7 %collective-permute-start.12 = (bf16[2,256,256]{2,1,0:T(8,128)(2,1)S(1)}, bf16[2,256,256]{2,1,0:T(8,128)(2,1)S(1)}, u32[]{:S(2)}, u32[]{:S(2)}) collective-permute-start(bf16[2,256,256]{2,1,0:T(8,128)(2,1)S(1)} %pad_maximum_fusion.7.own), channel_id=1, source_target_pairs={{4,0},{13,1},{6,2},{15,3},{8,4},{1,5},{10,6},{3,7},{12,8},{5,9},{1... | collective-permute-start | bytes 786440 | tf_op jit(solution)/shard_map/ppermute | solution.py:31
  51.0 8.3 %collective-permute-done.12 = bf16[2,256,256]{2,1,0:T(8,128)(2,1)S(1)} collective-permute-done((bf16[2,256,256]{2,1,0:T(8,128)(2,1)S(1)}, bf16[2,256,256]{2,1,0:T(8,128)(2,1)S(1)}, u32[]{:S(2)}, u32[]{:S(2)}) %collective-permute-start.12) | collective-permute-done | bytes 262176 | tf_op jit(solution)/shard_map/ppermute | solution.py:31
  59.3 0.7 collective-permute-start.14
  59.9 0.9 %collective-permute-start.13 = (bf16[2,256,256]{2,1,0:T(8,128)(2,1)S(1)}, bf16[2,256,256]{2,1,0:T(8,128)(2,1)S(1)}, u32[]{:S(2)}, u32[]{:S(2)}) collective-permute-start(bf16[2,256,256]{2,1,0:T(8,128)(2,1)S(1)} %collective-permute-done.12), channel_id=1, source_target_pairs={{2,0},{15,1},{4,2},{1,3},{6,4},{3,5},{8,6},{5,7},{10,8},{7,9},{12,... | collective-permute-start | bytes 786440 | tf_op jit(solution)/shard_map/ppermute | solution.py:31
  60.9 1.2 %collective-permute-done.11 = bf16[2,256,256]{2,1,0:T(8,128)(2,1)S(1)} collective-permute-done((bf16[2,256,256]{2,1,0:T(8,128)(2,1)S(1)}, bf16[2,256,256]{2,1,0:T(8,128)(2,1)S(1)}, u32[]{:S(2)}, u32[]{:S(2)}) %collective-permute-start.11) | collective-permute-done | bytes 262176 | tf_op jit(solution)/shard_map/ppermute | solution.py:31
  62.0 0.1 pad_maximum_fusion.5.mine
  62.1 4.1 %collective-permute-start.15 = (bf16[2,2,256,256]{3,2,1,0:T(8,128)(2,1)S(1)}, bf16[2,2,256,256]{3,2,1,0:T(8,128)(2,1)S(1)}, u32[]{:S(2)}, u32[]{:S(2)}) collective-permute-start(bf16[2,2,256,256]{3,2,1,0:T(8,128)(2,1)S(1)} %pad_maximum_fusion.5.mine), channel_id=1, source_target_pairs={{1,0},{0,1},{3,2},{2,3},{5,4},{4,5},{7,6},{6,7},{9,8},{8,9},{11,10... | collective-permute-start | bytes 1572872 | tf_op jit(solution)/shard_map/ppermute | solution.py:31
  66.2 0.1 slice.28
  66.2 2.7 %collective-permute-start.20 = (bf16[2,256,1024]{2,1,0:T(8,128)(2,1)S(1)}, bf16[2,256,1024]{2,1,0:T(8,128)(2,1)S(1)}, u32[]{:S(2)}, u32[]{:S(2)}) collective-permute-start(bf16[2,256,1024]{2,1,0:T(8,128)(2,1)S(1)} %slice.28), channel_id=1, source_target_pairs={{16,0},{65,1},{18,2},{67,3},{20,4},{69,5},{22,6},{71,7},{24,8},{73... | collective-permute-start | bytes 3145736 | tf_op jit(solution)/shard_map/ppermute | solution.py:31
  68.9 0.1 slice.29
  69.0 0.1 collective-permute-start.21
  69.1 0.1 pad_maximum_fusion.6.far
  69.2 1.8 %shard_map.38.single = f32[256,1024]{1,0:T(8,128)S(1)} custom-call(bf16[256,4096]{1,0:T(8,128)(2,1)S(1)} %get-tuple-element.20.row_ref, bf16[4,256,1024]{2,1,0:T(8,128)(2,1)S(1)} %pad_maximum_fusion.refs_0_, bf16[4,256,1024]{2,1,0:T(8,128)(2,1)S(1)} %collective-permute-done.17.refs_1_, bf16[4,256,1024]{2,1,0:T(8,128)(2,1)S(1)} %collective-permute-done.18.refs_2_), custom_call_target="tpu_custom_call" | custom-call | flops 2147483648 | bytes 1048576 | tf_op jit(solution)/shard_map/pallas_call | solution.py:159
  71.0 7.1 %collective-permute-start.19 = (bf16[2,2,256,256]{3,2,1,0:T(8,128)(2,1)S(1)}, bf16[2,2,256,256]{3,2,1,0:T(8,128)(2,1)S(1)}, u32[]{:S(2)}, u32[]{:S(2)}) collective-permute-start(bf16[2,2,256,256]{3,2,1,0:T(8,128)(2,1)S(1)} %pad_maximum_fusion.6.far), channel_id=1, source_target_pairs={{1,0},{0,1},{3,2},{2,3},{5,4},{4,5},{7,6},{6,7},{9,8},{8,9},{11,10... | collective-permute-start | bytes 1572872 | tf_op jit(solution)/shard_map/ppermute | solution.py:31
  78.1 1.5 %collective-permute-done.19.other_far = bf16[2,2,256,256]{3,2,1,0:T(8,128)(2,1)S(1)} collective-permute-done((bf16[2,2,256,256]{3,2,1,0:T(8,128)(2,1)S(1)}, bf16[2,2,256,256]{3,2,1,0:T(8,128)(2,1)S(1)}, u32[]{:S(2)}, u32[]{:S(2)}) %collective-permute-start.19) | collective-permute-done | bytes 524320 | tf_op jit(solution)/shard_map/ppermute | solution.py:31
  79.6 2.1 %shard_map.39 = (bf16[256,4096]{1,0:T(8,128)(2,1)S(1)}, f32[256,1024]{1,0:T(8,128)S(1)}) custom-call(bf16[2,256,256]{2,1,0:T(8,128)(2,1)S(1)} %pad_maximum_fusion.7.own, bf16[2,2,256,256]{3,2,1,0:T(8,128)(2,1)S(1)} %pad_maximum_fusion.5.mine, bf16[2,2,256,256]{3,2,1,0:T(8,128)(2,1)S(1)} %pad_maximum_fusion.6.far, ...), custom_call_target="tpu_custom_call" | custom-call | flops 2147483648 | bytes 1048576 | tf_op jit(solution)/shard_map/pallas_call | solution.py:159
  81.8 0.7 shard_map.40.total
  82.5 1.7 %collective-permute-done.21.refs_0_ = bf16[2,256,1024]{2,1,0:T(8,128)(2,1)S(1)} collective-permute-done((bf16[2,256,1024]{2,1,0:T(8,128)(2,1)S(1)}, bf16[2,256,1024]{2,1,0:T(8,128)(2,1)S(1)}, u32[]{:S(2)}, u32[]{:S(2)}) %collective-permute-start.21) | collective-permute-done | bytes 1048608 | tf_op jit(solution)/shard_map/ppermute | solution.py:31
  84.2 1.5 %shard_map.41 = bf16[256,1024]{1,0:T(8,128)(2,1)} custom-call(bf16[256,4096]{1,0:T(8,128)(2,1)S(1)} %get-tuple-element.20.row_ref, bf16[256,4096]{1,0:T(8,128)(2,1)S(1)} %get-tuple-element.26.squared_ref, f32[256,1024]{1,0:T(8,128)S(1)} %shard_map.40.total, bf16[2,256,1024]{2,1,0:T(8,128)(2,1)S(1)} %collective-permute-done.21.refs_0_), custom_call_target="tpu_custom_call" | custom-call | flops 33554432 | bytes 1048576 | tf_op jit(solution)/shard_map/pallas_call | solution.py:159
  (24 shorter events, 0.3 us)
Async XLA Ops:
  0.0 1.9 %copy-start = (bf16[256,2048]{1,0:T(8,128)(2,1)S(1)}, bf16[256,2048]{1,0:T(8,128)(2,1)}, u32[]{:S(2)}) copy-start(bf16[256,2048]{1,0:T(8,128)(2,1)} %param.4) | copy-start | bytes 3145732
  2.1 17.8 %collective-permute-start.3 = (bf16[256,1280]{1,0:T(8,128)(2,1)S(1)}, bf16[256,1280]{1,0:T(8,128)(2,1)S(1)}, u32[]{:S(2)}, u32[]{:S(2)}) collective-permute-start(bf16[256,1280]{1,0:T(8,128)(2,1)S(1)} %pad_maximum_fusion.2), channel_id=1, source_target_pairs={{192,0},{49,1},{194,2},{51,3},{196,4},{53,5},{198,6},{55,7},{200,8... | collective-permute-start | bytes 1966088 | tf_op jit(solution)/shard_map/ppermute | solution.py:31
  4.2 15.7 %collective-permute-start.2 = (bf16[256,1280]{1,0:T(8,128)(2,1)S(1)}, bf16[256,1280]{1,0:T(8,128)(2,1)S(1)}, u32[]{:S(2)}, u32[]{:S(2)}) collective-permute-start(bf16[256,1280]{1,0:T(8,128)(2,1)S(1)} %pad_maximum_fusion.2), channel_id=1, source_target_pairs={{64,0},{17,1},{66,2},{19,3},{68,4},{21,5},{70,6},{23,7},{72,8},{25... | collective-permute-start | bytes 1966088 | tf_op jit(solution)/shard_map/ppermute | solution.py:31
  5.5 9.7 %collective-permute-start = (bf16[256,512]{1,0:T(8,128)(2,1)S(1)}, bf16[256,512]{1,0:T(8,128)(2,1)S(1)}, u32[]{:S(2)}, u32[]{:S(2)}) collective-permute-start(bf16[256,512]{1,0:T(8,128)(2,1)S(1)} %bitcast_multiply_fusion.own), channel_id=1, source_target_pairs={{2,0},{15,1},{4,2},{1,3},{6,4},{3,5},{8,6},{5,7},{10,8},{7,9},{12,... | collective-permute-start | bytes 786440 | tf_op jit(solution)/shard_map/ppermute | solution.py:31
  7.3 12.5 %collective-permute-start.1 = (bf16[256,512]{1,0:T(8,128)(2,1)S(1)}, bf16[256,512]{1,0:T(8,128)(2,1)S(1)}, u32[]{:S(2)}, u32[]{:S(2)}) collective-permute-start(bf16[256,512]{1,0:T(8,128)(2,1)S(1)} %bitcast_multiply_fusion.own), channel_id=1, source_target_pairs={{4,0},{13,1},{6,2},{15,3},{8,4},{1,5},{10,6},{3,7},{12,8},{5,9},{1... | collective-permute-start | bytes 786440 | tf_op jit(solution)/shard_map/ppermute | solution.py:31
  10.3 9.6 %collective-permute-start.4 = (bf16[256,256]{1,0:T(8,128)(2,1)S(1)}, bf16[256,256]{1,0:T(8,128)(2,1)S(1)}, u32[]{:S(2)}, u32[]{:S(2)}) collective-permute-start(bf16[256,256]{1,0:T(8,128)(2,1)S(1)} %constant_dynamic-slice_fusion.1), channel_id=1, source_target_pairs={{128,0},{33,1},{130,2},{35,3},{132,4},{37,5},{134,6},{39,7},{136,8... | collective-permute-start | bytes 393224 | tf_op jit(solution)/shard_map/ppermute | solution.py:31
  15.3 9.8 %collective-permute-start.16 = (bf16[256,1024]{1,0:T(8,128)(2,1)S(1)}, bf16[256,1024]{1,0:T(8,128)(2,1)S(1)}, u32[]{:S(2)}, u32[]{:S(2)}) collective-permute-start(bf16[256,1024]{1,0:T(8,128)(2,1)S(1)} %constant_dynamic-slice_fusion), channel_id=1, source_target_pairs={{128,0},{33,1},{130,2},{35,3},{132,4},{37,5},{134,6},{39,7},{136,8... | collective-permute-start | bytes 1572872 | tf_op jit(solution)/shard_map/ppermute | solution.py:31
  20.0 19.0 %collective-permute-start.6 = (bf16[4,256,256]{2,1,0:T(8,128)(2,1)S(1)}, bf16[4,256,256]{2,1,0:T(8,128)(2,1)S(1)}, u32[]{:S(2)}, u32[]{:S(2)}) collective-permute-start(bf16[4,256,256]{2,1,0:T(8,128)(2,1)S(1)} %pad_maximum_fusion.4.refs_0_), channel_id=1, source_target_pairs={{16,0},{65,1},{18,2},{67,3},{20,4},{69,5},{22,6},{71,7},{24,8},{73... | collective-permute-start | bytes 1572872 | tf_op jit(solution)/shard_map/ppermute | solution.py:31
  22.5 18.1 %collective-permute-start.7 = (bf16[4,256,256]{2,1,0:T(8,128)(2,1)S(1)}, bf16[4,256,256]{2,1,0:T(8,128)(2,1)S(1)}, u32[]{:S(2)}, u32[]{:S(2)}) collective-permute-start(bf16[4,256,256]{2,1,0:T(8,128)(2,1)S(1)} %pad_maximum_fusion.4.refs_0_), channel_id=1, source_target_pairs={{48,0},{193,1},{50,2},{195,3},{52,4},{197,5},{54,6},{199,7},{56,8}... | collective-permute-start | bytes 1572872 | tf_op jit(solution)/shard_map/ppermute | solution.py:31
  22.5 19.8 %collective-permute-start.8 = (bf16[4,256,256]{2,1,0:T(8,128)(2,1)S(1)}, bf16[4,256,256]{2,1,0:T(8,128)(2,1)S(1)}, u32[]{:S(2)}, u32[]{:S(2)}) collective-permute-start(bf16[4,256,256]{2,1,0:T(8,128)(2,1)S(1)} %pad_maximum_fusion.4.refs_0_), channel_id=1, source_target_pairs={{32,0},{129,1},{34,2},{131,3},{36,4},{133,5},{38,6},{135,7},{40,8}... | collective-permute-start | bytes 1572872 | tf_op jit(solution)/shard_map/ppermute | solution.py:31
  24.2 18.2 %collective-permute-start.5 = (bf16[2,256,512]{2,1,0:T(8,128)(2,1)S(1)}, bf16[2,256,512]{2,1,0:T(8,128)(2,1)S(1)}, u32[]{:S(2)}, u32[]{:S(2)}) collective-permute-start(bf16[2,256,512]{2,1,0:T(8,128)(2,1)S(1)} %pad_maximum_fusion.3), channel_id=1, source_target_pairs={{4,0},{13,1},{6,2},{15,3},{8,4},{1,5},{10,6},{3,7},{12,8},{5,9},{1... | collective-permute-start | bytes 1572872 | tf_op jit(solution)/shard_map/ppermute | solution.py:31
  40.7 25.5 %collective-permute-start.17 = (bf16[4,256,1024]{2,1,0:T(8,128)(2,1)S(1)}, bf16[4,256,1024]{2,1,0:T(8,128)(2,1)S(1)}, u32[]{:S(2)}, u32[]{:S(2)}) collective-permute-start(bf16[4,256,1024]{2,1,0:T(8,128)(2,1)S(1)} %pad_maximum_fusion.refs_0_), channel_id=1, source_target_pairs={{16,0},{65,1},{18,2},{67,3},{20,4},{69,5},{22,6},{71,7},{24,8},{73... | collective-permute-start | bytes 6291464 | tf_op jit(solution)/shard_map/ppermute | solution.py:31
  42.4 26.5 %collective-permute-start.18 = (bf16[4,256,1024]{2,1,0:T(8,128)(2,1)S(1)}, bf16[4,256,1024]{2,1,0:T(8,128)(2,1)S(1)}, u32[]{:S(2)}, u32[]{:S(2)}) collective-permute-start(bf16[4,256,1024]{2,1,0:T(8,128)(2,1)S(1)} %pad_maximum_fusion.refs_0_), channel_id=1, source_target_pairs={{48,0},{193,1},{50,2},{195,3},{52,4},{197,5},{54,6},{199,7},{56,8}... | collective-permute-start | bytes 6291464 | tf_op jit(solution)/shard_map/ppermute | solution.py:31
  42.5 3.3 %collective-permute-start.9 = (bf16[4,256,512]{2,1,0:T(8,128)(2,1)S(1)}, bf16[4,256,512]{2,1,0:T(8,128)(2,1)S(1)}, u32[]{:S(2)}, u32[]{:S(2)}) collective-permute-start(bf16[4,256,512]{2,1,0:T(8,128)(2,1)S(1)} %pad_maximum_fusion.1.mine), channel_id=1, source_target_pairs={{1,0},{0,1},{3,2},{2,3},{5,4},{4,5},{7,6},{6,7},{9,8},{8,9},{11,10... | collective-permute-start | bytes 3145736 | tf_op jit(solution)/shard_map/ppermute | solution.py:31
  46.9 1.4 %collective-permute-start.10 = (bf16[256,256]{1,0:T(8,128)(2,1)S(1)}, bf16[256,256]{1,0:T(8,128)(2,1)S(1)}, u32[]{:S(2)}, u32[]{:S(2)}) collective-permute-start(bf16[256,256]{1,0:T(8,128)(2,1)S(1)} %get-tuple-element.21), channel_id=1, source_target_pairs={{1,0},{0,1},{3,2},{2,3},{5,4},{4,5},{7,6},{6,7},{9,8},{8,9},{11,10... | collective-permute-start | bytes 393224 | tf_op jit(solution)/shard_map/ppermute | solution.py:31
  48.4 10.9 %collective-permute-start.12 = (bf16[2,256,256]{2,1,0:T(8,128)(2,1)S(1)}, bf16[2,256,256]{2,1,0:T(8,128)(2,1)S(1)}, u32[]{:S(2)}, u32[]{:S(2)}) collective-permute-start(bf16[2,256,256]{2,1,0:T(8,128)(2,1)S(1)} %pad_maximum_fusion.7.own), channel_id=1, source_target_pairs={{4,0},{13,1},{6,2},{15,3},{8,4},{1,5},{10,6},{3,7},{12,8},{5,9},{1... | collective-permute-start | bytes 786440 | tf_op jit(solution)/shard_map/ppermute | solution.py:31
  51.0 11.0 %collective-permute-start.11 = (bf16[2,256,256]{2,1,0:T(8,128)(2,1)S(1)}, bf16[2,256,256]{2,1,0:T(8,128)(2,1)S(1)}, u32[]{:S(2)}, u32[]{:S(2)}) collective-permute-start(bf16[2,256,256]{2,1,0:T(8,128)(2,1)S(1)} %pad_maximum_fusion.7.own), channel_id=1, source_target_pairs={{2,0},{15,1},{4,2},{1,3},{6,4},{3,5},{8,6},{5,7},{10,8},{7,9},{12,... | collective-permute-start | bytes 786440 | tf_op jit(solution)/shard_map/ppermute | solution.py:31
  59.3 9.8 %collective-permute-start.14 = (bf16[2,256,256]{2,1,0:T(8,128)(2,1)S(1)}, bf16[2,256,256]{2,1,0:T(8,128)(2,1)S(1)}, u32[]{:S(2)}, u32[]{:S(2)}) collective-permute-start(bf16[2,256,256]{2,1,0:T(8,128)(2,1)S(1)} %collective-permute-done.12), channel_id=1, source_target_pairs={{4,0},{6,2},{8,4},{10,6},{12,8},{14,10},{0,12},{2,14},{20,16},{22,... | collective-permute-start | bytes 786440 | tf_op jit(solution)/shard_map/ppermute | solution.py:31
  59.9 9.1 %collective-permute-start.13 = (bf16[2,256,256]{2,1,0:T(8,128)(2,1)S(1)}, bf16[2,256,256]{2,1,0:T(8,128)(2,1)S(1)}, u32[]{:S(2)}, u32[]{:S(2)}) collective-permute-start(bf16[2,256,256]{2,1,0:T(8,128)(2,1)S(1)} %collective-permute-done.12), channel_id=1, source_target_pairs={{2,0},{15,1},{4,2},{1,3},{6,4},{3,5},{8,6},{5,7},{10,8},{7,9},{12,... | collective-permute-start | bytes 786440 | tf_op jit(solution)/shard_map/ppermute | solution.py:31
  62.1 16.0 %collective-permute-start.15 = (bf16[2,2,256,256]{3,2,1,0:T(8,128)(2,1)S(1)}, bf16[2,2,256,256]{3,2,1,0:T(8,128)(2,1)S(1)}, u32[]{:S(2)}, u32[]{:S(2)}) collective-permute-start(bf16[2,2,256,256]{3,2,1,0:T(8,128)(2,1)S(1)} %pad_maximum_fusion.5.mine), channel_id=1, source_target_pairs={{1,0},{0,1},{3,2},{2,3},{5,4},{4,5},{7,6},{6,7},{9,8},{8,9},{11,10... | collective-permute-start | bytes 1572872 | tf_op jit(solution)/shard_map/ppermute | solution.py:31
  66.2 15.5 %collective-permute-start.20 = (bf16[2,256,1024]{2,1,0:T(8,128)(2,1)S(1)}, bf16[2,256,1024]{2,1,0:T(8,128)(2,1)S(1)}, u32[]{:S(2)}, u32[]{:S(2)}) collective-permute-start(bf16[2,256,1024]{2,1,0:T(8,128)(2,1)S(1)} %slice.28), channel_id=1, source_target_pairs={{16,0},{65,1},{18,2},{67,3},{20,4},{69,5},{22,6},{71,7},{24,8},{73... | collective-permute-start | bytes 3145736 | tf_op jit(solution)/shard_map/ppermute | solution.py:31
  69.0 15.2 %collective-permute-start.21 = (bf16[2,256,1024]{2,1,0:T(8,128)(2,1)S(1)}, bf16[2,256,1024]{2,1,0:T(8,128)(2,1)S(1)}, u32[]{:S(2)}, u32[]{:S(2)}) collective-permute-start(bf16[2,256,1024]{2,1,0:T(8,128)(2,1)S(1)} %slice.29), channel_id=1, source_target_pairs={{48,0},{193,1},{50,2},{195,3},{52,4},{197,5},{54,6},{199,7},{56,8}... | collective-permute-start | bytes 3145736 | tf_op jit(solution)/shard_map/ppermute | solution.py:31
  71.0 8.7 %collective-permute-start.19 = (bf16[2,2,256,256]{3,2,1,0:T(8,128)(2,1)S(1)}, bf16[2,2,256,256]{3,2,1,0:T(8,128)(2,1)S(1)}, u32[]{:S(2)}, u32[]{:S(2)}) collective-permute-start(bf16[2,2,256,256]{3,2,1,0:T(8,128)(2,1)S(1)} %pad_maximum_fusion.6.far), channel_id=1, source_target_pairs={{1,0},{0,1},{3,2},{2,3},{5,4},{4,5},{7,6},{6,7},{9,8},{8,9},{11,10... | collective-permute-start | bytes 1572872 | tf_op jit(solution)/shard_map/ppermute | solution.py:31
